TPU v7x, 256 devices: a whole 4x4x8 slice. The times are simulated.
256 devices in a mesh: freq: 64 (over z, y, core), tm: 4 (over x).
Axes of the slice: x: 4, y: 4, z: 8, core: 2. Of those that a mesh axis runs over, the one named last changes fastest.
Arguments:
- filterbank: float32 [4096, 8192], P('freq', 'tm'), may hold values from -6 to 6
- low_rows: int32 [9, 4096], P(None, 'freq'), may hold values from 0 to 63, as said below
- high_rows: int32 [9, 4096], P(None, 'freq'), may hold values from 0 to 63, as said below
- delays: int32 [9, 4096], P(None, 'freq'), may hold values from 0 to 256, as said below
Outputs:
- dm_transform: float32 [4096, 8192], P('freq', 'tm')
Inputs may be any that keep to these rules, and one draw needn't show every extreme that they name: `low_rows`: at a level i below 6 an entry is below 2^i, at a level across owners below 64. The first row of every output sub-band takes row 0, its last row the largest allowed. `high_rows`: at a level i below 6 an entry is below 2^i, at a level across owners below 64. The first row of every output sub-band takes row 0, its last row the largest allowed. `delays`: at level i an entry is at most min(2^i, 512); the first row of every output sub-band has delay 0, its last row that bound.
All inputs are finite; a program needn't handle non-finite values.
Results may differ from a plain program's by a relative error of at most 0.00002.
Values sent between devices are 32-bit elements; how exact they have to be, the bound alone decides.
No kernel may reach another device: no remote copies, remote signals or barrier semaphores. Data moves between devices by JAX's collectives and lax.ppermute only.
A program may use at most 128 MiB of HBM per device.

v0:
```python
import math

import jax
import jax.numpy as jnp
from jax import lax
from jax.sharding import PartitionSpec as P

LOCAL = 6
CROSS = 3
LEVELS = 9
T_DEV = 2048


def passed_along(value, axis, steps):
    count = lax.axis_size(axis)
    first, last = (max(0, -steps), min(count, count - steps))
    return lax.ppermute(value, axis, [(source, source + steps) for source in range(first, last)])


def swapped(x, axis, bit):
    return lax.ppermute(x, axis, [(i, i ^ 1 << bit) for i in range(lax.axis_size(axis))])


def delayed(high_part, lag_rows, lag_bound):
    bit_count = lag_bound.bit_length()
    spare_cols = 2**bit_count - 1 - lag_bound
    current = high_part
    if spare_cols > 0:
        current = jnp.concatenate(
            [current, jnp.zeros((current.shape[0], spare_cols), current.dtype)], axis=1
        )
    offsets = lag_bound - lag_rows
    for bit_pos in reversed(range(bit_count)):
        step_cols = 2**bit_pos
        kept_cols = current.shape[1] - step_cols
        bit_set = jnp.bitwise_and(jnp.right_shift(offsets, bit_pos), 1) == 1
        current = jnp.where(
            bit_set[:, None], current[:, step_cols : step_cols + kept_cols], current[:, :kept_cols]
        )
    return current


def combine(low_src, high_src, low_idx, high_idx, lag_rows, lag_bound):
    low_part = jnp.take(low_src, low_idx, axis=0)
    high_part = jnp.take(high_src, high_idx, axis=0)
    return low_part + delayed(high_part, lag_rows, lag_bound)


def own_indices(row_count, merge_step, low_rows, high_rows):
    row_ids = jnp.arange(row_count, dtype=jnp.int32)
    band_span = 2 ** (merge_step + 1)
    band_start = row_ids - row_ids % band_span
    return (band_start + low_rows[merge_step], band_start + band_span // 2 + high_rows[merge_step])


def on_device(filterbank, low_rows, high_rows, delays):
    lag_bounds = [min(2**merge_step, T_DEV // 4) for merge_step in range(LEVELS)]
    row_count = filterbank.shape[0]
    spectra = filterbank
    for merge_step in range(LOCAL):
        lag_bound = lag_bounds[merge_step]
        rim_cols = passed_along(spectra[:, T_DEV - lag_bound :], "tm", 1)
        high_src = jnp.concatenate([rim_cols, spectra], axis=1)
        low_idx, high_idx = own_indices(row_count, merge_step, low_rows, high_rows)
        spectra = combine(spectra, high_src, low_idx, high_idx, delays[merge_step], lag_bound)
    for pair_bit in range(CROSS):
        merge_step = LOCAL + pair_bit
        lag_bound = lag_bounds[merge_step]
        is_upper = jnp.bitwise_and(jnp.right_shift(lax.axis_index("freq"), pair_bit), 1) == 1
        rim_cols = passed_along(spectra[:, T_DEV - lag_bound :], "tm", 1)
        own_ext = jnp.concatenate([rim_cols, spectra], axis=1)
        partner_ext = swapped(own_ext, "freq", pair_bit)
        high_src = jnp.where(is_upper, own_ext, partner_ext)
        low_src = jnp.where(is_upper, partner_ext, own_ext)[:, lag_bound:]
        spectra = combine(
            low_src,
            high_src,
            low_rows[merge_step],
            high_rows[merge_step],
            delays[merge_step],
            lag_bound,
        )
    return spectra * (1.0 / math.sqrt(2.0**LEVELS))


def solution(mesh):
    placed = (P("freq", "tm"), P(None, "freq"), P(None, "freq"), P(None, "freq"))
    return jax.shard_map(
        on_device, mesh=mesh, in_specs=placed, out_specs=P("freq", "tm"), check_vma=False
    )
```

profile of v0, /device:TPU:96, one launch (start us, length us, event | category | flops | bytes accessed | tf_op | source)
XLA Modules:
  0.0 107.0 jit_solution(13949279271817159442)
XLA Ops:
  0.0 0.8 slice.390
  0.8 3.5 %collective-permute-start = (f32[64,1]{1,0:T(8,128)S(1)}, f32[64,1]{1,0:T(8,128)S(1)}, u32[]{:S(2)}, u32[]{:S(2)}) collective-permute-start(f32[64,1]{1,0:T(8,128)S(1)} %slice.390), channel_id=1, source_target_pairs={{0,1},{1,2},{2,3},{4,5},{5,6},{6,7},{8,9},{9,10},{10,11},{12,13},{... | collective-permute-start | bytes 776 | tf_op jit(solution)/shard_map/ppermute | solution.py:17
  4.5 0.7 copy-done.3
  5.3 2.1 %gather_fusion.9 = f32[64,2048]{1,0:T(8,128)S(1)} fusion(f32[64,2048]{1,0:T(8,128)} %param.6, s32[1024]{0:T(1024)S(1)} %pad_clamp_fusion.17), kind=kCustom, calls=%fused_computation.clone | custom fusion | bytes 1048832 | tf_op jit(solution)/shard_map/jit(_take)/gather | solution.py:44
  7.6 0.8 gather_fusion
  8.5 0.2 fusion.17
  8.9 3.4 %collective-permute-start.1 = (f32[64,2]{1,0:T(8,128)S(1)}, f32[64,2]{1,0:T(8,128)S(1)}, u32[]{:S(2)}, u32[]{:S(2)}) collective-permute-start(f32[64,2]{1,0:T(8,128)S(1)} %slice.554), channel_id=1, source_target_pairs={{0,1},{1,2},{2,3},{4,5},{5,6},{6,7},{8,9},{9,10},{10,11},{12,13},{... | collective-permute-start | bytes 1544 | tf_op jit(solution)/shard_map/ppermute | solution.py:17
  12.3 0.8 gather_fusion.10
  13.0 0.8 collective-permute-done.1
  14.0 0.8 gather_fusion.1
  15.2 0.2 fusion.16
  15.5 4.2 %collective-permute-start.2 = (f32[64,4]{1,0:T(8,128)S(1)}, f32[64,4]{1,0:T(8,128)S(1)}, u32[]{:S(2)}, u32[]{:S(2)}) collective-permute-start(f32[64,4]{1,0:T(8,128)S(1)} %slice.558), channel_id=1, source_target_pairs={{0,1},{1,2},{2,3},{4,5},{5,6},{6,7},{8,9},{9,10},{10,11},{12,13},{... | collective-permute-start | bytes 3080 | tf_op jit(solution)/shard_map/ppermute | solution.py:17
  19.7 0.8 gather_fusion.11
  20.5 0.8 collective-permute-done.2
  21.5 0.8 gather_fusion.2
  22.9 0.2 fusion.15
  23.2 4.2 %collective-permute-start.3 = (f32[64,8]{1,0:T(8,128)S(1)}, f32[64,8]{1,0:T(8,128)S(1)}, u32[]{:S(2)}, u32[]{:S(2)}) collective-permute-start(f32[64,8]{1,0:T(8,128)S(1)} %slice.564), channel_id=1, source_target_pairs={{0,1},{1,2},{2,3},{4,5},{5,6},{6,7},{8,9},{9,10},{10,11},{12,13},{... | collective-permute-start | bytes 6152 | tf_op jit(solution)/shard_map/ppermute | solution.py:17
  27.4 0.8 gather_fusion.12
  28.2 0.8 collective-permute-done.3
  29.2 0.8 gather_fusion.3
  30.8 0.2 fusion.14
  31.1 4.2 %collective-permute-start.4 = (f32[64,16]{1,0:T(8,128)S(1)}, f32[64,16]{1,0:T(8,128)S(1)}, u32[]{:S(2)}, u32[]{:S(2)}) collective-permute-start(f32[64,16]{1,0:T(8,128)S(1)} %slice.572), channel_id=1, source_target_pairs={{0,1},{1,2},{2,3},{4,5},{5,6},{6,7},{8,9},{9,10},{10,11},{12,13},{... | collective-permute-start | bytes 12296 | tf_op jit(solution)/shard_map/ppermute | solution.py:17
  35.3 0.8 gather_fusion.13
  36.1 0.8 collective-permute-done.4
  37.1 0.8 gather_fusion.4
  38.9 0.2 fusion.13
  39.2 4.2 %collective-permute-start.5 = (f32[64,32]{1,0:T(8,128)S(1)}, f32[64,32]{1,0:T(8,128)S(1)}, u32[]{:S(2)}, u32[]{:S(2)}) collective-permute-start(f32[64,32]{1,0:T(8,128)S(1)} %slice.582), channel_id=1, source_target_pairs={{0,1},{1,2},{2,3},{4,5},{5,6},{6,7},{8,9},{9,10},{10,11},{12,13},{... | collective-permute-start | bytes 24584 | tf_op jit(solution)/shard_map/ppermute | solution.py:17
  43.4 0.8 gather_fusion.14
  44.2 0.8 collective-permute-done.5
  45.2 0.8 gather_fusion.5
  47.6 4.2 %collective-permute-start.6 = (f32[64,64]{1,0:T(8,128)S(1)}, f32[64,64]{1,0:T(8,128)S(1)}, u32[]{:S(2)}, u32[]{:S(2)}) collective-permute-start(f32[64,64]{1,0:T(8,128)S(1)} %slice.594), channel_id=1, source_target_pairs={{0,1},{1,2},{2,3},{4,5},{5,6},{6,7},{8,9},{9,10},{10,11},{12,13},{... | collective-permute-start | bytes 49160 | tf_op jit(solution)/shard_map/ppermute | solution.py:17
  51.8 1.6 %collective-permute-done.6 = f32[64,64]{1,0:T(8,128)S(1)} collective-permute-done((f32[64,64]{1,0:T(8,128)S(1)}, f32[64,64]{1,0:T(8,128)S(1)}, u32[]{:S(2)}, u32[]{:S(2)}) %collective-permute-start.6) | collective-permute-done | bytes 16416 | tf_op jit(solution)/shard_map/ppermute | solution.py:17
  53.7 1.9 %collective-permute-done.7 = f32[64,2112]{1,0:T(8,128)S(1)} collective-permute-done((f32[64,2112]{1,0:T(8,128)S(1)}, f32[64,2112]{1,0:T(8,128)S(1)}, u32[]{:S(2)}, u32[]{:S(2)}) %collective-permute-start.7) | collective-permute-done | bytes 540704 | tf_op jit(solution)/shard_map/ppermute | solution.py:21
  55.8 0.8 gather_fusion.15
  56.8 0.8 gather_fusion.6
  59.3 4.4 %collective-permute-start.8 = (f32[64,128]{1,0:T(8,128)S(1)}, f32[64,128]{1,0:T(8,128)S(1)}, u32[]{:S(2)}, u32[]{:S(2)}) collective-permute-start(f32[64,128]{1,0:T(8,128)S(1)} %slice.611), channel_id=1, source_target_pairs={{0,1},{1,2},{2,3},{4,5},{5,6},{6,7},{8,9},{9,10},{10,11},{12,13},{... | collective-permute-start | bytes 98312 | tf_op jit(solution)/shard_map/ppermute | solution.py:17
  63.7 1.6 %collective-permute-done.8 = f32[64,128]{1,0:T(8,128)S(1)} collective-permute-done((f32[64,128]{1,0:T(8,128)S(1)}, f32[64,128]{1,0:T(8,128)S(1)}, u32[]{:S(2)}, u32[]{:S(2)}) %collective-permute-start.8) | collective-permute-done | bytes 32800 | tf_op jit(solution)/shard_map/ppermute | solution.py:17
  65.3 1.7 %collective-permute-start.9 = (f32[64,2176]{1,0:T(8,128)S(1)}, f32[64,2176]{1,0:T(8,128)S(1)}, u32[]{:S(2)}, u32[]{:S(2)}) collective-permute-start(f32[64,2176]{1,0:T(8,128)S(1)} %pad_maximum_fusion.2), channel_id=1, source_target_pairs={{0,8},{4,12},{8,0},{12,4},{16,24},{20,28},{24,16},{28,20},{32,40},... | collective-permute-start | bytes 1671176 | tf_op jit(solution)/shard_map/ppermute | solution.py:21
  67.0 12.2 %collective-permute-done.9 = f32[64,2176]{1,0:T(8,128)S(1)} collective-permute-done((f32[64,2176]{1,0:T(8,128)S(1)}, f32[64,2176]{1,0:T(8,128)S(1)}, u32[]{:S(2)}, u32[]{:S(2)}) %collective-permute-start.9) | collective-permute-done | bytes 557088 | tf_op jit(solution)/shard_map/ppermute | solution.py:21
  79.3 0.8 gather_fusion.16
  80.1 0.8 gather_fusion.7
  82.7 3.9 %collective-permute-start.10 = (f32[64,256]{1,0:T(8,128)S(1)}, f32[64,256]{1,0:T(8,128)S(1)}, u32[]{:S(2)}, u32[]{:S(2)}) collective-permute-start(f32[64,256]{1,0:T(8,128)S(1)} %slice.630), channel_id=1, source_target_pairs={{0,1},{1,2},{2,3},{4,5},{5,6},{6,7},{8,9},{9,10},{10,11},{12,13},{... | collective-permute-start | bytes 196616 | tf_op jit(solution)/shard_map/ppermute | solution.py:17
  86.7 1.9 %collective-permute-done.10 = f32[64,256]{1,0:T(8,128)S(1)} collective-permute-done((f32[64,256]{1,0:T(8,128)S(1)}, f32[64,256]{1,0:T(8,128)S(1)}, u32[]{:S(2)}, u32[]{:S(2)}) %collective-permute-start.10) | collective-permute-done | bytes 65568 | tf_op jit(solution)/shard_map/ppermute | solution.py:17
  88.6 3.3 %collective-permute-start.11 = (f32[64,2304]{1,0:T(8,128)S(1)}, f32[64,2304]{1,0:T(8,128)S(1)}, u32[]{:S(2)}, u32[]{:S(2)}) collective-permute-start(f32[64,2304]{1,0:T(8,128)S(1)} %pad_maximum_fusion), channel_id=1, source_target_pairs={{0,16},{4,20},{8,24},{12,28},{16,0},{20,4},{24,8},{28,12},{32,48},... | collective-permute-start | bytes 1769480 | tf_op jit(solution)/shard_map/ppermute | solution.py:21
  91.9 10.7 %collective-permute-done.11 = f32[64,2304]{1,0:T(8,128)S(1)} collective-permute-done((f32[64,2304]{1,0:T(8,128)S(1)}, f32[64,2304]{1,0:T(8,128)S(1)}, u32[]{:S(2)}, u32[]{:S(2)}) %collective-permute-start.11) | collective-permute-done | bytes 589856 | tf_op jit(solution)/shard_map/ppermute | solution.py:21
  102.7 0.8 gather_fusion.17
  103.5 0.8 gather_fusion.8
  106.0 1.0 fusion.9
  (104 shorter events, 12.1 us)
Async XLA Ops:
  0.0 4.4 %copy-start.1 = (s32[9,64]{1,0:T(8,128)S(1)}, s32[9,64]{1,0:T(8,128)}, u32[]{:S(2)}) copy-start(s32[9,64]{1,0:T(8,128)} %param.8) | copy-start | bytes 6916
  0.8 3.6 %copy-start.2 = (s32[9,64]{1,0:T(8,128)S(1)}, s32[9,64]{1,0:T(8,128)}, u32[]{:S(2)}) copy-start(s32[9,64]{1,0:T(8,128)} %param.9) | copy-start | bytes 6916
  0.8 6.6 %collective-permute-start = (f32[64,1]{1,0:T(8,128)S(1)}, f32[64,1]{1,0:T(8,128)S(1)}, u32[]{:S(2)}, u32[]{:S(2)}) collective-permute-start(f32[64,1]{1,0:T(8,128)S(1)} %slice.390), channel_id=1, source_target_pairs={{0,1},{1,2},{2,3},{4,5},{5,6},{6,7},{8,9},{9,10},{10,11},{12,13},{... | collective-permute-start | bytes 776 | tf_op jit(solution)/shard_map/ppermute | solution.py:17
  4.5 0.7 copy-start.3
  5.3 2.1 %copy-start = (f32[64,2048]{1,0:T(8,128)S(1)}, f32[64,2048]{1,0:T(8,128)}, u32[]{:S(2)}) copy-start(f32[64,2048]{1,0:T(8,128)} %param.6) | copy-start | bytes 1572868
  8.9 5.0 %collective-permute-start.1 = (f32[64,2]{1,0:T(8,128)S(1)}, f32[64,2]{1,0:T(8,128)S(1)}, u32[]{:S(2)}, u32[]{:S(2)}) collective-permute-start(f32[64,2]{1,0:T(8,128)S(1)} %slice.554), channel_id=1, source_target_pairs={{0,1},{1,2},{2,3},{4,5},{5,6},{6,7},{8,9},{9,10},{10,11},{12,13},{... | collective-permute-start | bytes 1544 | tf_op jit(solution)/shard_map/ppermute | solution.py:17
  15.5 5.8 %collective-permute-start.2 = (f32[64,4]{1,0:T(8,128)S(1)}, f32[64,4]{1,0:T(8,128)S(1)}, u32[]{:S(2)}, u32[]{:S(2)}) collective-permute-start(f32[64,4]{1,0:T(8,128)S(1)} %slice.558), channel_id=1, source_target_pairs={{0,1},{1,2},{2,3},{4,5},{5,6},{6,7},{8,9},{9,10},{10,11},{12,13},{... | collective-permute-start | bytes 3080 | tf_op jit(solution)/shard_map/ppermute | solution.py:17
  23.2 5.8 %collective-permute-start.3 = (f32[64,8]{1,0:T(8,128)S(1)}, f32[64,8]{1,0:T(8,128)S(1)}, u32[]{:S(2)}, u32[]{:S(2)}) collective-permute-start(f32[64,8]{1,0:T(8,128)S(1)} %slice.564), channel_id=1, source_target_pairs={{0,1},{1,2},{2,3},{4,5},{5,6},{6,7},{8,9},{9,10},{10,11},{12,13},{... | collective-permute-start | bytes 6152 | tf_op jit(solution)/shard_map/ppermute | solution.py:17
  31.1 5.8 %collective-permute-start.4 = (f32[64,16]{1,0:T(8,128)S(1)}, f32[64,16]{1,0:T(8,128)S(1)}, u32[]{:S(2)}, u32[]{:S(2)}) collective-permute-start(f32[64,16]{1,0:T(8,128)S(1)} %slice.572), channel_id=1, source_target_pairs={{0,1},{1,2},{2,3},{4,5},{5,6},{6,7},{8,9},{9,10},{10,11},{12,13},{... | collective-permute-start | bytes 12296 | tf_op jit(solution)/shard_map/ppermute | solution.py:17
  39.2 5.8 %collective-permute-start.5 = (f32[64,32]{1,0:T(8,128)S(1)}, f32[64,32]{1,0:T(8,128)S(1)}, u32[]{:S(2)}, u32[]{:S(2)}) collective-permute-start(f32[64,32]{1,0:T(8,128)S(1)} %slice.582), channel_id=1, source_target_pairs={{0,1},{1,2},{2,3},{4,5},{5,6},{6,7},{8,9},{9,10},{10,11},{12,13},{... | collective-permute-start | bytes 24584 | tf_op jit(solution)/shard_map/ppermute | solution.py:17
  47.6 5.8 %collective-permute-start.6 = (f32[64,64]{1,0:T(8,128)S(1)}, f32[64,64]{1,0:T(8,128)S(1)}, u32[]{:S(2)}, u32[]{:S(2)}) collective-permute-start(f32[64,64]{1,0:T(8,128)S(1)} %slice.594), channel_id=1, source_target_pairs={{0,1},{1,2},{2,3},{4,5},{5,6},{6,7},{8,9},{9,10},{10,11},{12,13},{... | collective-permute-start | bytes 49160 | tf_op jit(solution)/shard_map/ppermute | solution.py:17
  53.6 2.0 %collective-permute-start.7 = (f32[64,2112]{1,0:T(8,128)S(1)}, f32[64,2112]{1,0:T(8,128)S(1)}, u32[]{:S(2)}, u32[]{:S(2)}) collective-permute-start(f32[64,2112]{1,0:T(8,128)S(1)} %pad_maximum_fusion.1), channel_id=1, source_target_pairs={{0,4},{4,0},{8,12},{12,8},{16,20},{20,16},{24,28},{28,24},{32,36},... | collective-permute-start | bytes 1622024 | tf_op jit(solution)/shard_map/ppermute | solution.py:21
  59.3 6.0 %collective-permute-start.8 = (f32[64,128]{1,0:T(8,128)S(1)}, f32[64,128]{1,0:T(8,128)S(1)}, u32[]{:S(2)}, u32[]{:S(2)}) collective-permute-start(f32[64,128]{1,0:T(8,128)S(1)} %slice.611), channel_id=1, source_target_pairs={{0,1},{1,2},{2,3},{4,5},{5,6},{6,7},{8,9},{9,10},{10,11},{12,13},{... | collective-permute-start | bytes 98312 | tf_op jit(solution)/shard_map/ppermute | solution.py:17
  65.3 13.9 %collective-permute-start.9 = (f32[64,2176]{1,0:T(8,128)S(1)}, f32[64,2176]{1,0:T(8,128)S(1)}, u32[]{:S(2)}, u32[]{:S(2)}) collective-permute-start(f32[64,2176]{1,0:T(8,128)S(1)} %pad_maximum_fusion.2), channel_id=1, source_target_pairs={{0,8},{4,12},{8,0},{12,4},{16,24},{20,28},{24,16},{28,20},{32,40},... | collective-permute-start | bytes 1671176 | tf_op jit(solution)/shard_map/ppermute | solution.py:21
  82.7 5.8 %collective-permute-start.10 = (f32[64,256]{1,0:T(8,128)S(1)}, f32[64,256]{1,0:T(8,128)S(1)}, u32[]{:S(2)}, u32[]{:S(2)}) collective-permute-start(f32[64,256]{1,0:T(8,128)S(1)} %slice.630), channel_id=1, source_target_pairs={{0,1},{1,2},{2,3},{4,5},{5,6},{6,7},{8,9},{9,10},{10,11},{12,13},{... | collective-permute-start | bytes 196616 | tf_op jit(solution)/shard_map/ppermute | solution.py:17
  88.6 14.0 %collective-permute-start.11 = (f32[64,2304]{1,0:T(8,128)S(1)}, f32[64,2304]{1,0:T(8,128)S(1)}, u32[]{:S(2)}, u32[]{:S(2)}) collective-permute-start(f32[64,2304]{1,0:T(8,128)S(1)} %pad_maximum_fusion), channel_id=1, source_target_pairs={{0,16},{4,20},{8,24},{12,28},{16,0},{20,4},{24,8},{28,12},{32,48},... | collective-permute-start | bytes 1769480 | tf_op jit(solution)/shard_map/ppermute | solution.py:21
where the time goes:
time: 108 us; the launch traced here: 107 us
  starting transfers between devices  41.4 us (38%)
  waiting for transfers between devices  33.9 us (31%)
  local copies, waits for them, and re-layouts  17.3 us (16%)
  other arithmetic  13.7 us (13%)
    ppermute x9, starting transfers between devices, passed_along(): lax.ppermute(value, axis, [(source, source + steps) for source in range(f...  36.3 us
    ppermute x3, waiting for transfers between devices, swapped(): lax.ppermute(x, axis, [(i, i ^ 1 << bit) for i in range(lax.axis_size(axi...  24.8 us
    ppermute x9, waiting for transfers between devices, passed_along(): lax.ppermute(value, axis, [(source, source + steps) for source in range(f...  9.07 us
    gather x9, local copies, waits for them, and re-layouts, combine(): low_part = jnp.take(low_src, low_idx, axis=0)  8.14 us
    select_n x36, other arithmetic, delayed(): jnp.where(bit_set[:, None], current[:, step_cols:step_cols + kept_cols],...  7.51 us
    gather x9, local copies, waits for them, and re-layouts, combine(): high_part = jnp.take(high_src, high_idx, axis=0)  7.2 us
    ppermute x3, starting transfers between devices, swapped(): lax.ppermute(x, axis, [(i, i ^ 1 << bit) for i in range(lax.axis_size(axi...  5.03 us
  transfers between devices with their start and end apart: 12, of which 11 were waited for; matrix products, arithmetic and copies ran while one was open for 6% of the time, Pallas kernels for 0%

commit v1 on v0

v1 whole, which is shorter than its diff:
```python
import functools
import math

import jax
import jax.numpy as jnp
from jax import lax
from jax.experimental import pallas as pl
from jax.experimental.pallas import tpu as pltpu
from jax.sharding import PartitionSpec as P

LOCAL = 6
LEVELS = 9
ROWS = 64
LANES = 128
CHUNKS = 16
HALO = 4
GUARD = 8
SCALE = 1.0 / math.sqrt(2.0**LEVELS)
F32 = jnp.float32


def vmem_spec():
    return pl.BlockSpec(memory_space=pltpu.VMEM)


def smem_spec():
    return pl.BlockSpec(memory_space=pltpu.SMEM)


def in_vmem(value):
    return pltpu.with_memory_space_constraint(value, pltpu.VMEM)


def lanes(count):
    return lax.broadcasted_iota(jnp.int32, (count, LANES), 1)


def delayed(src, base, lag, count):
    start = base - lax.shift_right_logical(lag, 7)
    turn = jnp.bitwise_and(lag, LANES - 1)
    here = src[pl.ds(start, count), :]
    before = src[pl.ds(start - 1, count), :]
    return pltpu.roll(jnp.where(lanes(count) < LANES - turn, here, before), turn, axis=1)


def local_levels(first, mid, low, high, lag, out, width):
    src, dst = first, mid
    for level in range(1, LOCAL):
        span = 2 ** (level + 1)
        target = out if level == LOCAL - 1 else dst
        for row in range(ROWS):
            start = row - row % span
            low_at = GUARD + (start + low[level, row]) * width
            high_at = GUARD + (start + span // 2 + high[level, row]) * width
            for chunk in range(0, width, 8):
                target[pl.ds(GUARD + row * width + chunk, 8), :] = src[
                    pl.ds(low_at + chunk, 8), :
                ] + delayed(src, high_at + chunk, lag[level, row], 8)
        src, dst = dst, src


def first_level(pair_low, pair_high, buf, row, width):
    before = jnp.concatenate([jnp.zeros((1, LANES), F32), pair_high[: width - 1]], axis=0)
    late = pltpu.roll(jnp.where(lanes(width) < LANES - 1, pair_high, before), 1, axis=1)
    buf[pl.ds(GUARD + row * width, width), :] = pair_low + pair_high
    buf[pl.ds(GUARD + (row + 1) * width, width), :] = pair_low + late


def main_kernel(x, low, high, lag, low_v, high_v, lag_v, out, head, tab, buf_a, buf_b):
    zeros = jnp.zeros((GUARD, LANES), F32)
    for buf in (buf_a, buf_b, out):
        buf[0:GUARD, :] = zeros
    for group in range(8):
        head[pl.ds(group * 32, 32), :] = x[pl.ds(group * 128, 32), :]
    for at, table in enumerate((low_v, high_v, lag_v)):
        tab[pl.ds(2 * at, 2), :] = table[LOCAL + 1 : LEVELS, :]
    tab[6:8, :] = jnp.zeros((2, ROWS), jnp.int32)
    for row in range(0, ROWS, 2):
        at = (row // 8) * 128 + row % 8
        first_level(
            x[pl.ds(at, CHUNKS, stride=8), :],
            x[pl.ds(at + 1, CHUNKS, stride=8), :],
            buf_a,
            row,
            CHUNKS,
        )
    local_levels(buf_a, buf_b, low, high, lag, out, CHUNKS)


def head_kernel(halo, head, low, high, lag, out, buf_a, buf_b):
    zeros = jnp.zeros((GUARD, LANES), F32)
    for buf in (buf_a, buf_b, out):
        buf[0:GUARD, :] = zeros
    for row in range(0, ROWS, 2):
        at = (row // 8) * 32 + row % 8
        pair = [
            jnp.concatenate(
                [halo[pl.ds(at + k, 4, stride=8), :], head[pl.ds(at + k, 4, stride=8), :]], axis=0
            )
            for k in range(2)
        ]
        first_level(*pair, buf_a, row, 8)
    local_levels(buf_a, buf_b, low, high, lag, out, 8)


def cross_level(low_src, high_src, low, high, lag, width, put):
    for row in range(ROWS):
        low_at = GUARD + low[LOCAL, row] * width
        high_at = GUARD + high[LOCAL, row] * width
        for chunk in range(0, width, 8):
            put(
                row,
                chunk,
                low_src[pl.ds(low_at + chunk, 8), :]
                + delayed(high_src, high_at + chunk, lag[LOCAL, row], 8),
            )


def on_core(own, partner, run):
    core = jnp.bitwise_and(lax.axis_index("freq"), 1)
    pl.when(core == 0)(lambda: run(own, partner))
    pl.when(core == 1)(lambda: run(partner, own))


def core_main_kernel(own, partner, low, high, lag, out):
    def put(row, chunk, value):
        out[pl.ds(row * CHUNKS + chunk, 8), :] = value

    on_core(own, partner, lambda a, b: cross_level(a, b, low, high, lag, CHUNKS, put))


def core_head_kernel(own, partner, main, low, high, lag, out):
    width = HALO + CHUNKS

    def put(row, chunk, value):
        out[pl.ds(row * width, 8), :] = value

    on_core(own, partner, lambda a, b: cross_level(a, b, low, high, lag, 8, put))
    for row in range(ROWS):
        for chunk in (4, 8, 12):
            out[pl.ds(row * width + HALO + chunk, 4), :] = main[pl.ds(row * CHUNKS + chunk, 4), :]


def shares(l6, tabs, parts, outs):
    width = HALO + CHUNKS
    y = jnp.bitwise_and(lax.shift_right_logical(lax.axis_index("freq"), 1), 3)
    odd = jnp.bitwise_and(y, 1)
    upper7, upper8 = odd, lax.shift_right_logical(y, 1)
    own, across, near = tabs

    def table(k, entry, at):
        if k == 0:
            return own[entry, at]
        if k == 2:
            return across[entry, at]
        return near[entry + (0 if k == 1 else 8), at]

    for (steps, chunk, count), out in zip(parts, outs):

        def emit(k, steps=steps, chunk=chunk, count=count, out=out):
            for row in range(ROWS):
                via = table(k, 1 + 2 * upper8, row)
                lag = table(k, 5, row) * upper8
                source = table(k & 1, 2 * upper7, via)
                lag = lag + table(k & 1, 4, via) * upper7
                base = source * width + HALO + chunk
                for piece in range(0, count, 8):
                    out[pl.ds(row * count + piece, 8), :] = delayed(l6, base + piece, lag, 8)

        if steps in (0, 2):
            emit(steps)
        else:
            up = 1 if steps == 1 else 3
            pl.when(odd == 0)(lambda: emit(up))
            pl.when(odd == 1)(lambda: emit(4 - up))


def shares_kernel(parts, l6, own, across, near, *outs):
    shares(l6, (own, across, near), parts, outs)


def add_kernel(a, b, out):
    out[...] = a[...] + b[...]


def last_kernel(own, down_high, up_high, down_low, up_low, out):
    for row in range(ROWS):
        at = (row // 8) * 128 + row % 8
        for half, (a, b) in enumerate(((down_low, up_low), (down_high, up_high))):
            value = (
                own[pl.ds(row * CHUNKS + 8 * half, 8), :]
                + a[pl.ds(row * 8, 8), :]
                + b[pl.ds(row * 8, 8), :]
            )
            out[pl.ds(at + 64 * half, 8, stride=8), :] = value * SCALE


def call(kernel, ins, outs, scratch=()):
    values = [in_vmem(a) if where == "v" else a for a, where in ins]
    specs = [smem_spec() if where == "s" else vmem_spec() for _, where in ins]
    return pl.pallas_call(
        kernel,
        out_shape=outs,
        in_specs=specs,
        out_specs=[vmem_spec()] * len(outs),
        scratch_shapes=list(scratch),
    )(*values)


def pinned(sublanes, lane_count=LANES, dtype=F32):
    return pltpu.VMEM((sublanes, lane_count), dtype)


def ring(steps):
    return [(i, (i & ~6) | ((((i >> 1) + steps) & 3) << 1)) for i in range(64)]


def swap(bit):
    return [(i, i ^ bit) for i in range(64)]


def on_device(x, low, high, lag):
    tiles = x.reshape(8, 8, CHUNKS, LANES).transpose(0, 2, 1, 3)
    tail = tiles[:, CHUNKS - HALO :].reshape(8 * HALO * 8, LANES)
    halo = lax.ppermute(tail, "tm", [(0, 1), (1, 2), (2, 3)])
    tables = [(low, "s"), (high, "s"), (lag, "s")]

    l5, head, own_tab = call(
        main_kernel,
        [(tiles.reshape(1024, LANES), "b"), *tables, (low, "b"), (high, "b"), (lag, "b")],
        [pinned(GUARD + 1024), pinned(256), pinned(8, ROWS, jnp.int32)],
        [pltpu.VMEM((GUARD + 1024, LANES), F32)] * 2,
    )
    l5_far = lax.ppermute(l5, "freq", swap(1))
    across = lax.ppermute(own_tab, "freq", swap(4))
    near = lax.ppermute(jnp.concatenate([own_tab, across], axis=0), "freq", swap(2))
    (l5h,) = call(
        head_kernel,
        [(halo, "v"), (head, "v"), *tables],
        [pinned(GUARD + 512)],
        [pltpu.VMEM((GUARD + 512, LANES), F32)] * 2,
    )
    l5h_far = lax.ppermute(l5h, "freq", swap(1))
    (l6m,) = call(core_main_kernel, [(l5, "v"), (l5_far, "v"), *tables], [pinned(1024)])
    (l6,) = call(
        core_head_kernel,
        [(l5h, "v"), (l5h_far, "v"), (l6m, "v"), *tables],
        [pinned(ROWS * (HALO + CHUNKS))],
    )
    tabs = [(own_tab, "s"), (across, "s"), (near, "s")]

    def share(*parts):
        return call(
            functools.partial(shares_kernel, parts),
            [(l6, "v"), *tabs],
            [pinned(ROWS * count) for _, _, count in parts],
        )

    def add(a, b):
        return call(add_kernel, [(a, "v"), (b, "v")], [pinned(a.shape[0])])[0]

    one_up, one_down = ring(1), ring(-1)
    far_up, far_down = share((2, 8, 8), (2, 0, 8))
    relay_up = lax.ppermute(far_up, "freq", one_up)
    relay_down = lax.ppermute(far_down, "freq", one_down)
    next_up, next_down = share((1, 0, 8), (3, 8, 8))
    low_up = lax.ppermute(next_up, "freq", one_up)
    high_down = lax.ppermute(next_down, "freq", one_down)
    more_up, more_down, mine = share((1, 8, 8), (3, 0, 8), (0, 0, 16))
    high_up = lax.ppermute(add(more_up, relay_up), "freq", one_up)
    low_down = lax.ppermute(add(more_down, relay_down), "freq", one_down)
    (out,) = call(
        last_kernel,
        [(mine, "v"), (high_down, "v"), (high_up, "v"), (low_down, "v"), (low_up, "v")],
        [jax.ShapeDtypeStruct((1024, LANES), F32)],
    )
    return out.reshape(8, CHUNKS, 8, LANES).transpose(0, 2, 1, 3).reshape(ROWS, CHUNKS * LANES)


def solution(mesh):
    placed = (P("freq", "tm"), P(None, "freq"), P(None, "freq"), P(None, "freq"))
    return jax.shard_map(
        on_device, mesh=mesh, in_specs=placed, out_specs=P("freq", "tm"), check_vma=False
    )
```

time: 108 us -> 50.5 us (0.47)
  the two profiles are of different devices: /device:TPU:96 before, /device:TPU:70 now
where the time goes in v1:
time: 50.5 us; the launch traced here: 50 us
  waiting for transfers between devices  17.3 us (34%)
  Pallas kernels  16.5 us (33%)
  starting transfers between devices  14 us (28%)
  local copies, waits for them, and re-layouts  2.1 us (4%)
    pallas_call x10, Pallas kernels, call(): pl.pallas_call(kernel, out_shape=outs, in_specs=specs, out_specs=[vmem_sp...  16.5 us
    ppermute x1, waiting for transfers between devices, on_device(): halo = lax.ppermute(tail, 'tm', [(0, 1), (1, 2), (2, 3)])  6.48 us
    ppermute x1, waiting for transfers between devices, on_device(): low_up = lax.ppermute(next_up, 'freq', one_up)  5.03 us
    ppermute x1, waiting for transfers between devices, on_device(): high_up = lax.ppermute(add(more_up, relay_up), 'freq', one_up)  3.33 us
    ppermute x1, starting transfers between devices, on_device(): across = lax.ppermute(own_tab, 'freq', swap(4))  3.28 us
    ppermute x1, starting transfers between devices, on_device(): high_down = lax.ppermute(next_down, 'freq', one_down)  2.63 us
    ppermute x1, starting transfers between devices, on_device(): relay_down = lax.ppermute(far_down, 'freq', one_down)  2.26 us
    ppermute x1, starting transfers between devices, on_device(): low_down = lax.ppermute(add(more_down, relay_down), 'freq', one_down)  2.1 us
  transfers between devices with their start and end apart: 11, of which 6 were waited for; matrix products, arithmetic and copies ran while one was open for 2% of the time, Pallas kernels for 20%

profile of v1, /device:TPU:70, one launch (start us, length us, event | category | flops | bytes accessed | tf_op | source)
XLA Modules:
  0.0 50.0 jit_solution(1759611953241041423)
XLA Ops:
  0.0 2.8 %shard_map.46 = (f32[1032,128]{1,0:T(8,128)S(1)}, f32[256,128]{1,0:T(8,128)S(1)}, s32[8,64]{1,0:T(8,128)S(1)}) custom-call(f32[1024,128]{1,0:T(8,128)} %bitcast.11, s32[9,64]{1,0:T(8,128)} %low.7, s32[9,64]{1,0:T(8,128)} %high.7, s32[9,64]{1,0:T(8,128)} %lag.7, s32[9,64]{1,0:T(8,128)} %low.7, s32[9,64]{1,0:T(8,128)} %high.7, s32[9,64]{1,0:T(8,128)} %lag.7), custom_call_target="tpu_custom_call" | custom-call | tf_op jit(solution)/shard_map/pallas_call | solution.py:201
  2.8 0.0 copy-start
  2.8 0.1 collective-permute-start.2
  2.9 0.9 %slice.4 = f32[8,4,8,128]{3,2,1,0:T(8,128)S(1)} slice(f32[8,16,8,128]{3,2,1,0:T(8,128)} %bitcast.12), slice={[0:8], [12:16], [0:8], [0:128]} | slice | bytes 262144 | tf_op jit(solution)/shard_map/slice | solution.py:224
  3.9 1.3 %collective-permute-start = (f32[256,128]{1,0:T(8,128)S(1)}, f32[256,128]{1,0:T(8,128)S(1)}, u32[]{:S(2)}, u32[]{:S(2)}) collective-permute-start(f32[256,128]{1,0:T(8,128)S(1)} %bitcast.13), channel_id=1, source_target_pairs={{0,1},{1,2},{2,3},{4,5},{5,6},{6,7},{8,9},{9,10},{10,11},{12,13},{... | collective-permute-start | bytes 393224 | tf_op jit(solution)/shard_map/ppermute | solution.py:225
  5.2 6.5 %collective-permute-done.halo = f32[256,128]{1,0:T(8,128)S(1)} collective-permute-done((f32[256,128]{1,0:T(8,128)S(1)}, f32[256,128]{1,0:T(8,128)S(1)}, u32[]{:S(2)}, u32[]{:S(2)}) %collective-permute-start) | collective-permute-done | bytes 131104 | tf_op jit(solution)/shard_map/ppermute | solution.py:225
  11.7 2.3 %shard_map.47.own = f32[520,128]{1,0:T(8,128)S(1)} custom-call(f32[256,128]{1,0:T(8,128)S(1)} %collective-permute-done.halo, f32[256,128]{1,0:T(8,128)S(1)} %get-tuple-element.15.head, s32[9,64]{1,0:T(8,128)} %low.7, s32[9,64]{1,0:T(8,128)} %high.7, s32[9,64]{1,0:T(8,128)} %lag.7), custom_call_target="tpu_custom_call" | custom-call | tf_op jit(solution)/shard_map/pallas_call | solution.py:201
  13.9 0.1 collective-permute-start.1
  14.0 3.3 %collective-permute-start.3 = (s32[8,64]{1,0:T(8,128)S(1)}, s32[8,64]{1,0:T(8,128)S(1)}, u32[]{:S(2)}, u32[]{:S(2)}) collective-permute-start(s32[8,64]{1,0:T(8,128)S(1)} %get-tuple-element.17.own), channel_id=1, source_target_pairs={{0,16},{4,20},{8,24},{12,28},{16,0},{20,4},{24,8},{28,12},{32,48},... | collective-permute-start | bytes 6152 | tf_op jit(solution)/shard_map/ppermute | solution.py:235
  17.3 1.9 %collective-permute-done.3.across = s32[8,64]{1,0:T(8,128)S(1)} collective-permute-done((s32[8,64]{1,0:T(8,128)S(1)}, s32[8,64]{1,0:T(8,128)S(1)}, u32[]{:S(2)}, u32[]{:S(2)}) %collective-permute-start.3) | collective-permute-done | bytes 2080 | tf_op jit(solution)/shard_map/ppermute | solution.py:235
  19.2 0.0 copy-done
  19.2 0.0 copy-start.2
  19.2 0.6 %copy-done.2 = s32[8,64]{1,0:T(8,128)} copy-done((s32[8,64]{1,0:T(8,128)}, s32[8,64]{1,0:T(8,128)S(1)}, u32[]{:S(2)}) %copy-start.2) | copy-done | bytes 2072
  19.8 1.6 %collective-permute-start.4 = (s32[16,64]{1,0:T(8,128)S(1)}, s32[16,64]{1,0:T(8,128)S(1)}, u32[]{:S(2)}, u32[]{:S(2)}) collective-permute-start(s32[16,64]{1,0:T(8,128)S(1)} %pad_add_fusion), channel_id=1, source_target_pairs={{0,8},{4,12},{8,0},{12,4},{16,24},{20,28},{24,16},{28,20},{32,40},... | collective-permute-start | bytes 12296 | tf_op jit(solution)/shard_map/ppermute | solution.py:236
  21.4 0.0 collective-permute-done.2.partner
  21.4 1.4 %shard_map.48.main = f32[1024,128]{1,0:T(8,128)S(1)} custom-call(f32[1032,128]{1,0:T(8,128)S(1)} %get-tuple-element.16.own, f32[1032,128]{1,0:T(8,128)S(1)} %collective-permute-done.2.partner, s32[9,64]{1,0:T(8,128)} %low.7, s32[9,64]{1,0:T(8,128)} %high.7, s32[9,64]{1,0:T(8,128)} %lag.7), custom_call_target="tpu_custom_call" | custom-call | tf_op jit(solution)/shard_map/pallas_call | solution.py:201
  22.9 0.0 collective-permute-done.1.partner
  22.9 1.4 %shard_map.49.l6 = f32[1280,128]{1,0:T(8,128)S(1)} custom-call(f32[520,128]{1,0:T(8,128)S(1)} %shard_map.47.own, f32[520,128]{1,0:T(8,128)S(1)} %collective-permute-done.1.partner, f32[1024,128]{1,0:T(8,128)S(1)} %shard_map.48.main, s32[9,64]{1,0:T(8,128)} %low.7, s32[9,64]{1,0:T(8,128)} %high.7, s32[9,64]{1,0:T(8,128)} %lag.7), custom_call_target="tpu_custom_call" | custom-call | tf_op jit(solution)/shard_map/pallas_call | solution.py:201
  24.2 0.0 collective-permute-done.4.near
  24.2 0.0 copy-start.1
  24.3 0.6 %copy-done.1 = s32[16,64]{1,0:T(8,128)} copy-done((s32[16,64]{1,0:T(8,128)}, s32[16,64]{1,0:T(8,128)S(1)}, u32[]{:S(2)}) %copy-start.1) | copy-done | bytes 4120
  24.8 2.5 %shard_map.52 = (f32[512,128]{1,0:T(8,128)}, f32[512,128]{1,0:T(8,128)S(1)}) custom-call(f32[1280,128]{1,0:T(8,128)S(1)} %shard_map.49.l6, s32[8,64]{1,0:T(8,128)} %copy-done, s32[8,64]{1,0:T(8,128)} %copy-done.2, s32[16,64]{1,0:T(8,128)} %copy-done.1), custom_call_target="tpu_custom_call" | custom-call | tf_op jit(solution)/shard_map/pallas_call | solution.py:201
  27.3 2.3 %collective-permute-start.8 = (f32[512,128]{1,0:T(8,128)S(1)}, f32[512,128]{1,0:T(8,128)S(1)}, u32[]{:S(2)}, u32[]{:S(2)}) collective-permute-start(f32[512,128]{1,0:T(8,128)S(1)} %get-tuple-element.23), channel_id=1, source_target_pairs={{0,24},{4,28},{8,0},{12,4},{16,8},{20,12},{24,16},{28,20},{32,56},... | collective-permute-start | bytes 786440 | tf_op jit(solution)/shard_map/ppermute | solution.py:265
  29.6 0.0 collective-permute-start.6
  29.6 2.6 %shard_map.51 = (f32[512,128]{1,0:T(8,128)}, f32[512,128]{1,0:T(8,128)S(1)}) custom-call(f32[1280,128]{1,0:T(8,128)S(1)} %shard_map.49.l6, s32[8,64]{1,0:T(8,128)} %copy-done, s32[8,64]{1,0:T(8,128)} %copy-done.2, s32[16,64]{1,0:T(8,128)} %copy-done.1), custom_call_target="tpu_custom_call" | custom-call | tf_op jit(solution)/shard_map/pallas_call | solution.py:201
  32.2 0.6 %collective-permute-start.10 = (f32[512,128]{1,0:T(8,128)}, f32[512,128]{1,0:T(8,128)S(1)}, u32[]{:S(2)}, u32[]{:S(2)}) collective-permute-start(f32[512,128]{1,0:T(8,128)} %get-tuple-element.24), channel_id=1, source_target_pairs={{0,8},{4,12},{8,16},{12,20},{16,24},{20,28},{24,0},{28,4},{32,40},... | collective-permute-start | bytes 786440 | tf_op jit(solution)/shard_map/ppermute | solution.py:267
  32.8 2.6 %collective-permute-start.5 = (f32[512,128]{1,0:T(8,128)S(1)}, f32[512,128]{1,0:T(8,128)S(1)}, u32[]{:S(2)}, u32[]{:S(2)}) collective-permute-start(f32[512,128]{1,0:T(8,128)S(1)} %get-tuple-element.19), channel_id=1, source_target_pairs={{0,24},{4,28},{8,0},{12,4},{16,8},{20,12},{24,16},{28,20},{32,56},... | collective-permute-start | bytes 786440 | tf_op jit(solution)/shard_map/ppermute | solution.py:268
  35.4 2.5 %shard_map.50 = (f32[512,128]{1,0:T(8,128)S(1)}, f32[512,128]{1,0:T(8,128)S(1)}, f32[1024,128]{1,0:T(8,128)S(1)}) custom-call(f32[1280,128]{1,0:T(8,128)S(1)} %shard_map.49.l6, s32[8,64]{1,0:T(8,128)} %copy-done, s32[8,64]{1,0:T(8,128)} %copy-done.2, s32[16,64]{1,0:T(8,128)} %copy-done.1), custom_call_target="tpu_custom_call" | custom-call | tf_op jit(solution)/shard_map/pallas_call | solution.py:201
  37.9 0.0 collective-permute-done.8.b
  38.0 2.1 %collective-permute-start.9 = (f32[512,128]{1,0:T(8,128)S(1)}, f32[512,128]{1,0:T(8,128)S(1)}, u32[]{:S(2)}, u32[]{:S(2)}) collective-permute-start(f32[512,128]{1,0:T(8,128)S(1)} %shard_map.54), channel_id=1, source_target_pairs={{0,24},{4,28},{8,0},{12,4},{16,8},{20,12},{24,16},{28,20},{32,56},... | collective-permute-start | bytes 786440 | tf_op jit(solution)/shard_map/ppermute | solution.py:271
  40.1 0.2 collective-permute-done.6.b
  40.3 0.1 collective-permute-start.7
  40.4 5.0 %collective-permute-done.10.up_low = f32[512,128]{1,0:T(8,128)S(1)} collective-permute-done((f32[512,128]{1,0:T(8,128)}, f32[512,128]{1,0:T(8,128)S(1)}, u32[]{:S(2)}, u32[]{:S(2)}) %collective-permute-start.10) | collective-permute-done | bytes 262176 | tf_op jit(solution)/shard_map/ppermute | solution.py:267
  45.4 0.0 collective-permute-done.5.down_high
  45.4 0.4 collective-permute-done.9.down_low
  45.8 3.3 %collective-permute-done.7.up_high = f32[512,128]{1,0:T(8,128)S(1)} collective-permute-done((f32[512,128]{1,0:T(8,128)S(1)}, f32[512,128]{1,0:T(8,128)S(1)}, u32[]{:S(2)}, u32[]{:S(2)}) %collective-permute-start.7) | collective-permute-done | bytes 262176 | tf_op jit(solution)/shard_map/ppermute | solution.py:270
  49.1 0.9 %shard_map.55 = f32[1024,128]{1,0:T(8,128)} custom-call(f32[1024,128]{1,0:T(8,128)S(1)} %get-tuple-element.18.own, f32[512,128]{1,0:T(8,128)S(1)} %collective-permute-done.5.down_high, f32[512,128]{1,0:T(8,128)S(1)} %collective-permute-done.7.up_high, f32[512,128]{1,0:T(8,128)S(1)} %collective-permute-done.9.down_low, ...), custom_call_target="tpu_custom_call" | custom-call | tf_op jit(solution)/shard_map/pallas_call | solution.py:201
  (3 shorter events, 0.1 us)
Async XLA Ops:
  2.8 16.4 %copy-start = (s32[8,64]{1,0:T(8,128)}, s32[8,64]{1,0:T(8,128)S(1)}, u32[]{:S(2)}) copy-start(s32[8,64]{1,0:T(8,128)S(1)} %get-tuple-element.17.own) | copy-start | bytes 6148
  2.8 18.6 %collective-permute-start.2 = (f32[1032,128]{1,0:T(8,128)S(1)}, f32[1032,128]{1,0:T(8,128)S(1)}, u32[]{:S(2)}, u32[]{:S(2)}) collective-permute-start(f32[1032,128]{1,0:T(8,128)S(1)} %get-tuple-element.16.own), channel_id=1, source_target_pairs={{0,4},{4,0},{8,12},{12,8},{16,20},{20,16},{24,28},{28,24},{32,36},... | collective-permute-start | bytes 1585160 | tf_op jit(solution)/shard_map/ppermute | solution.py:234
  3.9 7.8 %collective-permute-start = (f32[256,128]{1,0:T(8,128)S(1)}, f32[256,128]{1,0:T(8,128)S(1)}, u32[]{:S(2)}, u32[]{:S(2)}) collective-permute-start(f32[256,128]{1,0:T(8,128)S(1)} %bitcast.13), channel_id=1, source_target_pairs={{0,1},{1,2},{2,3},{4,5},{5,6},{6,7},{8,9},{9,10},{10,11},{12,13},{... | collective-permute-start | bytes 393224 | tf_op jit(solution)/shard_map/ppermute | solution.py:225
  13.9 8.9 %collective-permute-start.1 = (f32[520,128]{1,0:T(8,128)S(1)}, f32[520,128]{1,0:T(8,128)S(1)}, u32[]{:S(2)}, u32[]{:S(2)}) collective-permute-start(f32[520,128]{1,0:T(8,128)S(1)} %shard_map.47.own), channel_id=1, source_target_pairs={{0,4},{4,0},{8,12},{12,8},{16,20},{20,16},{24,28},{28,24},{32,36},... | collective-permute-start | bytes 798728 | tf_op jit(solution)/shard_map/ppermute | solution.py:243
  14.0 5.2 %collective-permute-start.3 = (s32[8,64]{1,0:T(8,128)S(1)}, s32[8,64]{1,0:T(8,128)S(1)}, u32[]{:S(2)}, u32[]{:S(2)}) collective-permute-start(s32[8,64]{1,0:T(8,128)S(1)} %get-tuple-element.17.own), channel_id=1, source_target_pairs={{0,16},{4,20},{8,24},{12,28},{16,0},{20,4},{24,8},{28,12},{32,48},... | collective-permute-start | bytes 6152 | tf_op jit(solution)/shard_map/ppermute | solution.py:235
  19.2 0.6 %copy-start.2 = (s32[8,64]{1,0:T(8,128)}, s32[8,64]{1,0:T(8,128)S(1)}, u32[]{:S(2)}) copy-start(s32[8,64]{1,0:T(8,128)S(1)} %collective-permute-done.3.across) | copy-start | bytes 6148
  19.8 4.4 %collective-permute-start.4 = (s32[16,64]{1,0:T(8,128)S(1)}, s32[16,64]{1,0:T(8,128)S(1)}, u32[]{:S(2)}, u32[]{:S(2)}) collective-permute-start(s32[16,64]{1,0:T(8,128)S(1)} %pad_add_fusion), channel_id=1, source_target_pairs={{0,8},{4,12},{8,0},{12,4},{16,24},{20,28},{24,16},{28,20},{32,40},... | collective-permute-start | bytes 12296 | tf_op jit(solution)/shard_map/ppermute | solution.py:236
  24.2 0.6 %copy-start.1 = (s32[16,64]{1,0:T(8,128)}, s32[16,64]{1,0:T(8,128)S(1)}, u32[]{:S(2)}) copy-start(s32[16,64]{1,0:T(8,128)S(1)} %collective-permute-done.4.near) | copy-start | bytes 12292
  27.3 10.6 %collective-permute-start.8 = (f32[512,128]{1,0:T(8,128)S(1)}, f32[512,128]{1,0:T(8,128)S(1)}, u32[]{:S(2)}, u32[]{:S(2)}) collective-permute-start(f32[512,128]{1,0:T(8,128)S(1)} %get-tuple-element.23), channel_id=1, source_target_pairs={{0,24},{4,28},{8,0},{12,4},{16,8},{20,12},{24,16},{28,20},{32,56},... | collective-permute-start | bytes 786440 | tf_op jit(solution)/shard_map/ppermute | solution.py:265
  29.6 10.7 %collective-permute-start.6 = (f32[512,128]{1,0:T(8,128)}, f32[512,128]{1,0:T(8,128)S(1)}, u32[]{:S(2)}, u32[]{:S(2)}) collective-permute-start(f32[512,128]{1,0:T(8,128)} %get-tuple-element.21), channel_id=1, source_target_pairs={{0,8},{4,12},{8,16},{12,20},{16,24},{20,28},{24,0},{28,4},{32,40},... | collective-permute-start | bytes 786440 | tf_op jit(solution)/shard_map/ppermute | solution.py:264
  32.2 13.2 %collective-permute-start.10 = (f32[512,128]{1,0:T(8,128)}, f32[512,128]{1,0:T(8,128)S(1)}, u32[]{:S(2)}, u32[]{:S(2)}) collective-permute-start(f32[512,128]{1,0:T(8,128)} %get-tuple-element.24), channel_id=1, source_target_pairs={{0,8},{4,12},{8,16},{12,20},{16,24},{20,28},{24,0},{28,4},{32,40},... | collective-permute-start | bytes 786440 | tf_op jit(solution)/shard_map/ppermute | solution.py:267
  32.8 12.6 %collective-permute-start.5 = (f32[512,128]{1,0:T(8,128)S(1)}, f32[512,128]{1,0:T(8,128)S(1)}, u32[]{:S(2)}, u32[]{:S(2)}) collective-permute-start(f32[512,128]{1,0:T(8,128)S(1)} %get-tuple-element.19), channel_id=1, source_target_pairs={{0,24},{4,28},{8,0},{12,4},{16,8},{20,12},{24,16},{28,20},{32,56},... | collective-permute-start | bytes 786440 | tf_op jit(solution)/shard_map/ppermute | solution.py:268
  38.0 7.8 %collective-permute-start.9 = (f32[512,128]{1,0:T(8,128)S(1)}, f32[512,128]{1,0:T(8,128)S(1)}, u32[]{:S(2)}, u32[]{:S(2)}) collective-permute-start(f32[512,128]{1,0:T(8,128)S(1)} %shard_map.54), channel_id=1, source_target_pairs={{0,24},{4,28},{8,0},{12,4},{16,8},{20,12},{24,16},{28,20},{32,56},... | collective-permute-start | bytes 786440 | tf_op jit(solution)/shard_map/ppermute | solution.py:271
  40.3 8.8 %collective-permute-start.7 = (f32[512,128]{1,0:T(8,128)S(1)}, f32[512,128]{1,0:T(8,128)S(1)}, u32[]{:S(2)}, u32[]{:S(2)}) collective-permute-start(f32[512,128]{1,0:T(8,128)S(1)} %shard_map.53), channel_id=1, source_target_pairs={{0,8},{4,12},{8,16},{12,20},{16,24},{20,28},{24,0},{28,4},{32,40},... | collective-permute-start | bytes 786440 | tf_op jit(solution)/shard_map/ppermute | solution.py:270

commit v2 on v0

v2 whole, which is shorter than its diff:
```python
import functools
import math

import jax
import jax.numpy as jnp
from jax import lax
from jax.experimental import pallas as pl
from jax.experimental.pallas import tpu as pltpu
from jax.sharding import PartitionSpec as P

LOCAL = 6
LEVELS = 9
ROWS = 64
LANES = 128
CHUNKS = 16
PITCH = 24
PACKED = 18
REACH = 9
SCALE = 1.0 / math.sqrt(2.0**LEVELS)
F32 = jnp.float32
HEAD = ((2, 0, 4), (1, 0, 4), (3, 0, 4), (0, 0, 4))


def lanes(count):
    return lax.broadcasted_iota(jnp.int32, (count, LANES), 1)


def place():
    at = lax.axis_index("freq")
    return [jnp.bitwise_and(lax.shift_right_logical(at, bit), 1) for bit in range(3)]


def turned(here, before, turn):
    return pltpu.roll(
        jnp.where(lanes(here.shape[0]) < LANES - turn, here, before), turn, axis=1
    )


def level_codes(low, high, lag):
    row = lax.broadcasted_iota(jnp.int32, (LEVELS, ROWS), 1)
    level = lax.broadcasted_iota(jnp.int32, (LEVELS, ROWS), 0)
    span = lax.shift_left(2, level)
    local = level < LOCAL
    start = jnp.where(local, jnp.bitwise_and(row, -span), 0)
    half = jnp.where(local, lax.shift_right_logical(span, 1), 0)
    pitch = jnp.where(local, PITCH, PACKED)
    return (start + low) * pitch + (start + half + high) * pitch * 2048 + lag * 2**22


def opened(code):
    return (
        jnp.bitwise_and(code, 2047),
        jnp.bitwise_and(lax.shift_right_logical(code, 11), 2047),
        lax.shift_right_logical(code, 22),
    )


def pieces(src, code, skip, high_skip, spans):
    low_at, high_at, turn = opened(code)
    return [
        src[pl.ds(low_at + (skip + first), count), :]
        + turned(
            src[pl.ds(high_at + (high_skip + first), count), :],
            src[pl.ds(high_at + (high_skip + first - 1), count), :],
            turn,
        )
        for first, count in spans
    ]


WHOLE = ((0, 8), (8, 8), (16, 1))


def main_kernel(
    x_h, low_h, high_h, lag_h, out, tab, codes, x, low, high, lag, plan, buf_a, buf_b, sems
):
    copies = [
        pltpu.make_async_copy(source, target, sems.at[at])
        for at, (source, target) in enumerate(((low_h, low), (high_h, high), (lag_h, lag)))
    ]
    parts = [
        pltpu.make_async_copy(
            x_h.at[pl.ds(part * 256, 256)], x.at[pl.ds(part * 256, 256)], sems.at[3 + part]
        )
        for part in range(4)
    ]
    for copy in copies + parts:
        copy.start()
    for row in range(ROWS):
        out[pl.ds(row * PACKED, 1), :] = jnp.zeros((1, LANES), F32)
    for row in range(ROWS + 1):
        for buf in (buf_a, buf_b):
            buf[pl.ds(row * PITCH, 8), :] = jnp.zeros((8, LANES), F32)
    for copy in copies:
        copy.wait()
    plan[...] = jnp.zeros_like(plan)
    plan[0:LEVELS, 0:ROWS] = level_codes(low[...], high[...], lag[...])
    planned = pltpu.make_async_copy(plan, codes, sems.at[7])
    planned.start()
    tab[...] = jnp.zeros_like(tab)
    for at, table in enumerate((low, high, lag)):
        tab[pl.ds(2 * at, 2), 0:ROWS] = table[LOCAL + 1 : LEVELS, :]
    none = jnp.zeros((1, LANES), F32)
    for part, copy in enumerate(parts):
        copy.wait()
        for row in range(part * 16, part * 16 + 16, 2):
            at = (row // 8) * 128 + row % 8
            low_row = x[pl.ds(at, CHUNKS, stride=8), :]
            high_row = x[pl.ds(at + 1, CHUNKS, stride=8), :]
            before = jnp.concatenate([none, high_row[: CHUNKS - 1]], axis=0)
            to = row * PITCH + 8
            buf_a[pl.ds(to, CHUNKS), :] = low_row + high_row
            buf_a[pl.ds(to + PITCH, CHUNKS), :] = low_row + turned(high_row, before, 1)
            buf_a[pl.ds(to + PITCH + CHUNKS, 1), :] = turned(none, high_row[CHUNKS - 1 :], 1)
    planned.wait()
    src, dst = buf_a, buf_b
    for level in range(1, LOCAL):
        last = level == LOCAL - 1
        for row in range(ROWS):
            to = row * PACKED + 1 if last else row * PITCH + 8
            for (first, count), piece in zip(WHOLE, pieces(src, codes[level, row], 8, 8, WHOLE)):
                (out if last else dst)[pl.ds(to + first, count), :] = piece
        src, dst = dst, src


def term_codes(tab7, tab8, odd, upper, pitch):
    def rows(tab, at):
        return jnp.broadcast_to(tab[at : at + 1, :], (8, LANES))

    via = jnp.where(upper == 1, rows(tab8, 3), rows(tab8, 1))
    late = jnp.where(upper == 1, rows(tab8, 5), 0)
    source = jnp.where(odd == 1, rows(tab7, 2), rows(tab7, 0))
    later = jnp.where(odd == 1, rows(tab7, 4), 0)
    late = late + jnp.take_along_axis(later, via, axis=1)
    source = jnp.take_along_axis(source, via, axis=1)
    at = source * pitch - lax.shift_right_logical(late, 7)
    return (at * LANES + jnp.bitwise_and(late, LANES - 1))[0:1]


def shares(src, ahead, codes, parts, put, narrow=False):
    for part, (which, chunk, count) in enumerate(parts):
        for row in range(ROWS):
            code = codes[which, row]
            at = lax.shift_right_arithmetic(code, 7)
            if narrow:
                at = at - lax.shift_left(lax.shift_right_arithmetic(at + 8, 4), 3)
            turn = jnp.bitwise_and(code, LANES - 1)
            for first in range(0, count, 8):
                size = min(8, count - first)
                to = ahead + chunk + first
                put(
                    part,
                    row * count + first,
                    size,
                    turned(src[pl.ds(at + to, size), :], src[pl.ds(at + (to - 1), size), :], turn),
                )


def into(*outs):
    def put(part, at, size, value):
        outs[part][pl.ds(at, size), :] = value

    return put


def core_main_kernel(
    own, partner, codes, tab, l6, long_up, long_down, short_up, short_down, edge, both
):
    core = place()[0]
    size = own.shape[0]
    both[pl.ds(pl.multiple_of(core * size, 8), size), :] = own[...]
    both[pl.ds(pl.multiple_of((1 - core) * size, 8), size), :] = partner[...]
    for message in (long_up, long_down):
        message[0:8, :] = tab[...].astype(F32)
    for row in range(ROWS):
        first, second, past = pieces(both, codes[LOCAL, row], 1, size + 1, WHOLE)
        l6[pl.ds(row * CHUNKS, 8), :] = first
        l6[pl.ds(row * CHUNKS + 8, 8), :] = second
        edge[pl.ds(row * 4, 3), :] = second[5:8]
        edge[pl.ds(row * 4 + 3, 1), :] = past
        at = 8 + row * REACH
        long_up[pl.ds(at, 1), :] = first[7:8]
        long_up[pl.ds(at + 1, 8), :] = second
        long_down[pl.ds(at, 7), :] = first[1:8]
        long_down[pl.ds(at + 7, 2), :] = second[0:2]
        short_up[pl.ds(row * 6, 6), :] = first[1:7]
        short_down[pl.ds(row * 6, 6), :] = second[2:8]


def tables_of(message):
    return message[0:8, :].astype(jnp.int32)


def relay_kernel(long_up, long_down, up, down, plan, terms, sem):
    _, odd, upper = place()
    below, above = tables_of(long_up), tables_of(long_down)
    same = jnp.bitwise_xor(upper, odd)
    plan[...] = jnp.zeros_like(plan)
    plan[0:1, :] = term_codes(below, above, 1 - odd, 1 - same, REACH)
    plan[1:2, :] = term_codes(above, below, 1 - odd, same, REACH)
    copy = pltpu.make_async_copy(plan, terms, sem)
    copy.start()
    copy.wait()
    shares(long_up, 11, terms, ((0, 0, 6),), into(up))
    shares(long_down, 11, terms, ((1, 0, 6),), into(down))


def head_kernel(
    l6, edge, tab, across, long_up, long_down, far, up, down, mine, terms, buf, plan, sem
):
    _, odd, upper = place()
    own, other = tab[...], across[...]
    below, above = tables_of(long_up), tables_of(long_down)
    pair = jnp.where(odd == 1, below, above)
    plan[...] = jnp.zeros_like(plan)
    plan[0:1, :] = term_codes(own, own, odd, upper, CHUNKS)
    plan[1:2, :] = term_codes(pair, above, odd, upper, CHUNKS)
    plan[2:3, :] = term_codes(own, other, odd, upper, CHUNKS)
    plan[3:4, :] = term_codes(pair, below, odd, upper, CHUNKS)
    near = term_codes(own, own, 1 - odd, upper, CHUNKS)
    away = term_codes(other, own, 1 - odd, 1 - upper, CHUNKS)
    plan[4:5, :] = jnp.where(odd == 1, near, away)
    plan[5:6, :] = jnp.where(odd == 1, away, near)
    copy = pltpu.make_async_copy(plan, terms, sem)
    copy.start()
    inner = lax.axis_index("tm") > 0
    for row in range(ROWS):
        ahead = jnp.where(inner, edge[pl.ds(row * 4, 4), :], 0.0)
        buf[pl.ds(row * 8 + 1, 3), :] = ahead[0:3]
        buf[pl.ds(row * 8 + 4, 1), :] = ahead[3:4] + l6[pl.ds(row * CHUNKS, 1), :]
        buf[pl.ds(row * 8 + 5, 3), :] = l6[pl.ds(row * CHUNKS + 1, 3), :]
    copy.wait()
    shares(buf, 4, terms, HEAD, into(far, up, down, mine), narrow=True)


def direct_kernel(l6, long_up, long_down, short_up, short_down, terms, out, low_buf, high_buf):
    for row in range(ROWS):
        at, to = 8 + row * REACH, row * CHUNKS
        low_buf[pl.ds(to + 1, 6), :] = short_up[pl.ds(row * 6, 6), :]
        low_buf[pl.ds(to + 7, 9), :] = long_up[pl.ds(at, 9), :]
        high_buf[pl.ds(to + 1, 9), :] = long_down[pl.ds(at, 9), :]
        high_buf[pl.ds(to + 10, 6), :] = short_down[pl.ds(row * 6, 6), :]
    for row in range(ROWS):
        for first, count in ((4, 8), (12, 4)):
            total = None
            for which, src in ((0, l6), (4, low_buf), (5, high_buf)):
                code = terms[which, row]
                at = lax.shift_right_arithmetic(code, 7)
                term = turned(
                    src[pl.ds(at + first, count), :],
                    src[pl.ds(at + (first - 1), count), :],
                    jnp.bitwise_and(code, LANES - 1),
                )
                total = term if total is None else total + term
            out[pl.ds(row * 12 + first - 4, count), :] = total


def last_kernel(mine, mid_down, high_up, mine_head, far, up, down, out):
    for row in range(ROWS):
        at = (row // 8) * 128 + row % 8
        head = [a[pl.ds(row * 4, 4), :] for a in (mine_head, far, up, down)]
        out[pl.ds(at, 4, stride=8), :] = (head[0] + head[1] + head[2] + head[3]) * SCALE
        for chunk, arrived in ((4, mid_down), (10, high_up)):
            value = mine[pl.ds(row * 12 + chunk - 4, 6), :] + arrived[pl.ds(row * 6, 6), :]
            out[pl.ds(at + 8 * chunk, 6, stride=8), :] = value * SCALE


def call(kernel, ins, outs, scratch=()):
    pins = {"v": pltpu.VMEM, "t": pltpu.SMEM, "h": pltpu.HBM}
    kinds = {"v": pltpu.VMEM, "t": pltpu.SMEM, "h": pltpu.HBM}
    values = [
        pltpu.with_memory_space_constraint(a, pins[where]) if where in pins else a for a, where in ins
    ]
    return pl.pallas_call(
        kernel,
        out_shape=outs,
        in_specs=[pl.BlockSpec(memory_space=kinds[where]) for _, where in ins],
        out_specs=[
            pl.BlockSpec(memory_space=pltpu.SMEM if "smem" in str(o).lower() else pltpu.VMEM) for o in outs
        ],
        scratch_shapes=list(scratch),
        compiler_params=pltpu.CompilerParams(vmem_limit_bytes=16 * 2**20),
    )(*values)


def pinned(sublanes, lane_count=LANES, dtype=F32):
    return pltpu.VMEM((sublanes, lane_count), dtype)


def ring(steps):
    return [(i, (i & ~6) | ((((i >> 1) + steps) & 3) << 1)) for i in range(64)]


def swap(bit):
    return [(i, i ^ bit) for i in range(64)]


def on_device(x, low, high, lag):
    tiles = x.reshape(8, 8, CHUNKS, LANES).transpose(0, 2, 1, 3).reshape(1024, LANES)
    sem = pltpu.SemaphoreType.DMA
    ints = jnp.int32
    one_up, one_down = ring(1), ring(-1)
    plan, terms_ref = pltpu.VMEM((8, LANES), ints), pltpu.SMEM((8, LANES), ints)

    l5, own_tab, codes = call(
        main_kernel,
        [(a, "h") for a in (tiles, low, high, lag)],
        [pinned(ROWS * PACKED), pinned(8, LANES, ints), pltpu.SMEM((16, LANES), ints)],
        [pltpu.VMEM((1024, LANES), F32)]
        + [pltpu.VMEM((LEVELS, ROWS), ints)] * 3
        + [pltpu.VMEM((16, LANES), ints)]
        + [pltpu.VMEM((ROWS * PITCH + 8, LANES), F32)] * 2
        + [sem((8,))],
    )
    l5_far = lax.ppermute(l5, "freq", swap(1))
    across = lax.ppermute(own_tab, "freq", swap(4))
    l6, long_up, long_down, short_up, short_down, edge = call(
        core_main_kernel,
        [(l5, "v"), (l5_far, "v"), (codes, "t"), (own_tab, "v")],
        [pinned(1024)]
        + [pinned(8 + ROWS * REACH)] * 2
        + [pinned(ROWS * 6)] * 2
        + [pinned(ROWS * 4)],
        [pltpu.VMEM((2 * ROWS * PACKED, LANES), F32)],
    )
    long_up = lax.ppermute(long_up, "freq", one_up)
    long_down = lax.ppermute(long_down, "freq", one_down)
    short_up = lax.ppermute(short_up, "freq", one_up)
    short_down = lax.ppermute(short_down, "freq", one_down)
    edge = lax.ppermute(edge, "tm", [(i, (i + 1) % 4) for i in range(4)])

    relay_up, relay_down = call(
        relay_kernel,
        [(long_up, "v"), (long_down, "v")],
        [pinned(ROWS * 6), pinned(ROWS * 6)],
        [plan, terms_ref, sem],
    )
    high_up = lax.ppermute(relay_up, "freq", one_up)
    mid_down = lax.ppermute(relay_down, "freq", one_down)

    head_far, head_up, head_down, mine_head, terms = call(
        head_kernel,
        [(a, "v") for a in (l6, edge, own_tab, across, long_up, long_down)],
        [pinned(ROWS * 4)] * 4 + [terms_ref],
        [pltpu.VMEM((512, LANES), F32), plan, sem],
    )
    far = lax.ppermute(head_far, "freq", swap(4))
    up = lax.ppermute(head_up, "freq", one_up)
    down = lax.ppermute(head_down, "freq", one_down)
    (mine,) = call(
        direct_kernel,
        [(a, "v") for a in (l6, long_up, long_down, short_up, short_down)] + [(terms, "t")],
        [pinned(ROWS * 12)],
        [pltpu.VMEM((1024, LANES), F32)] * 2,
    )
    last = [mine, mid_down, high_up, mine_head, far, up, down]
    (out,) = call(
        last_kernel, [(a, "v") for a in last], [jax.ShapeDtypeStruct((1024, LANES), F32)]
    )
    return out.reshape(8, CHUNKS, 8, LANES).transpose(0, 2, 1, 3).reshape(ROWS, CHUNKS * LANES)


def solution(mesh):
    placed = (P("freq", "tm"), P(None, "freq"), P(None, "freq"), P(None, "freq"))
    return jax.shard_map(
        on_device, mesh=mesh, in_specs=placed, out_specs=P("freq", "tm"), check_vma=False
    )
```

time: 108 us -> 35.9 us (0.33)
  starting transfers between devices: 41.4 us -> 16.9 us
  waiting for transfers between devices: 33.9 us -> 11.2 us
  local copies, waits for them, and re-layouts: 17.3 us -> 0 us
  other arithmetic: 13.7 us -> 0 us
  Pallas kernels: 0 us -> 7.62 us
    ppermute x12, starting transfers between devices: 41.4 us -> 16.9 us  [the longest x1 2.97 us: on_device(): down = lax.ppermute(head_down, 'freq', one_down)]
    ppermute x12, waiting for transfers between devices: 33.9 us -> 11.2 us  [the longest x1 3.18 us: on_device(): long_up = lax.ppermute(long_up, 'freq', one_up)]
    gather x18 -> x0, local copies, waits for them, and re-layouts: 15.3 us -> none  [the longest x9 8.14 us: combine(): low_part = jnp.take(low_src, low_idx, axis=0)]
    select_n x52 -> x0, other arithmetic: 9.14 us -> none  [the longest x36 7.51 us: delayed(): jnp.where(bit_set[:, None], current[:, step_cols:step_cols + kept_cols],...]
    pallas_call x0 -> x6, Pallas kernels: none -> 7.62 us  [call(): pl.pallas_call(kernel, out_shape=outs, in_specs=[pl.BlockSpec(memory_spac...]
    add x8 -> x0, other arithmetic: 1.82 us -> none  [combine(): return low_part + delayed(high_part, lag_rows, lag_bound)]
    concatenate x9 -> x0, other arithmetic: 1.53 us -> none  [the longest x6 1.25 us: on_device(): high_src = jnp.concatenate([rim_cols, spectra], axis=1)]
    slice x9 -> x0, local copies, waits for them, and re-layouts: 1.31 us -> none  [on_device(): rim_cols = passed_along(spectra[:, T_DEV - lag_bound:], 'tm', 1)]
  transfers between devices with their start and end apart: 12 -> 12, of which waited for: 11 -> 5; matrix products, arithmetic and copies ran while one was open for 6% -> 0% of each run, Pallas kernels for 0% -> 9%
where the time goes in v2:
time: 35.9 us; the launch traced here: 35.8 us
  starting transfers between devices  16.9 us (47%)
  waiting for transfers between devices  11.2 us (31%)
  Pallas kernels  7.62 us (21%)
    pallas_call x6, Pallas kernels, call(): pl.pallas_call(kernel, out_shape=outs, in_specs=[pl.BlockSpec(memory_spac...  7.62 us
    ppermute x1, waiting for transfers between devices, on_device(): long_up = lax.ppermute(long_up, 'freq', one_up)  3.18 us
    ppermute x1, waiting for transfers between devices, on_device(): up = lax.ppermute(head_up, 'freq', one_up)  3.05 us
    ppermute x1, starting transfers between devices, on_device(): down = lax.ppermute(head_down, 'freq', one_down)  2.97 us
    ppermute x1, starting transfers between devices, on_device(): short_down = lax.ppermute(short_down, 'freq', one_down)  2.88 us
    ppermute x1, waiting for transfers between devices, on_device(): far = lax.ppermute(head_far, 'freq', swap(4))  2.1 us
    ppermute x1, waiting for transfers between devices, on_device(): l5_far = lax.ppermute(l5, 'freq', swap(1))  1.99 us
    ppermute x1, starting transfers between devices, on_device(): across = lax.ppermute(own_tab, 'freq', swap(4))  1.99 us
  transfers between devices with their start and end apart: 12, of which 5 were waited for; matrix products, arithmetic and copies ran while one was open for 0% of the time, Pallas kernels for 9%

profile of v2, /device:TPU:96, one launch (start us, length us, event | category | flops | bytes accessed | tf_op | source)
XLA Modules:
  0.0 35.8 jit_solution(7877319292221659402)
XLA Ops:
  0.0 2.9 %shard_map.46 = (f32[1152,128]{1,0:T(8,128)S(1)}, s32[8,128]{1,0:T(8,128)S(1)}, s32[16,128]{1,0:T(8,128)S(4)}) custom-call(f32[1024,128]{1,0:T(8,128)} %bitcast.10, s32[9,64]{1,0:T(8,128)} %low_h.1, s32[9,64]{1,0:T(8,128)} %high_h.1, s32[9,64]{1,0:T(8,128)} %lag_h.1), custom_call_target="tpu_custom_call" | custom-call | tf_op jit(solution)/shard_map/pallas_call | solution.py:274
  2.9 0.1 collective-permute-start
  3.0 2.0 %collective-permute-done.partner = f32[1152,128]{1,0:T(8,128)S(1)} collective-permute-done((f32[1152,128]{1,0:T(8,128)S(1)}, f32[1152,128]{1,0:T(8,128)S(1)}, u32[]{:S(2)}, u32[]{:S(2)}) %collective-permute-start) | collective-permute-done | bytes 589856 | tf_op jit(solution)/shard_map/ppermute | solution.py:315
  5.0 0.4 %shard_map.47 = (f32[1024,128]{1,0:T(8,128)S(1)}, f32[584,128]{1,0:T(8,128)S(1)}, f32[584,128]{1,0:T(8,128)S(1)}, f32[384,128]{1,0:T(8,128)S(1)}, f32[384,128]{1,0:T(8,128)S(1)}, /*index=5*/f32[256,128]{1,0:T(8,128)S(1)}) custom-call(f32[1152,128]{1,0:T(8,128)S(1)} %get-tuple-element.21.own, f32[1152,128]{1,0:T(8,128)S(1)} %collective-permute-done.partner, ...), custom_call_target="tpu_custom_call" | custom-call | tf_op jit(solution)/shard_map/pallas_call | solution.py:274
  5.4 1.6 %collective-permute-start.1 = (f32[584,128]{1,0:T(8,128)S(1)}, f32[584,128]{1,0:T(8,128)S(1)}, u32[]{:S(2)}, u32[]{:S(2)}) collective-permute-start(f32[584,128]{1,0:T(8,128)S(1)} %get-tuple-element.25), channel_id=1, source_target_pairs={{0,8},{4,12},{8,16},{12,20},{16,24},{20,28},{24,0},{28,4},{32,40},... | collective-permute-start | bytes 897032 | tf_op jit(solution)/shard_map/ppermute | solution.py:326
  7.0 1.7 %collective-permute-start.2 = (f32[584,128]{1,0:T(8,128)S(1)}, f32[584,128]{1,0:T(8,128)S(1)}, u32[]{:S(2)}, u32[]{:S(2)}) collective-permute-start(f32[584,128]{1,0:T(8,128)S(1)} %get-tuple-element.26), channel_id=1, source_target_pairs={{0,24},{4,28},{8,0},{12,4},{16,8},{20,12},{24,16},{28,20},{32,56},... | collective-permute-start | bytes 897032 | tf_op jit(solution)/shard_map/ppermute | solution.py:327
  8.7 0.4 %collective-permute-start.3 = (f32[384,128]{1,0:T(8,128)S(1)}, f32[384,128]{1,0:T(8,128)S(1)}, u32[]{:S(2)}, u32[]{:S(2)}) collective-permute-start(f32[384,128]{1,0:T(8,128)S(1)} %get-tuple-element.27), channel_id=1, source_target_pairs={{0,8},{4,12},{8,16},{12,20},{16,24},{20,28},{24,0},{28,4},{32,40},... | collective-permute-start | bytes 589832 | tf_op jit(solution)/shard_map/ppermute | solution.py:328
  9.1 2.9 %collective-permute-start.4 = (f32[384,128]{1,0:T(8,128)S(1)}, f32[384,128]{1,0:T(8,128)S(1)}, u32[]{:S(2)}, u32[]{:S(2)}) collective-permute-start(f32[384,128]{1,0:T(8,128)S(1)} %get-tuple-element.28), channel_id=1, source_target_pairs={{0,24},{4,28},{8,0},{12,4},{16,8},{20,12},{24,16},{28,20},{32,56},... | collective-permute-start | bytes 589832 | tf_op jit(solution)/shard_map/ppermute | solution.py:329
  11.9 1.5 %collective-permute-start.5 = (f32[256,128]{1,0:T(8,128)S(1)}, f32[256,128]{1,0:T(8,128)S(1)}, u32[]{:S(2)}, u32[]{:S(2)}) collective-permute-start(f32[256,128]{1,0:T(8,128)S(1)} %get-tuple-element.29), channel_id=1, source_target_pairs={{0,1},{1,2},{2,3},{3,0},{4,5},{5,6},{6,7},{7,4},{8,9},{9,10},{10,1... | collective-permute-start | bytes 393224 | tf_op jit(solution)/shard_map/ppermute | solution.py:330
  13.4 3.2 %collective-permute-done.1.long_up = f32[584,128]{1,0:T(8,128)S(1)} collective-permute-done((f32[584,128]{1,0:T(8,128)S(1)}, f32[584,128]{1,0:T(8,128)S(1)}, u32[]{:S(2)}, u32[]{:S(2)}) %collective-permute-start.1) | collective-permute-done | bytes 299040 | tf_op jit(solution)/shard_map/ppermute | solution.py:326
  16.6 2.0 %collective-permute-start.6 = (s32[8,128]{1,0:T(8,128)S(1)}, s32[8,128]{1,0:T(8,128)S(1)}, u32[]{:S(2)}, u32[]{:S(2)}) collective-permute-start(s32[8,128]{1,0:T(8,128)S(1)} %get-tuple-element.23.tab), channel_id=1, source_target_pairs={{0,16},{4,20},{8,24},{12,28},{16,0},{20,4},{24,8},{28,12},{32,48},... | collective-permute-start | bytes 12296 | tf_op jit(solution)/shard_map/ppermute | solution.py:316
  18.6 0.0 collective-permute-done.2.long_down
  18.6 0.9 %shard_map.50 = (f32[384,128]{1,0:T(8,128)S(1)}, f32[384,128]{1,0:T(8,128)S(1)}) custom-call(f32[584,128]{1,0:T(8,128)S(1)} %collective-permute-done.1.long_up, f32[584,128]{1,0:T(8,128)S(1)} %collective-permute-done.2.long_down), custom_call_target="tpu_custom_call" | custom-call | tf_op jit(solution)/shard_map/pallas_call | solution.py:274
  19.5 1.3 %collective-permute-start.7 = (f32[384,128]{1,0:T(8,128)S(1)}, f32[384,128]{1,0:T(8,128)S(1)}, u32[]{:S(2)}, u32[]{:S(2)}) collective-permute-start(f32[384,128]{1,0:T(8,128)S(1)} %get-tuple-element.31), channel_id=1, source_target_pairs={{0,24},{4,28},{8,0},{12,4},{16,8},{20,12},{24,16},{28,20},{32,56},... | collective-permute-start | bytes 589832 | tf_op jit(solution)/shard_map/ppermute | solution.py:339
  20.9 0.8 %collective-permute-done.6.across = s32[8,128]{1,0:T(8,128)S(1)} collective-permute-done((s32[8,128]{1,0:T(8,128)S(1)}, s32[8,128]{1,0:T(8,128)S(1)}, u32[]{:S(2)}, u32[]{:S(2)}) %collective-permute-start.6) | collective-permute-done | bytes 4128 | tf_op jit(solution)/shard_map/ppermute | solution.py:316
  21.7 1.7 %collective-permute-start.8 = (f32[384,128]{1,0:T(8,128)S(1)}, f32[384,128]{1,0:T(8,128)S(1)}, u32[]{:S(2)}, u32[]{:S(2)}) collective-permute-start(f32[384,128]{1,0:T(8,128)S(1)} %get-tuple-element.32), channel_id=1, source_target_pairs={{0,8},{4,12},{8,16},{12,20},{16,24},{20,28},{24,0},{28,4},{32,40},... | collective-permute-start | bytes 589832 | tf_op jit(solution)/shard_map/ppermute | solution.py:338
  23.4 0.0 collective-permute-done.5.edge
  23.4 1.5 %shard_map.48 = (f32[256,128]{1,0:T(8,128)S(1)}, f32[256,128]{1,0:T(8,128)S(1)}, f32[256,128]{1,0:T(8,128)S(1)}, f32[256,128]{1,0:T(8,128)S(1)}, s32[8,128]{1,0:T(8,128)S(4)}) custom-call(f32[1024,128]{1,0:T(8,128)S(1)} %get-tuple-element.24.l6, f32[256,128]{1,0:T(8,128)S(1)} %collective-permute-done.5.edge, s32[8,128]{1,0:T(8,128)S(1)} %get-tuple-element.23.tab, ...), custom_call_target="tpu_custom_call" | custom-call | tf_op jit(solution)/shard_map/pallas_call | solution.py:274
  24.9 0.3 collective-permute-start.10
  25.3 0.0 collective-permute-done.3.short_up
  25.3 3.0 %collective-permute-start.11 = (f32[256,128]{1,0:T(8,128)S(1)}, f32[256,128]{1,0:T(8,128)S(1)}, u32[]{:S(2)}, u32[]{:S(2)}) collective-permute-start(f32[256,128]{1,0:T(8,128)S(1)} %get-tuple-element.36), channel_id=1, source_target_pairs={{0,24},{4,28},{8,0},{12,4},{16,8},{20,12},{24,16},{28,20},{32,56},... | collective-permute-start | bytes 393224 | tf_op jit(solution)/shard_map/ppermute | solution.py:349
  28.3 0.0 collective-permute-done.4.short_down
  28.3 0.5 %collective-permute-start.9 = (f32[256,128]{1,0:T(8,128)S(1)}, f32[256,128]{1,0:T(8,128)S(1)}, u32[]{:S(2)}, u32[]{:S(2)}) collective-permute-start(f32[256,128]{1,0:T(8,128)S(1)} %get-tuple-element.34), channel_id=1, source_target_pairs={{0,16},{4,20},{8,24},{12,28},{16,0},{20,4},{24,8},{28,12},{32,48},... | collective-permute-start | bytes 393224 | tf_op jit(solution)/shard_map/ppermute | solution.py:347
  28.7 0.8 %shard_map.49.mine = f32[768,128]{1,0:T(8,128)S(1)} custom-call(f32[1024,128]{1,0:T(8,128)S(1)} %get-tuple-element.24.l6, f32[584,128]{1,0:T(8,128)S(1)} %collective-permute-done.1.long_up, f32[584,128]{1,0:T(8,128)S(1)} %collective-permute-done.2.long_down, f32[384,128]{1,0:T(8,128)S(1)} %collective-permute-done.3.short_up, ...), custom_call_target="tpu_custom_call" | custom-call | tf_op jit(solution)/shard_map/pallas_call | solution.py:274
  29.6 3.1 %collective-permute-done.10.up = f32[256,128]{1,0:T(8,128)S(1)} collective-permute-done((f32[256,128]{1,0:T(8,128)S(1)}, f32[256,128]{1,0:T(8,128)S(1)}, u32[]{:S(2)}, u32[]{:S(2)}) %collective-permute-start.10) | collective-permute-done | bytes 131104 | tf_op jit(solution)/shard_map/ppermute | solution.py:348
  32.6 0.0 collective-permute-done.11.down
  32.6 2.1 %collective-permute-done.9.far = f32[256,128]{1,0:T(8,128)S(1)} collective-permute-done((f32[256,128]{1,0:T(8,128)S(1)}, f32[256,128]{1,0:T(8,128)S(1)}, u32[]{:S(2)}, u32[]{:S(2)}) %collective-permute-start.9) | collective-permute-done | bytes 131104 | tf_op jit(solution)/shard_map/ppermute | solution.py:347
  34.7 0.0 collective-permute-done.7.mid_down
  34.7 0.0 collective-permute-done.8.high_up
  34.7 1.0 %shard_map.51 = f32[1024,128]{1,0:T(8,128)} custom-call(f32[768,128]{1,0:T(8,128)S(1)} %shard_map.49.mine, f32[384,128]{1,0:T(8,128)S(1)} %collective-permute-done.7.mid_down, f32[384,128]{1,0:T(8,128)S(1)} %collective-permute-done.8.high_up, f32[256,128]{1,0:T(8,128)S(1)} %get-tuple-element.33.mine_head, f32[256,128]{1,0:T(8,128)S(1)} %collective-permute-done.9.far, ...), custom_call_target="tpu_custom_call" | custom-call | tf_op jit(solution)/shard_map/pallas_call | solution.py:274
Async XLA Ops:
  2.9 2.1 %collective-permute-start = (f32[1152,128]{1,0:T(8,128)S(1)}, f32[1152,128]{1,0:T(8,128)S(1)}, u32[]{:S(2)}, u32[]{:S(2)}) collective-permute-start(f32[1152,128]{1,0:T(8,128)S(1)} %get-tuple-element.21.own), channel_id=1, source_target_pairs={{0,4},{4,0},{8,12},{12,8},{16,20},{20,16},{24,28},{28,24},{32,36},... | collective-permute-start | bytes 1769480 | tf_op jit(solution)/shard_map/ppermute | solution.py:315
  5.4 11.2 %collective-permute-start.1 = (f32[584,128]{1,0:T(8,128)S(1)}, f32[584,128]{1,0:T(8,128)S(1)}, u32[]{:S(2)}, u32[]{:S(2)}) collective-permute-start(f32[584,128]{1,0:T(8,128)S(1)} %get-tuple-element.25), channel_id=1, source_target_pairs={{0,8},{4,12},{8,16},{12,20},{16,24},{20,28},{24,0},{28,4},{32,40},... | collective-permute-start | bytes 897032 | tf_op jit(solution)/shard_map/ppermute | solution.py:326
  7.0 11.6 %collective-permute-start.2 = (f32[584,128]{1,0:T(8,128)S(1)}, f32[584,128]{1,0:T(8,128)S(1)}, u32[]{:S(2)}, u32[]{:S(2)}) collective-permute-start(f32[584,128]{1,0:T(8,128)S(1)} %get-tuple-element.26), channel_id=1, source_target_pairs={{0,24},{4,28},{8,0},{12,4},{16,8},{20,12},{24,16},{28,20},{32,56},... | collective-permute-start | bytes 897032 | tf_op jit(solution)/shard_map/ppermute | solution.py:327
  8.7 16.6 %collective-permute-start.3 = (f32[384,128]{1,0:T(8,128)S(1)}, f32[384,128]{1,0:T(8,128)S(1)}, u32[]{:S(2)}, u32[]{:S(2)}) collective-permute-start(f32[384,128]{1,0:T(8,128)S(1)} %get-tuple-element.27), channel_id=1, source_target_pairs={{0,8},{4,12},{8,16},{12,20},{16,24},{20,28},{24,0},{28,4},{32,40},... | collective-permute-start | bytes 589832 | tf_op jit(solution)/shard_map/ppermute | solution.py:328
  9.1 19.2 %collective-permute-start.4 = (f32[384,128]{1,0:T(8,128)S(1)}, f32[384,128]{1,0:T(8,128)S(1)}, u32[]{:S(2)}, u32[]{:S(2)}) collective-permute-start(f32[384,128]{1,0:T(8,128)S(1)} %get-tuple-element.28), channel_id=1, source_target_pairs={{0,24},{4,28},{8,0},{12,4},{16,8},{20,12},{24,16},{28,20},{32,56},... | collective-permute-start | bytes 589832 | tf_op jit(solution)/shard_map/ppermute | solution.py:329
  11.9 11.5 %collective-permute-start.5 = (f32[256,128]{1,0:T(8,128)S(1)}, f32[256,128]{1,0:T(8,128)S(1)}, u32[]{:S(2)}, u32[]{:S(2)}) collective-permute-start(f32[256,128]{1,0:T(8,128)S(1)} %get-tuple-element.29), channel_id=1, source_target_pairs={{0,1},{1,2},{2,3},{3,0},{4,5},{5,6},{6,7},{7,4},{8,9},{9,10},{10,1... | collective-permute-start | bytes 393224 | tf_op jit(solution)/shard_map/ppermute | solution.py:330
  16.6 5.1 %collective-permute-start.6 = (s32[8,128]{1,0:T(8,128)S(1)}, s32[8,128]{1,0:T(8,128)S(1)}, u32[]{:S(2)}, u32[]{:S(2)}) collective-permute-start(s32[8,128]{1,0:T(8,128)S(1)} %get-tuple-element.23.tab), channel_id=1, source_target_pairs={{0,16},{4,20},{8,24},{12,28},{16,0},{20,4},{24,8},{28,12},{32,48},... | collective-permute-start | bytes 12296 | tf_op jit(solution)/shard_map/ppermute | solution.py:316
  19.5 15.2 %collective-permute-start.7 = (f32[384,128]{1,0:T(8,128)S(1)}, f32[384,128]{1,0:T(8,128)S(1)}, u32[]{:S(2)}, u32[]{:S(2)}) collective-permute-start(f32[384,128]{1,0:T(8,128)S(1)} %get-tuple-element.31), channel_id=1, source_target_pairs={{0,24},{4,28},{8,0},{12,4},{16,8},{20,12},{24,16},{28,20},{32,56},... | collective-permute-start | bytes 589832 | tf_op jit(solution)/shard_map/ppermute | solution.py:339
  21.7 13.0 %collective-permute-start.8 = (f32[384,128]{1,0:T(8,128)S(1)}, f32[384,128]{1,0:T(8,128)S(1)}, u32[]{:S(2)}, u32[]{:S(2)}) collective-permute-start(f32[384,128]{1,0:T(8,128)S(1)} %get-tuple-element.32), channel_id=1, source_target_pairs={{0,8},{4,12},{8,16},{12,20},{16,24},{20,28},{24,0},{28,4},{32,40},... | collective-permute-start | bytes 589832 | tf_op jit(solution)/shard_map/ppermute | solution.py:338
  24.9 7.7 %collective-permute-start.10 = (f32[256,128]{1,0:T(8,128)S(1)}, f32[256,128]{1,0:T(8,128)S(1)}, u32[]{:S(2)}, u32[]{:S(2)}) collective-permute-start(f32[256,128]{1,0:T(8,128)S(1)} %get-tuple-element.35), channel_id=1, source_target_pairs={{0,8},{4,12},{8,16},{12,20},{16,24},{20,28},{24,0},{28,4},{32,40},... | collective-permute-start | bytes 393224 | tf_op jit(solution)/shard_map/ppermute | solution.py:348
  25.3 7.3 %collective-permute-start.11 = (f32[256,128]{1,0:T(8,128)S(1)}, f32[256,128]{1,0:T(8,128)S(1)}, u32[]{:S(2)}, u32[]{:S(2)}) collective-permute-start(f32[256,128]{1,0:T(8,128)S(1)} %get-tuple-element.36), channel_id=1, source_target_pairs={{0,24},{4,28},{8,0},{12,4},{16,8},{20,12},{24,16},{28,20},{32,56},... | collective-permute-start | bytes 393224 | tf_op jit(solution)/shard_map/ppermute | solution.py:349
  28.3 6.5 %collective-permute-start.9 = (f32[256,128]{1,0:T(8,128)S(1)}, f32[256,128]{1,0:T(8,128)S(1)}, u32[]{:S(2)}, u32[]{:S(2)}) collective-permute-start(f32[256,128]{1,0:T(8,128)S(1)} %get-tuple-element.34), channel_id=1, source_target_pairs={{0,16},{4,20},{8,24},{12,28},{16,0},{20,4},{24,8},{28,12},{32,48},... | collective-permute-start | bytes 393224 | tf_op jit(solution)/shard_map/ppermute | solution.py:347

commit v3 on v2

--- a/solution.py
+++ b/solution.py
@@ -15,10 +15,13 @@
 CHUNKS = 16
 PITCH = 24
 PACKED = 18
-REACH = 9
+WIDE = 20
+PART = 10
+SPARE = 3
+UP, DOWN = 19 - PART + SPARE, PART - 1 + SPARE
+REST_UP, REST_DOWN = PART - SPARE, 20 - PART - SPARE
 SCALE = 1.0 / math.sqrt(2.0**LEVELS)
 F32 = jnp.float32
-HEAD = ((2, 0, 4), (1, 0, 4), (3, 0, 4), (0, 0, 4))
 
 
 def lanes(count):
@@ -137,35 +140,28 @@
     return (at * LANES + jnp.bitwise_and(late, LANES - 1))[0:1]
 
 
-def shares(src, ahead, codes, parts, put, narrow=False):
-    for part, (which, chunk, count) in enumerate(parts):
-        for row in range(ROWS):
-            code = codes[which, row]
-            at = lax.shift_right_arithmetic(code, 7)
-            if narrow:
-                at = at - lax.shift_left(lax.shift_right_arithmetic(at + 8, 4), 3)
-            turn = jnp.bitwise_and(code, LANES - 1)
-            for first in range(0, count, 8):
-                size = min(8, count - first)
-                to = ahead + chunk + first
-                put(
-                    part,
-                    row * count + first,
-                    size,
-                    turned(src[pl.ds(at + to, size), :], src[pl.ds(at + (to - 1), size), :], turn),
-                )
-
-
-def into(*outs):
-    def put(part, at, size, value):
-        outs[part][pl.ds(at, size), :] = value
+def shares(src, ahead, codes, which, count, put):
+    for row in range(ROWS):
+        code = codes[which, row]
+        at = lax.shift_right_arithmetic(code, 7)
+        turn = jnp.bitwise_and(code, LANES - 1)
+        for first in range(0, count, 8):
+            size = min(8, count - first)
+            to = ahead + first
+            value = turned(
+                src[pl.ds(at + to, size), :], src[pl.ds(at + (to - 1), size), :], turn
+            )
+            put(row * count + first, size, value)
+
+
+def into(out):
+    def put(at, size, value):
+        out[pl.ds(at, size), :] = value
 
     return put
 
 
-def core_main_kernel(
-    own, partner, codes, tab, l6, long_up, long_down, short_up, short_down, edge, both
-):
+def core_main_kernel(own, partner, codes, tab, l6, long_up, long_down, edge, both):
     core = place()[0]
     size = own.shape[0]
     both[pl.ds(pl.multiple_of(core * size, 8), size), :] = own[...]
@@ -178,91 +174,105 @@
         l6[pl.ds(row * CHUNKS + 8, 8), :] = second
         edge[pl.ds(row * 4, 3), :] = second[5:8]
         edge[pl.ds(row * 4 + 3, 1), :] = past
-        at = 8 + row * REACH
-        long_up[pl.ds(at, 1), :] = first[7:8]
-        long_up[pl.ds(at + 1, 8), :] = second
+        at = 8 + row * UP
+        long_up[pl.ds(at, UP - 8), :] = first[16 - UP :]
+        long_up[pl.ds(at + UP - 8, 8), :] = second
+        at = 8 + row * DOWN
         long_down[pl.ds(at, 7), :] = first[1:8]
-        long_down[pl.ds(at + 7, 2), :] = second[0:2]
-        short_up[pl.ds(row * 6, 6), :] = first[1:7]
-        short_down[pl.ds(row * 6, 6), :] = second[2:8]
-
-
-def tables_of(message):
-    return message[0:8, :].astype(jnp.int32)
-
-
-def relay_kernel(long_up, long_down, up, down, plan, terms, sem):
+        long_down[pl.ds(at + 7, DOWN - 7), :] = second[0 : DOWN - 7]
+
+
+def history_kernel(l6, edge, whole, rest_up, rest_down):
+    inner = lax.axis_index("tm") > 0
+    for row in range(ROWS):
+        at = row * WIDE
+        ahead = jnp.where(inner, edge[pl.ds(row * 4, 4), :], 0.0)
+        block = l6[pl.ds(row * CHUNKS, CHUNKS), :]
+        whole[pl.ds(at, 1), :] = jnp.zeros((1, LANES), F32)
+        whole[pl.ds(at + 1, 3), :] = ahead[0:3]
+        whole[pl.ds(at + 4, 1), :] = ahead[3:4] + block[0:1]
+        whole[pl.ds(at + 5, CHUNKS - 1), :] = block[1:]
+        to = row * REST_UP
+        rest_up[pl.ds(to, 3), :] = ahead[0:3]
+        rest_up[pl.ds(to + 3, 1), :] = ahead[3:4] + block[0:1]
+        rest_up[pl.ds(to + 4, REST_UP - 4), :] = block[1 : REST_UP - 3]
+        to = row * REST_DOWN
+        rest_down[pl.ds(to, 3), :] = ahead[0:3]
+        rest_down[pl.ds(to + 3, 1), :] = ahead[3:4] + block[0:1]
+        rest_down[pl.ds(to + 4, REST_DOWN - 4), :] = block[20 - REST_DOWN :]
+
+
+def relay_kernel(long_up, long_down, up, down, terms, plan, sem):
     _, odd, upper = place()
-    below, above = tables_of(long_up), tables_of(long_down)
+    below, above = [message[0:8, :].astype(jnp.int32) for message in (long_up, long_down)]
     same = jnp.bitwise_xor(upper, odd)
     plan[...] = jnp.zeros_like(plan)
-    plan[0:1, :] = term_codes(below, above, 1 - odd, 1 - same, REACH)
-    plan[1:2, :] = term_codes(above, below, 1 - odd, same, REACH)
+    plan[0:1, :] = term_codes(below, above, 1 - odd, 1 - same, UP)
+    plan[1:2, :] = term_codes(above, below, 1 - odd, same, DOWN)
+    plan[2:3, :] = term_codes(below, above, 1 - odd, 1 - same, REST_UP)
+    plan[3:4, :] = term_codes(above, below, 1 - odd, same, 8)
     copy = pltpu.make_async_copy(plan, terms, sem)
     copy.start()
+    up[ROWS * (16 - PART) :, :] = long_up[0:8, :]
     copy.wait()
-    shares(long_up, 11, terms, ((0, 0, 6),), into(up))
-    shares(long_down, 11, terms, ((1, 0, 6),), into(down))
-
-
-def head_kernel(
-    l6, edge, tab, across, long_up, long_down, far, up, down, mine, terms, buf, plan, sem
+    shares(long_up, 11 + SPARE, terms, 0, 16 - PART, into(up))
+    shares(long_down, 11, terms, 1, PART - 4, into(down))
+
+
+def first_relay_kernel(rest_up, rest_down, long_down, terms, tab, up, down, passed, buf):
+    passed[...] = tab[...]
+    shares(rest_up, 5, terms, 2, 2, into(up))
+    for row in range(ROWS):
+        buf[pl.ds(row * 8 + 1, 4), :] = rest_down[pl.ds(row * REST_DOWN, 4), :]
+        buf[pl.ds(row * 8 + 5, 1), :] = long_down[pl.ds(8 + row * DOWN, 1), :]
+    shares(buf, 4, terms, 3, 2, into(down))
+
+
+def direct_kernel(
+    whole, long_up, rest_up, long_down, rest_down, tab, relay, *refs
 ):
+    out, low_buf, high_buf, plan, terms, sem = refs
     _, odd, upper = place()
-    own, other = tab[...], across[...]
-    below, above = tables_of(long_up), tables_of(long_down)
-    pair = jnp.where(odd == 1, below, above)
+    own, other = tab[...], relay[ROWS * (16 - PART) :, :].astype(jnp.int32)
     plan[...] = jnp.zeros_like(plan)
-    plan[0:1, :] = term_codes(own, own, odd, upper, CHUNKS)
-    plan[1:2, :] = term_codes(pair, above, odd, upper, CHUNKS)
-    plan[2:3, :] = term_codes(own, other, odd, upper, CHUNKS)
-    plan[3:4, :] = term_codes(pair, below, odd, upper, CHUNKS)
-    near = term_codes(own, own, 1 - odd, upper, CHUNKS)
-    away = term_codes(other, own, 1 - odd, 1 - upper, CHUNKS)
-    plan[4:5, :] = jnp.where(odd == 1, near, away)
-    plan[5:6, :] = jnp.where(odd == 1, away, near)
+    plan[0:1, :] = term_codes(own, own, odd, upper, WIDE)
+    near = term_codes(own, own, 1 - odd, upper, WIDE)
+    away = term_codes(other, own, 1 - odd, 1 - upper, WIDE)
+    plan[1:2, :] = jnp.where(odd == 1, near, away)
+    plan[2:3, :] = jnp.where(odd == 1, away, near)
     copy = pltpu.make_async_copy(plan, terms, sem)
     copy.start()
-    inner = lax.axis_index("tm") > 0
-    for row in range(ROWS):
-        ahead = jnp.where(inner, edge[pl.ds(row * 4, 4), :], 0.0)
-        buf[pl.ds(row * 8 + 1, 3), :] = ahead[0:3]
-        buf[pl.ds(row * 8 + 4, 1), :] = ahead[3:4] + l6[pl.ds(row * CHUNKS, 1), :]
-        buf[pl.ds(row * 8 + 5, 3), :] = l6[pl.ds(row * CHUNKS + 1, 3), :]
+    for row in range(ROWS):
+        to, rest = row * WIDE, row * REST_DOWN
+        low_buf[pl.ds(to + 1, REST_UP), :] = rest_up[pl.ds(row * REST_UP, REST_UP), :]
+        low_buf[pl.ds(to + 1 + REST_UP, UP), :] = long_up[pl.ds(8 + row * UP, UP), :]
+        high_buf[pl.ds(to + 1, 4), :] = rest_down[pl.ds(rest, 4), :]
+        high_buf[pl.ds(to + 5, DOWN), :] = long_down[pl.ds(8 + row * DOWN, DOWN), :]
+        high_buf[pl.ds(to + 5 + DOWN, REST_DOWN - 4), :] = rest_down[
+            pl.ds(rest + 4, REST_DOWN - 4), :
+        ]
     copy.wait()
-    shares(buf, 4, terms, HEAD, into(far, up, down, mine), narrow=True)
-
-
-def direct_kernel(l6, long_up, long_down, short_up, short_down, terms, out, low_buf, high_buf):
-    for row in range(ROWS):
-        at, to = 8 + row * REACH, row * CHUNKS
-        low_buf[pl.ds(to + 1, 6), :] = short_up[pl.ds(row * 6, 6), :]
-        low_buf[pl.ds(to + 7, 9), :] = long_up[pl.ds(at, 9), :]
-        high_buf[pl.ds(to + 1, 9), :] = long_down[pl.ds(at, 9), :]
-        high_buf[pl.ds(to + 10, 6), :] = short_down[pl.ds(row * 6, 6), :]
-    for row in range(ROWS):
-        for first, count in ((4, 8), (12, 4)):
+    for row in range(ROWS):
+        found = []
+        for which in range(3):
+            code = terms[which, row]
+            found.append((lax.shift_right_arithmetic(code, 7), jnp.bitwise_and(code, LANES - 1)))
+        for first in (0, 8):
+            to = 4 + first
             total = None
-            for which, src in ((0, l6), (4, low_buf), (5, high_buf)):
-                code = terms[which, row]
-                at = lax.shift_right_arithmetic(code, 7)
-                term = turned(
-                    src[pl.ds(at + first, count), :],
-                    src[pl.ds(at + (first - 1), count), :],
-                    jnp.bitwise_and(code, LANES - 1),
-                )
+            for src, (at, turn) in zip((whole, low_buf, high_buf), found):
+                term = turned(src[pl.ds(at + to, 8), :], src[pl.ds(at + (to - 1), 8), :], turn)
                 total = term if total is None else total + term
-            out[pl.ds(row * 12 + first - 4, count), :] = total
-
-
-def last_kernel(mine, mid_down, high_up, mine_head, far, up, down, out):
+            out[pl.ds(row * CHUNKS + first, 8), :] = total
+
+
+def last_kernel(mine, down_first, up_first, down, up, out):
+    spans = ((down_first, 0, 2), (up_first, 2, 2), (down, 4, PART - 4), (up, PART, 16 - PART))
     for row in range(ROWS):
         at = (row // 8) * 128 + row % 8
-        head = [a[pl.ds(row * 4, 4), :] for a in (mine_head, far, up, down)]
-        out[pl.ds(at, 4, stride=8), :] = (head[0] + head[1] + head[2] + head[3]) * SCALE
-        for chunk, arrived in ((4, mid_down), (10, high_up)):
-            value = mine[pl.ds(row * 12 + chunk - 4, 6), :] + arrived[pl.ds(row * 6, 6), :]
-            out[pl.ds(at + 8 * chunk, 6, stride=8), :] = value * SCALE
+        for arrived, chunk, count in spans:
+            value = mine[pl.ds(row * CHUNKS + chunk, count), :] + arrived[pl.ds(row * count, count), :]
+            out[pl.ds(at + 8 * chunk, count, stride=8), :] = value * SCALE
 
 
 def call(kernel, ins, outs, scratch=()):
@@ -313,49 +323,52 @@
         + [sem((8,))],
     )
     l5_far = lax.ppermute(l5, "freq", swap(1))
-    across = lax.ppermute(own_tab, "freq", swap(4))
-    l6, long_up, long_down, short_up, short_down, edge = call(
+    l6, long_up, long_down, edge = call(
         core_main_kernel,
         [(l5, "v"), (l5_far, "v"), (codes, "t"), (own_tab, "v")],
-        [pinned(1024)]
-        + [pinned(8 + ROWS * REACH)] * 2
-        + [pinned(ROWS * 6)] * 2
-        + [pinned(ROWS * 4)],
+        [pinned(1024), pinned(8 + ROWS * UP), pinned(8 + ROWS * DOWN), pinned(ROWS * 4)],
         [pltpu.VMEM((2 * ROWS * PACKED, LANES), F32)],
     )
     long_up = lax.ppermute(long_up, "freq", one_up)
     long_down = lax.ppermute(long_down, "freq", one_down)
-    short_up = lax.ppermute(short_up, "freq", one_up)
-    short_down = lax.ppermute(short_down, "freq", one_down)
     edge = lax.ppermute(edge, "tm", [(i, (i + 1) % 4) for i in range(4)])
 
-    relay_up, relay_down = call(
+    whole, rest_up, rest_down = call(
+        history_kernel,
+        [(l6, "v"), (edge, "v")],
+        [pinned(ROWS * WIDE), pinned(ROWS * REST_UP), pinned(ROWS * REST_DOWN)],
+    )
+    rest_up = lax.ppermute(rest_up, "freq", one_up)
+    rest_down = lax.ppermute(rest_down, "freq", one_down)
+
+    relay_up, relay_down, terms = call(
         relay_kernel,
         [(long_up, "v"), (long_down, "v")],
-        [pinned(ROWS * 6), pinned(ROWS * 6)],
-        [plan, terms_ref, sem],
-    )
-    high_up = lax.ppermute(relay_up, "freq", one_up)
-    mid_down = lax.ppermute(relay_down, "freq", one_down)
-
-    head_far, head_up, head_down, mine_head, terms = call(
-        head_kernel,
-        [(a, "v") for a in (l6, edge, own_tab, across, long_up, long_down)],
-        [pinned(ROWS * 4)] * 4 + [terms_ref],
-        [pltpu.VMEM((512, LANES), F32), plan, sem],
-    )
-    far = lax.ppermute(head_far, "freq", swap(4))
-    up = lax.ppermute(head_up, "freq", one_up)
-    down = lax.ppermute(head_down, "freq", one_down)
+        [pinned(ROWS * (16 - PART) + 8), pinned(ROWS * (PART - 4)), terms_ref],
+        [plan, sem],
+    )
+    up = lax.ppermute(relay_up, "freq", one_up)
+    down = lax.ppermute(relay_down, "freq", one_down)
+
+    relay_up, relay_down, tab = call(
+        first_relay_kernel,
+        [(rest_up, "v"), (rest_down, "v"), (long_down, "v"), (terms, "t"), (own_tab, "v")],
+        [pinned(ROWS * 2), pinned(ROWS * 2), pinned(8, LANES, ints)],
+        [pltpu.VMEM((512, LANES), F32)],
+    )
+    up_first = lax.ppermute(relay_up, "freq", one_up)
+    down_first = lax.ppermute(relay_down, "freq", one_down)
+
     (mine,) = call(
         direct_kernel,
-        [(a, "v") for a in (l6, long_up, long_down, short_up, short_down)] + [(terms, "t")],
-        [pinned(ROWS * 12)],
-        [pltpu.VMEM((1024, LANES), F32)] * 2,
-    )
-    last = [mine, mid_down, high_up, mine_head, far, up, down]
+        [(a, "v") for a in (whole, long_up, rest_up, long_down, rest_down, tab, up)],
+        [pinned(ROWS * CHUNKS)],
+        [pltpu.VMEM((ROWS * WIDE, LANES), F32)] * 2 + [plan, terms_ref, sem],
+    )
     (out,) = call(
-        last_kernel, [(a, "v") for a in last], [jax.ShapeDtypeStruct((1024, LANES), F32)]
+        last_kernel,
+        [(a, "v") for a in (mine, down_first, up_first, down, up)],
+        [jax.ShapeDtypeStruct((1024, LANES), F32)],
     )
     return out.reshape(8, CHUNKS, 8, LANES).transpose(0, 2, 1, 3).reshape(ROWS, CHUNKS * LANES)
 

time: 35.9 us -> 33.6 us (0.936)
  starting transfers between devices: 16.9 us -> 14.4 us
  waiting for transfers between devices: 11.2 us -> 12 us
  Pallas kernels: 7.62 us -> 7.03 us
    ppermute x1, waiting for transfers between devices: 0.01 us -> 4.84 us  [on_device(): edge = lax.ppermute(edge, 'tm', [(i, (i + 1) % 4) for i in range(4)])]
    ppermute x1, waiting for transfers between devices: 3.18 us -> 0.01 us  [on_device(): long_up = lax.ppermute(long_up, 'freq', one_up)]
    ppermute x8 -> x6, starting transfers between devices: 12 us -> 9.49 us  [the longest x1 3.02 us: on_device(): rest_down = lax.ppermute(rest_down, 'freq', one_down)]
    ppermute x8 -> x6, waiting for transfers between devices: 5.99 us -> 4.62 us  [the longest x1 3.57 us: on_device(): up_first = lax.ppermute(relay_up, 'freq', one_up)]
    pallas_call x6 -> x7, Pallas kernels: 7.62 us -> 7.03 us  [call(): pl.pallas_call(kernel, out_shape=outs, in_specs=[pl.BlockSpec(memory_spac...]
    ppermute x1, waiting for transfers between devices: 0.01 us -> 0.58 us  [on_device(): long_down = lax.ppermute(long_down, 'freq', one_down)]
  transfers between devices with their start and end apart: 12 -> 10, of which waited for: 5 -> 8; matrix products, arithmetic and copies ran while one was open for 0% -> 0% of each run, Pallas kernels for 9% -> 8%
where the time goes in v3:
time: 33.6 us; the launch traced here: 33.5 us
  starting transfers between devices  14.4 us (43%)
  waiting for transfers between devices  12 us (36%)
  Pallas kernels  7.03 us (21%)
    pallas_call x7, Pallas kernels, call(): pl.pallas_call(kernel, out_shape=outs, in_specs=[pl.BlockSpec(memory_spac...  7.03 us
    ppermute x1, waiting for transfers between devices, on_device(): edge = lax.ppermute(edge, 'tm', [(i, (i + 1) % 4) for i in range(4)])  4.84 us
    ppermute x1, waiting for transfers between devices, on_device(): up_first = lax.ppermute(relay_up, 'freq', one_up)  3.57 us
    ppermute x1, starting transfers between devices, on_device(): rest_down = lax.ppermute(rest_down, 'freq', one_down)  3.02 us
    ppermute x1, starting transfers between devices, on_device(): down_first = lax.ppermute(relay_down, 'freq', one_down)  2.86 us
    ppermute x1, waiting for transfers between devices, on_device(): l5_far = lax.ppermute(l5, 'freq', swap(1))  1.99 us
    ppermute x1, starting transfers between devices, on_device(): long_down = lax.ppermute(long_down, 'freq', one_down)  1.67 us
    ppermute x1, starting transfers between devices, on_device(): up = lax.ppermute(relay_up, 'freq', one_up)  1.67 us
  transfers between devices with their start and end apart: 10, of which 8 were waited for; matrix products, arithmetic and copies ran while one was open for 0% of the time, Pallas kernels for 8%

profile of v3, /device:TPU:96, one launch (start us, length us, event | category | flops | bytes accessed | tf_op | source)
XLA Modules:
  0.0 33.5 jit_solution(6172184758957444957)
XLA Ops:
  0.0 2.9 %shard_map.46 = (f32[1152,128]{1,0:T(8,128)S(1)}, s32[8,128]{1,0:T(8,128)S(1)}, s32[16,128]{1,0:T(8,128)S(4)}) custom-call(f32[1024,128]{1,0:T(8,128)} %bitcast.10, s32[9,64]{1,0:T(8,128)} %low_h.1, s32[9,64]{1,0:T(8,128)} %high_h.1, s32[9,64]{1,0:T(8,128)} %lag_h.1), custom_call_target="tpu_custom_call" | custom-call | tf_op jit(solution)/shard_map/pallas_call | solution.py:284
  2.9 0.1 collective-permute-start
  3.0 2.0 %collective-permute-done.partner = f32[1152,128]{1,0:T(8,128)S(1)} collective-permute-done((f32[1152,128]{1,0:T(8,128)S(1)}, f32[1152,128]{1,0:T(8,128)S(1)}, u32[]{:S(2)}, u32[]{:S(2)}) %collective-permute-start) | collective-permute-done | bytes 589856 | tf_op jit(solution)/shard_map/ppermute | solution.py:325
  5.0 0.4 %shard_map.47 = (f32[1024,128]{1,0:T(8,128)S(1)}, f32[776,128]{1,0:T(8,128)S(1)}, f32[776,128]{1,0:T(8,128)S(1)}, f32[256,128]{1,0:T(8,128)S(1)}) custom-call(f32[1152,128]{1,0:T(8,128)S(1)} %get-tuple-element.21.own, f32[1152,128]{1,0:T(8,128)S(1)} %collective-permute-done.partner, s32[16,128]{1,0:T(8,128)S(4)} %get-tuple-element.22.codes, ...), custom_call_target="tpu_custom_call" | custom-call | tf_op jit(solution)/shard_map/pallas_call | solution.py:284
  5.4 1.6 %collective-permute-start.2 = (f32[776,128]{1,0:T(8,128)S(1)}, f32[776,128]{1,0:T(8,128)S(1)}, u32[]{:S(2)}, u32[]{:S(2)}) collective-permute-start(f32[776,128]{1,0:T(8,128)S(1)} %get-tuple-element.27), channel_id=1, source_target_pairs={{0,8},{4,12},{8,16},{12,20},{16,24},{20,28},{24,0},{28,4},{32,40},... | collective-permute-start | bytes 1191944 | tf_op jit(solution)/shard_map/ppermute | solution.py:332
  7.0 1.7 %collective-permute-start.4 = (f32[776,128]{1,0:T(8,128)S(1)}, f32[776,128]{1,0:T(8,128)S(1)}, u32[]{:S(2)}, u32[]{:S(2)}) collective-permute-start(f32[776,128]{1,0:T(8,128)S(1)} %get-tuple-element.29), channel_id=1, source_target_pairs={{0,24},{4,28},{8,0},{12,4},{16,8},{20,12},{24,16},{28,20},{32,56},... | collective-permute-start | bytes 1191944 | tf_op jit(solution)/shard_map/ppermute | solution.py:333
  8.7 1.5 %collective-permute-start.1 = (f32[256,128]{1,0:T(8,128)S(1)}, f32[256,128]{1,0:T(8,128)S(1)}, u32[]{:S(2)}, u32[]{:S(2)}) collective-permute-start(f32[256,128]{1,0:T(8,128)S(1)} %get-tuple-element.25), channel_id=1, source_target_pairs={{0,1},{1,2},{2,3},{3,0},{4,5},{5,6},{6,7},{7,4},{8,9},{9,10},{10,1... | collective-permute-start | bytes 393224 | tf_op jit(solution)/shard_map/ppermute | solution.py:334
  10.2 4.8 %collective-permute-done.1.edge = f32[256,128]{1,0:T(8,128)S(1)} collective-permute-done((f32[256,128]{1,0:T(8,128)S(1)}, f32[256,128]{1,0:T(8,128)S(1)}, u32[]{:S(2)}, u32[]{:S(2)}) %collective-permute-start.1) | collective-permute-done | bytes 131104 | tf_op jit(solution)/shard_map/ppermute | solution.py:334
  15.0 0.2 shard_map.48
  15.2 0.3 collective-permute-start.3
  15.5 3.0 %collective-permute-start.5 = (f32[448,128]{1,0:T(8,128)S(1)}, f32[448,128]{1,0:T(8,128)S(1)}, u32[]{:S(2)}, u32[]{:S(2)}) collective-permute-start(f32[448,128]{1,0:T(8,128)S(1)} %get-tuple-element.30), channel_id=1, source_target_pairs={{0,24},{4,28},{8,0},{12,4},{16,8},{20,12},{24,16},{28,20},{32,56},... | collective-permute-start | bytes 688136 | tf_op jit(solution)/shard_map/ppermute | solution.py:342
  18.5 0.0 collective-permute-done.2.long_up
  18.5 0.6 %collective-permute-done.4.long_down = f32[776,128]{1,0:T(8,128)S(1)} collective-permute-done((f32[776,128]{1,0:T(8,128)S(1)}, f32[776,128]{1,0:T(8,128)S(1)}, u32[]{:S(2)}, u32[]{:S(2)}) %collective-permute-start.4) | collective-permute-done | bytes 397344 | tf_op jit(solution)/shard_map/ppermute | solution.py:333
  19.1 1.0 %shard_map.49 = (f32[392,128]{1,0:T(8,128)S(1)}, f32[384,128]{1,0:T(8,128)S(1)}, s32[8,128]{1,0:T(8,128)S(4)}) custom-call(f32[776,128]{1,0:T(8,128)S(1)} %collective-permute-done.2.long_up, f32[776,128]{1,0:T(8,128)S(1)} %collective-permute-done.4.long_down), custom_call_target="tpu_custom_call" | custom-call | tf_op jit(solution)/shard_map/pallas_call | solution.py:284
  20.1 1.7 %collective-permute-start.6 = (f32[392,128]{1,0:T(8,128)S(1)}, f32[392,128]{1,0:T(8,128)S(1)}, u32[]{:S(2)}, u32[]{:S(2)}) collective-permute-start(f32[392,128]{1,0:T(8,128)S(1)} %get-tuple-element.33), channel_id=1, source_target_pairs={{0,8},{4,12},{8,16},{12,20},{16,24},{20,28},{24,0},{28,4},{32,40},... | collective-permute-start | bytes 602120 | tf_op jit(solution)/shard_map/ppermute | solution.py:350
  21.8 1.6 %collective-permute-start.9 = (f32[384,128]{1,0:T(8,128)S(1)}, f32[384,128]{1,0:T(8,128)S(1)}, u32[]{:S(2)}, u32[]{:S(2)}) collective-permute-start(f32[384,128]{1,0:T(8,128)S(1)} %get-tuple-element.36), channel_id=1, source_target_pairs={{0,24},{4,28},{8,0},{12,4},{16,8},{20,12},{24,16},{28,20},{32,56},... | collective-permute-start | bytes 589832 | tf_op jit(solution)/shard_map/ppermute | solution.py:351
  23.4 0.1 collective-permute-done.3.rest_up
  23.5 0.3 %collective-permute-done.5.rest_down = f32[448,128]{1,0:T(8,128)S(1)} collective-permute-done((f32[448,128]{1,0:T(8,128)S(1)}, f32[448,128]{1,0:T(8,128)S(1)}, u32[]{:S(2)}, u32[]{:S(2)}) %collective-permute-start.5) | collective-permute-done | bytes 229408 | tf_op jit(solution)/shard_map/ppermute | solution.py:342
  23.8 0.3 shard_map.50
  24.1 2.9 %collective-permute-start.7 = (f32[128,128]{1,0:T(8,128)S(1)}, f32[128,128]{1,0:T(8,128)S(1)}, u32[]{:S(2)}, u32[]{:S(2)}) collective-permute-start(f32[128,128]{1,0:T(8,128)S(1)} %get-tuple-element.34), channel_id=1, source_target_pairs={{0,24},{4,28},{8,0},{12,4},{16,8},{20,12},{24,16},{28,20},{32,56},... | collective-permute-start | bytes 196616 | tf_op jit(solution)/shard_map/ppermute | solution.py:360
  27.0 0.0 collective-permute-start.8
  27.0 0.2 collective-permute-done.6.relay.up
  27.2 1.2 %shard_map.51.mine = f32[1024,128]{1,0:T(8,128)S(1)} custom-call(f32[1280,128]{1,0:T(8,128)S(1)} %get-tuple-element.26.whole, f32[776,128]{1,0:T(8,128)S(1)} %collective-permute-done.2.long_up, f32[448,128]{1,0:T(8,128)S(1)} %collective-permute-done.3.rest_up, f32[776,128]{1,0:T(8,128)S(1)} %collective-permute-done.4.long_down, ...), custom_call_target="tpu_custom_call" | custom-call | tf_op jit(solution)/shard_map/pallas_call | solution.py:284
  28.4 0.4 %collective-permute-done.7.down_first = f32[128,128]{1,0:T(8,128)S(1)} collective-permute-done((f32[128,128]{1,0:T(8,128)S(1)}, f32[128,128]{1,0:T(8,128)S(1)}, u32[]{:S(2)}, u32[]{:S(2)}) %collective-permute-start.7) | collective-permute-done | bytes 65568 | tf_op jit(solution)/shard_map/ppermute | solution.py:360
  28.9 3.6 %collective-permute-done.8.up_first = f32[128,128]{1,0:T(8,128)S(1)} collective-permute-done((f32[128,128]{1,0:T(8,128)S(1)}, f32[128,128]{1,0:T(8,128)S(1)}, u32[]{:S(2)}, u32[]{:S(2)}) %collective-permute-start.8) | collective-permute-done | bytes 65568 | tf_op jit(solution)/shard_map/ppermute | solution.py:359
  32.4 0.0 collective-permute-done.9.down
  32.4 1.1 %shard_map.52 = f32[1024,128]{1,0:T(8,128)} custom-call(f32[1024,128]{1,0:T(8,128)S(1)} %shard_map.51.mine, f32[128,128]{1,0:T(8,128)S(1)} %collective-permute-done.7.down_first, f32[128,128]{1,0:T(8,128)S(1)} %collective-permute-done.8.up_first, f32[384,128]{1,0:T(8,128)S(1)} %collective-permute-done.9.down, f32[392,128]{1,0:T(8,128)S(1)} %collective-permute-done.6.relay.up), custom_call_target="tpu_custom_call" | custom-call | tf_op jit(solution)/shard_map/pallas_call | solution.py:284
Async XLA Ops:
  2.9 2.1 %collective-permute-start = (f32[1152,128]{1,0:T(8,128)S(1)}, f32[1152,128]{1,0:T(8,128)S(1)}, u32[]{:S(2)}, u32[]{:S(2)}) collective-permute-start(f32[1152,128]{1,0:T(8,128)S(1)} %get-tuple-element.21.own), channel_id=1, source_target_pairs={{0,4},{4,0},{8,12},{12,8},{16,20},{20,16},{24,28},{28,24},{32,36},... | collective-permute-start | bytes 1769480 | tf_op jit(solution)/shard_map/ppermute | solution.py:325
  5.4 13.2 %collective-permute-start.2 = (f32[776,128]{1,0:T(8,128)S(1)}, f32[776,128]{1,0:T(8,128)S(1)}, u32[]{:S(2)}, u32[]{:S(2)}) collective-permute-start(f32[776,128]{1,0:T(8,128)S(1)} %get-tuple-element.27), channel_id=1, source_target_pairs={{0,8},{4,12},{8,16},{12,20},{16,24},{20,28},{24,0},{28,4},{32,40},... | collective-permute-start | bytes 1191944 | tf_op jit(solution)/shard_map/ppermute | solution.py:332
  7.0 12.1 %collective-permute-start.4 = (f32[776,128]{1,0:T(8,128)S(1)}, f32[776,128]{1,0:T(8,128)S(1)}, u32[]{:S(2)}, u32[]{:S(2)}) collective-permute-start(f32[776,128]{1,0:T(8,128)S(1)} %get-tuple-element.29), channel_id=1, source_target_pairs={{0,24},{4,28},{8,0},{12,4},{16,8},{20,12},{24,16},{28,20},{32,56},... | collective-permute-start | bytes 1191944 | tf_op jit(solution)/shard_map/ppermute | solution.py:333
  8.7 6.3 %collective-permute-start.1 = (f32[256,128]{1,0:T(8,128)S(1)}, f32[256,128]{1,0:T(8,128)S(1)}, u32[]{:S(2)}, u32[]{:S(2)}) collective-permute-start(f32[256,128]{1,0:T(8,128)S(1)} %get-tuple-element.25), channel_id=1, source_target_pairs={{0,1},{1,2},{2,3},{3,0},{4,5},{5,6},{6,7},{7,4},{8,9},{9,10},{10,1... | collective-permute-start | bytes 393224 | tf_op jit(solution)/shard_map/ppermute | solution.py:334
  15.2 8.3 %collective-permute-start.3 = (f32[448,128]{1,0:T(8,128)S(1)}, f32[448,128]{1,0:T(8,128)S(1)}, u32[]{:S(2)}, u32[]{:S(2)}) collective-permute-start(f32[448,128]{1,0:T(8,128)S(1)} %get-tuple-element.28), channel_id=1, source_target_pairs={{0,8},{4,12},{8,16},{12,20},{16,24},{20,28},{24,0},{28,4},{32,40},... | collective-permute-start | bytes 688136 | tf_op jit(solution)/shard_map/ppermute | solution.py:341
  15.5 8.3 %collective-permute-start.5 = (f32[448,128]{1,0:T(8,128)S(1)}, f32[448,128]{1,0:T(8,128)S(1)}, u32[]{:S(2)}, u32[]{:S(2)}) collective-permute-start(f32[448,128]{1,0:T(8,128)S(1)} %get-tuple-element.30), channel_id=1, source_target_pairs={{0,24},{4,28},{8,0},{12,4},{16,8},{20,12},{24,16},{28,20},{32,56},... | collective-permute-start | bytes 688136 | tf_op jit(solution)/shard_map/ppermute | solution.py:342
  20.1 7.1 %collective-permute-start.6 = (f32[392,128]{1,0:T(8,128)S(1)}, f32[392,128]{1,0:T(8,128)S(1)}, u32[]{:S(2)}, u32[]{:S(2)}) collective-permute-start(f32[392,128]{1,0:T(8,128)S(1)} %get-tuple-element.33), channel_id=1, source_target_pairs={{0,8},{4,12},{8,16},{12,20},{16,24},{20,28},{24,0},{28,4},{32,40},... | collective-permute-start | bytes 602120 | tf_op jit(solution)/shard_map/ppermute | solution.py:350
  21.8 10.7 %collective-permute-start.9 = (f32[384,128]{1,0:T(8,128)S(1)}, f32[384,128]{1,0:T(8,128)S(1)}, u32[]{:S(2)}, u32[]{:S(2)}) collective-permute-start(f32[384,128]{1,0:T(8,128)S(1)} %get-tuple-element.36), channel_id=1, source_target_pairs={{0,24},{4,28},{8,0},{12,4},{16,8},{20,12},{24,16},{28,20},{32,56},... | collective-permute-start | bytes 589832 | tf_op jit(solution)/shard_map/ppermute | solution.py:351
  24.1 4.8 %collective-permute-start.7 = (f32[128,128]{1,0:T(8,128)S(1)}, f32[128,128]{1,0:T(8,128)S(1)}, u32[]{:S(2)}, u32[]{:S(2)}) collective-permute-start(f32[128,128]{1,0:T(8,128)S(1)} %get-tuple-element.34), channel_id=1, source_target_pairs={{0,24},{4,28},{8,0},{12,4},{16,8},{20,12},{24,16},{28,20},{32,56},... | collective-permute-start | bytes 196616 | tf_op jit(solution)/shard_map/ppermute | solution.py:360
  27.0 5.5 %collective-permute-start.8 = (f32[128,128]{1,0:T(8,128)S(1)}, f32[128,128]{1,0:T(8,128)S(1)}, u32[]{:S(2)}, u32[]{:S(2)}) collective-permute-start(f32[128,128]{1,0:T(8,128)S(1)} %get-tuple-element.35), channel_id=1, source_target_pairs={{0,8},{4,12},{8,16},{12,20},{16,24},{20,28},{24,0},{28,4},{32,40},... | collective-permute-start | bytes 196616 | tf_op jit(solution)/shard_map/ppermute | solution.py:359

commit v4 on v3

--- a/solution.py
+++ b/solution.py
@@ -16,10 +16,8 @@
 PITCH = 24
 PACKED = 18
 WIDE = 20
-PART = 10
-SPARE = 3
-UP, DOWN = 19 - PART + SPARE, PART - 1 + SPARE
-REST_UP, REST_DOWN = PART - SPARE, 20 - PART - SPARE
+TO_PAIR, TO_CROSS = 12, 12
+PAIR_REST, CROSS_REST = 19 - TO_PAIR, 19 - TO_CROSS
 SCALE = 1.0 / math.sqrt(2.0**LEVELS)
 F32 = jnp.float32
 
@@ -161,12 +159,12 @@
     return put
 
 
-def core_main_kernel(own, partner, codes, tab, l6, long_up, long_down, edge, both):
+def core_main_kernel(own, partner, codes, tab, l6, to_pair, to_cross, edge, both):
     core = place()[0]
     size = own.shape[0]
     both[pl.ds(pl.multiple_of(core * size, 8), size), :] = own[...]
     both[pl.ds(pl.multiple_of((1 - core) * size, 8), size), :] = partner[...]
-    for message in (long_up, long_down):
+    for message in (to_pair, to_cross):
         message[0:8, :] = tab[...].astype(F32)
     for row in range(ROWS):
         first, second, past = pieces(both, codes[LOCAL, row], 1, size + 1, WHOLE)
@@ -174,15 +172,15 @@
         l6[pl.ds(row * CHUNKS + 8, 8), :] = second
         edge[pl.ds(row * 4, 3), :] = second[5:8]
         edge[pl.ds(row * 4 + 3, 1), :] = past
-        at = 8 + row * UP
-        long_up[pl.ds(at, UP - 8), :] = first[16 - UP :]
-        long_up[pl.ds(at + UP - 8, 8), :] = second
-        at = 8 + row * DOWN
-        long_down[pl.ds(at, 7), :] = first[1:8]
-        long_down[pl.ds(at + 7, DOWN - 7), :] = second[0 : DOWN - 7]
-
-
-def history_kernel(l6, edge, whole, rest_up, rest_down):
+        at = 8 + row * TO_PAIR
+        to_pair[pl.ds(at, TO_PAIR - 8), :] = first[16 - TO_PAIR :]
+        to_pair[pl.ds(at + TO_PAIR - 8, 8), :] = second
+        at = 8 + row * TO_CROSS
+        to_cross[pl.ds(at, 7), :] = first[1:8]
+        to_cross[pl.ds(at + 7, TO_CROSS - 7), :] = second[0 : TO_CROSS - 7]
+
+
+def history_kernel(l6, edge, whole, pair_rest, cross_rest):
     inner = lax.axis_index("tm") > 0
     for row in range(ROWS):
         at = row * WIDE
@@ -192,64 +190,64 @@
         whole[pl.ds(at + 1, 3), :] = ahead[0:3]
         whole[pl.ds(at + 4, 1), :] = ahead[3:4] + block[0:1]
         whole[pl.ds(at + 5, CHUNKS - 1), :] = block[1:]
-        to = row * REST_UP
-        rest_up[pl.ds(to, 3), :] = ahead[0:3]
-        rest_up[pl.ds(to + 3, 1), :] = ahead[3:4] + block[0:1]
-        rest_up[pl.ds(to + 4, REST_UP - 4), :] = block[1 : REST_UP - 3]
-        to = row * REST_DOWN
-        rest_down[pl.ds(to, 3), :] = ahead[0:3]
-        rest_down[pl.ds(to + 3, 1), :] = ahead[3:4] + block[0:1]
-        rest_down[pl.ds(to + 4, REST_DOWN - 4), :] = block[20 - REST_DOWN :]
-
-
-def relay_kernel(long_up, long_down, up, down, terms, plan, sem):
+        to = row * PAIR_REST
+        pair_rest[pl.ds(to, 3), :] = ahead[0:3]
+        pair_rest[pl.ds(to + 3, 1), :] = ahead[3:4] + block[0:1]
+        pair_rest[pl.ds(to + 4, PAIR_REST - 4), :] = block[1 : PAIR_REST - 3]
+        to = row * CROSS_REST
+        cross_rest[pl.ds(to, 3), :] = ahead[0:3]
+        cross_rest[pl.ds(to + 3, 1), :] = ahead[3:4] + block[0:1]
+        cross_rest[pl.ds(to + 4, CROSS_REST - 4), :] = block[TO_CROSS + 1 :]
+
+
+def tables_of(message):
+    return message[0:8, :].astype(jnp.int32)
+
+
+def relay_kernel(pair, cross, for_pair, for_cross, terms, plan, sem):
     _, odd, upper = place()
-    below, above = [message[0:8, :].astype(jnp.int32) for message in (long_up, long_down)]
-    same = jnp.bitwise_xor(upper, odd)
+    pair_tab, cross_tab = tables_of(pair), tables_of(cross)
     plan[...] = jnp.zeros_like(plan)
-    plan[0:1, :] = term_codes(below, above, 1 - odd, 1 - same, UP)
-    plan[1:2, :] = term_codes(above, below, 1 - odd, same, DOWN)
-    plan[2:3, :] = term_codes(below, above, 1 - odd, 1 - same, REST_UP)
-    plan[3:4, :] = term_codes(above, below, 1 - odd, same, 8)
+    plan[0:1, :] = term_codes(cross_tab, pair_tab, 1 - odd, 1 - upper, TO_CROSS)
+    plan[1:2, :] = term_codes(pair_tab, cross_tab, 1 - odd, upper, TO_PAIR)
+    plan[2:3, :] = term_codes(cross_tab, pair_tab, 1 - odd, 1 - upper, 8)
     copy = pltpu.make_async_copy(plan, terms, sem)
     copy.start()
-    up[ROWS * (16 - PART) :, :] = long_up[0:8, :]
+    for_pair[ROWS * 4 :, :] = cross[0:8, :]
     copy.wait()
-    shares(long_up, 11 + SPARE, terms, 0, 16 - PART, into(up))
-    shares(long_down, 11, terms, 1, PART - 4, into(down))
-
-
-def first_relay_kernel(rest_up, rest_down, long_down, terms, tab, up, down, passed, buf):
-    passed[...] = tab[...]
-    shares(rest_up, 5, terms, 2, 2, into(up))
-    for row in range(ROWS):
-        buf[pl.ds(row * 8 + 1, 4), :] = rest_down[pl.ds(row * REST_DOWN, 4), :]
-        buf[pl.ds(row * 8 + 5, 1), :] = long_down[pl.ds(8 + row * DOWN, 1), :]
-    shares(buf, 4, terms, 3, 2, into(down))
-
-
-def direct_kernel(
-    whole, long_up, rest_up, long_down, rest_down, tab, relay, *refs
-):
-    out, low_buf, high_buf, plan, terms, sem = refs
+    shares(cross, 8 + 3, terms, 0, 4, into(for_pair))
+    shares(pair, 8 + TO_PAIR - 8, terms, 1, 8, into(for_cross))
+
+
+def first_relay_kernel(pair, pair_rest, cross, cross_rest, terms, for_pair, pair_whole, buf):
+    for row in range(ROWS):
+        buf[pl.ds(row * 8 + 1, 4), :] = cross_rest[pl.ds(row * CROSS_REST, 4), :]
+        buf[pl.ds(row * 8 + 5, 3), :] = cross[pl.ds(8 + row * TO_CROSS, 3), :]
+    shares(buf, 4, terms, 2, 4, into(for_pair))
+    for row in range(ROWS):
+        to = row * WIDE
+        pair_whole[pl.ds(to, 1), :] = jnp.zeros((1, LANES), F32)
+        pair_whole[pl.ds(to + 1, PAIR_REST), :] = pair_rest[pl.ds(row * PAIR_REST, PAIR_REST), :]
+        pair_whole[pl.ds(to + 1 + PAIR_REST, TO_PAIR), :] = pair[
+            pl.ds(8 + row * TO_PAIR, TO_PAIR), :
+        ]
+
+
+def direct_kernel(whole, pair_whole, cross, cross_rest, tab, relay, out, buf, plan, terms, sem):
     _, odd, upper = place()
-    own, other = tab[...], relay[ROWS * (16 - PART) :, :].astype(jnp.int32)
+    own, other = tab[...], relay[ROWS * 4 :, :].astype(jnp.int32)
     plan[...] = jnp.zeros_like(plan)
     plan[0:1, :] = term_codes(own, own, odd, upper, WIDE)
-    near = term_codes(own, own, 1 - odd, upper, WIDE)
-    away = term_codes(other, own, 1 - odd, 1 - upper, WIDE)
-    plan[1:2, :] = jnp.where(odd == 1, near, away)
-    plan[2:3, :] = jnp.where(odd == 1, away, near)
+    plan[1:2, :] = term_codes(own, own, 1 - odd, upper, WIDE)
+    plan[2:3, :] = term_codes(other, own, 1 - odd, 1 - upper, WIDE)
     copy = pltpu.make_async_copy(plan, terms, sem)
     copy.start()
     for row in range(ROWS):
-        to, rest = row * WIDE, row * REST_DOWN
-        low_buf[pl.ds(to + 1, REST_UP), :] = rest_up[pl.ds(row * REST_UP, REST_UP), :]
-        low_buf[pl.ds(to + 1 + REST_UP, UP), :] = long_up[pl.ds(8 + row * UP, UP), :]
-        high_buf[pl.ds(to + 1, 4), :] = rest_down[pl.ds(rest, 4), :]
-        high_buf[pl.ds(to + 5, DOWN), :] = long_down[pl.ds(8 + row * DOWN, DOWN), :]
-        high_buf[pl.ds(to + 5 + DOWN, REST_DOWN - 4), :] = rest_down[
-            pl.ds(rest + 4, REST_DOWN - 4), :
+        to, rest = row * WIDE, row * CROSS_REST
+        buf[pl.ds(to + 1, 4), :] = cross_rest[pl.ds(rest, 4), :]
+        buf[pl.ds(to + 5, TO_CROSS), :] = cross[pl.ds(8 + row * TO_CROSS, TO_CROSS), :]
+        buf[pl.ds(to + 5 + TO_CROSS, CROSS_REST - 4), :] = cross_rest[
+            pl.ds(rest + 4, CROSS_REST - 4), :
         ]
     copy.wait()
     for row in range(ROWS):
@@ -260,17 +258,16 @@
         for first in (0, 8):
             to = 4 + first
             total = None
-            for src, (at, turn) in zip((whole, low_buf, high_buf), found):
+            for src, (at, turn) in zip((whole, pair_whole, buf), found):
                 term = turned(src[pl.ds(at + to, 8), :], src[pl.ds(at + (to - 1), 8), :], turn)
                 total = term if total is None else total + term
             out[pl.ds(row * CHUNKS + first, 8), :] = total
 
 
-def last_kernel(mine, down_first, up_first, down, up, out):
-    spans = ((down_first, 0, 2), (up_first, 2, 2), (down, 4, PART - 4), (up, PART, 16 - PART))
+def last_kernel(mine, first, second, rest, out):
     for row in range(ROWS):
         at = (row // 8) * 128 + row % 8
-        for arrived, chunk, count in spans:
+        for arrived, chunk, count in ((first, 0, 4), (second, 4, 4), (rest, 8, 8)):
             value = mine[pl.ds(row * CHUNKS + chunk, count), :] + arrived[pl.ds(row * count, count), :]
             out[pl.ds(at + 8 * chunk, count, stride=8), :] = value * SCALE
 
@@ -297,10 +294,6 @@
     return pltpu.VMEM((sublanes, lane_count), dtype)
 
 
-def ring(steps):
-    return [(i, (i & ~6) | ((((i >> 1) + steps) & 3) << 1)) for i in range(64)]
-
-
 def swap(bit):
     return [(i, i ^ bit) for i in range(64)]
 
@@ -309,7 +302,7 @@
     tiles = x.reshape(8, 8, CHUNKS, LANES).transpose(0, 2, 1, 3).reshape(1024, LANES)
     sem = pltpu.SemaphoreType.DMA
     ints = jnp.int32
-    one_up, one_down = ring(1), ring(-1)
+    by_pair, by_cross = swap(2), swap(6)
     plan, terms_ref = pltpu.VMEM((8, LANES), ints), pltpu.SMEM((8, LANES), ints)
 
     l5, own_tab, codes = call(
@@ -323,51 +316,50 @@
         + [sem((8,))],
     )
     l5_far = lax.ppermute(l5, "freq", swap(1))
-    l6, long_up, long_down, edge = call(
+    l6, pair, cross, edge = call(
         core_main_kernel,
         [(l5, "v"), (l5_far, "v"), (codes, "t"), (own_tab, "v")],
-        [pinned(1024), pinned(8 + ROWS * UP), pinned(8 + ROWS * DOWN), pinned(ROWS * 4)],
+        [pinned(1024), pinned(8 + ROWS * TO_PAIR), pinned(8 + ROWS * TO_CROSS), pinned(ROWS * 4)],
         [pltpu.VMEM((2 * ROWS * PACKED, LANES), F32)],
     )
-    long_up = lax.ppermute(long_up, "freq", one_up)
-    long_down = lax.ppermute(long_down, "freq", one_down)
+    pair = lax.ppermute(pair, "freq", by_pair)
+    cross = lax.ppermute(cross, "freq", by_cross)
     edge = lax.ppermute(edge, "tm", [(i, (i + 1) % 4) for i in range(4)])
 
-    whole, rest_up, rest_down = call(
+    whole, pair_rest, cross_rest = call(
         history_kernel,
         [(l6, "v"), (edge, "v")],
-        [pinned(ROWS * WIDE), pinned(ROWS * REST_UP), pinned(ROWS * REST_DOWN)],
-    )
-    rest_up = lax.ppermute(rest_up, "freq", one_up)
-    rest_down = lax.ppermute(rest_down, "freq", one_down)
-
-    relay_up, relay_down, terms = call(
+        [pinned(ROWS * WIDE), pinned(ROWS * PAIR_REST), pinned(ROWS * CROSS_REST)],
+    )
+    pair_rest = lax.ppermute(pair_rest, "freq", by_pair)
+    cross_rest = lax.ppermute(cross_rest, "freq", by_cross)
+
+    for_pair, for_cross, terms = call(
         relay_kernel,
-        [(long_up, "v"), (long_down, "v")],
-        [pinned(ROWS * (16 - PART) + 8), pinned(ROWS * (PART - 4)), terms_ref],
+        [(pair, "v"), (cross, "v")],
+        [pinned(ROWS * 4 + 8), pinned(ROWS * 8), terms_ref],
         [plan, sem],
     )
-    up = lax.ppermute(relay_up, "freq", one_up)
-    down = lax.ppermute(relay_down, "freq", one_down)
-
-    relay_up, relay_down, tab = call(
+    second = lax.ppermute(for_pair, "freq", by_pair)
+    rest = lax.ppermute(for_cross, "freq", by_cross)
+
+    for_pair, pair_whole = call(
         first_relay_kernel,
-        [(rest_up, "v"), (rest_down, "v"), (long_down, "v"), (terms, "t"), (own_tab, "v")],
-        [pinned(ROWS * 2), pinned(ROWS * 2), pinned(8, LANES, ints)],
+        [(a, "v") for a in (pair, pair_rest, cross, cross_rest)] + [(terms, "t")],
+        [pinned(ROWS * 4), pinned(ROWS * WIDE)],
         [pltpu.VMEM((512, LANES), F32)],
     )
-    up_first = lax.ppermute(relay_up, "freq", one_up)
-    down_first = lax.ppermute(relay_down, "freq", one_down)
+    first = lax.ppermute(for_pair, "freq", by_pair)
 
     (mine,) = call(
         direct_kernel,
-        [(a, "v") for a in (whole, long_up, rest_up, long_down, rest_down, tab, up)],
+        [(a, "v") for a in (whole, pair_whole, cross, cross_rest, own_tab, second)],
         [pinned(ROWS * CHUNKS)],
-        [pltpu.VMEM((ROWS * WIDE, LANES), F32)] * 2 + [plan, terms_ref, sem],
+        [pltpu.VMEM((ROWS * WIDE, LANES), F32), plan, terms_ref, sem],
     )
     (out,) = call(
         last_kernel,
-        [(a, "v") for a in (mine, down_first, up_first, down, up)],
+        [(a, "v") for a in (mine, first, second, rest)],
         [jax.ShapeDtypeStruct((1024, LANES), F32)],
     )
     return out.reshape(8, CHUNKS, 8, LANES).transpose(0, 2, 1, 3).reshape(ROWS, CHUNKS * LANES)

time: 33.6 us -> 31.5 us (0.938)
  starting transfers between devices: 14.4 us -> 10.6 us
  waiting for transfers between devices: 12 us -> 13.9 us
    ppermute x8 -> x7, starting transfers between devices: 12.8 us -> 8.99 us  [the longest x1 2.54 us: on_device(): rest = lax.ppermute(for_cross, 'freq', by_cross)]
    ppermute x8 -> x7, waiting for transfers between devices: 5.21 us -> 7.25 us  [the longest x1 2.82 us: on_device(): cross = lax.ppermute(cross, 'freq', by_cross)]
  transfers between devices with their start and end apart: 10 -> 9, of which waited for: 8 -> 6; matrix products, arithmetic and copies ran while one was open for 0% -> 0% of each run, Pallas kernels for 8% -> 8%
where the time goes in v4:
time: 31.5 us; the launch traced here: 31.4 us
  waiting for transfers between devices  13.9 us (44%)
  starting transfers between devices  10.6 us (34%)
  Pallas kernels  6.82 us (22%)
    pallas_call x7, Pallas kernels, call(): pl.pallas_call(kernel, out_shape=outs, in_specs=[pl.BlockSpec(memory_spac...  6.82 us
    ppermute x1, waiting for transfers between devices, on_device(): edge = lax.ppermute(edge, 'tm', [(i, (i + 1) % 4) for i in range(4)])  4.69 us
    ppermute x1, waiting for transfers between devices, on_device(): cross = lax.ppermute(cross, 'freq', by_cross)  2.82 us
    ppermute x1, starting transfers between devices, on_device(): rest = lax.ppermute(for_cross, 'freq', by_cross)  2.54 us
    ppermute x1, waiting for transfers between devices, on_device(): second = lax.ppermute(for_pair, 'freq', by_pair)  2.3 us
    ppermute x1, starting transfers between devices, on_device(): cross = lax.ppermute(cross, 'freq', by_cross)  2.17 us
    ppermute x1, waiting for transfers between devices, on_device(): l5_far = lax.ppermute(l5, 'freq', swap(1))  1.99 us
    ppermute x1, starting transfers between devices, on_device(): pair = lax.ppermute(pair, 'freq', by_pair)  1.68 us
  transfers between devices with their start and end apart: 9, of which 6 were waited for; matrix products, arithmetic and copies ran while one was open for 0% of the time, Pallas kernels for 8%

profile of v4, /device:TPU:96, one launch (start us, length us, event | category | flops | bytes accessed | tf_op | source)
XLA Modules:
  0.0 31.4 jit_solution(2525467138252337510)
XLA Ops:
  0.0 2.9 %shard_map.46 = (f32[1152,128]{1,0:T(8,128)S(1)}, s32[8,128]{1,0:T(8,128)S(1)}, s32[16,128]{1,0:T(8,128)S(4)}) custom-call(f32[1024,128]{1,0:T(8,128)} %bitcast.10, s32[9,64]{1,0:T(8,128)} %low_h.1, s32[9,64]{1,0:T(8,128)} %high_h.1, s32[9,64]{1,0:T(8,128)} %lag_h.1), custom_call_target="tpu_custom_call" | custom-call | tf_op jit(solution)/shard_map/pallas_call | solution.py:281
  2.9 0.1 collective-permute-start
  3.0 2.0 %collective-permute-done.partner = f32[1152,128]{1,0:T(8,128)S(1)} collective-permute-done((f32[1152,128]{1,0:T(8,128)S(1)}, f32[1152,128]{1,0:T(8,128)S(1)}, u32[]{:S(2)}, u32[]{:S(2)}) %collective-permute-start) | collective-permute-done | bytes 589856 | tf_op jit(solution)/shard_map/ppermute | solution.py:318
  5.0 0.4 %shard_map.47 = (f32[1024,128]{1,0:T(8,128)S(1)}, f32[776,128]{1,0:T(8,128)S(1)}, f32[776,128]{1,0:T(8,128)S(1)}, f32[256,128]{1,0:T(8,128)S(1)}) custom-call(f32[1152,128]{1,0:T(8,128)S(1)} %get-tuple-element.20.own, f32[1152,128]{1,0:T(8,128)S(1)} %collective-permute-done.partner, s32[16,128]{1,0:T(8,128)S(4)} %get-tuple-element.21.codes, ...), custom_call_target="tpu_custom_call" | custom-call | tf_op jit(solution)/shard_map/pallas_call | solution.py:281
  5.4 1.7 %collective-permute-start.2 = (f32[776,128]{1,0:T(8,128)S(1)}, f32[776,128]{1,0:T(8,128)S(1)}, u32[]{:S(2)}, u32[]{:S(2)}) collective-permute-start(f32[776,128]{1,0:T(8,128)S(1)} %get-tuple-element.26), channel_id=1, source_target_pairs={{0,8},{4,12},{8,0},{12,4},{16,24},{20,28},{24,16},{28,20},{32,40},... | collective-permute-start | bytes 1191944 | tf_op jit(solution)/shard_map/ppermute | solution.py:325
  7.0 2.2 %collective-permute-start.4 = (f32[776,128]{1,0:T(8,128)S(1)}, f32[776,128]{1,0:T(8,128)S(1)}, u32[]{:S(2)}, u32[]{:S(2)}) collective-permute-start(f32[776,128]{1,0:T(8,128)S(1)} %get-tuple-element.28), channel_id=1, source_target_pairs={{0,24},{4,28},{8,16},{12,20},{16,8},{20,12},{24,0},{28,4},{32,56},... | collective-permute-start | bytes 1191944 | tf_op jit(solution)/shard_map/ppermute | solution.py:326
  9.2 1.5 %collective-permute-start.1 = (f32[256,128]{1,0:T(8,128)S(1)}, f32[256,128]{1,0:T(8,128)S(1)}, u32[]{:S(2)}, u32[]{:S(2)}) collective-permute-start(f32[256,128]{1,0:T(8,128)S(1)} %get-tuple-element.24), channel_id=1, source_target_pairs={{0,1},{1,2},{2,3},{3,0},{4,5},{5,6},{6,7},{7,4},{8,9},{9,10},{10,1... | collective-permute-start | bytes 393224 | tf_op jit(solution)/shard_map/ppermute | solution.py:327
  10.7 4.7 %collective-permute-done.1.edge = f32[256,128]{1,0:T(8,128)S(1)} collective-permute-done((f32[256,128]{1,0:T(8,128)S(1)}, f32[256,128]{1,0:T(8,128)S(1)}, u32[]{:S(2)}, u32[]{:S(2)}) %collective-permute-start.1) | collective-permute-done | bytes 131104 | tf_op jit(solution)/shard_map/ppermute | solution.py:327
  15.4 0.2 shard_map.48
  15.6 0.8 %collective-permute-start.3 = (f32[448,128]{1,0:T(8,128)S(1)}, f32[448,128]{1,0:T(8,128)S(1)}, u32[]{:S(2)}, u32[]{:S(2)}) collective-permute-start(f32[448,128]{1,0:T(8,128)S(1)} %get-tuple-element.27), channel_id=1, source_target_pairs={{0,8},{4,12},{8,0},{12,4},{16,24},{20,28},{24,16},{28,20},{32,40},... | collective-permute-start | bytes 688136 | tf_op jit(solution)/shard_map/ppermute | solution.py:334
  16.4 0.9 %collective-permute-start.5 = (f32[448,128]{1,0:T(8,128)S(1)}, f32[448,128]{1,0:T(8,128)S(1)}, u32[]{:S(2)}, u32[]{:S(2)}) collective-permute-start(f32[448,128]{1,0:T(8,128)S(1)} %get-tuple-element.29), channel_id=1, source_target_pairs={{0,24},{4,28},{8,16},{12,20},{16,8},{20,12},{24,0},{28,4},{32,56},... | collective-permute-start | bytes 688136 | tf_op jit(solution)/shard_map/ppermute | solution.py:335
  17.2 0.0 collective-permute-done.2.pair
  17.2 2.8 %collective-permute-done.4.cross = f32[776,128]{1,0:T(8,128)S(1)} collective-permute-done((f32[776,128]{1,0:T(8,128)S(1)}, f32[776,128]{1,0:T(8,128)S(1)}, u32[]{:S(2)}, u32[]{:S(2)}) %collective-permute-start.4) | collective-permute-done | bytes 397344 | tf_op jit(solution)/shard_map/ppermute | solution.py:326
  20.1 1.0 %shard_map.49 = (f32[264,128]{1,0:T(8,128)S(1)}, f32[512,128]{1,0:T(8,128)S(1)}, s32[8,128]{1,0:T(8,128)S(4)}) custom-call(f32[776,128]{1,0:T(8,128)S(1)} %collective-permute-done.2.pair, f32[776,128]{1,0:T(8,128)S(1)} %collective-permute-done.4.cross), custom_call_target="tpu_custom_call" | custom-call | tf_op jit(solution)/shard_map/pallas_call | solution.py:281
  21.1 2.5 %collective-permute-start.8 = (f32[512,128]{1,0:T(8,128)S(1)}, f32[512,128]{1,0:T(8,128)S(1)}, u32[]{:S(2)}, u32[]{:S(2)}) collective-permute-start(f32[512,128]{1,0:T(8,128)S(1)} %get-tuple-element.34), channel_id=1, source_target_pairs={{0,24},{4,28},{8,16},{12,20},{16,8},{20,12},{24,0},{28,4},{32,56},... | collective-permute-start | bytes 786440 | tf_op jit(solution)/shard_map/ppermute | solution.py:344
  23.6 0.0 collective-permute-start.6
  23.6 0.0 collective-permute-done.3.pair_rest
  23.6 1.5 %collective-permute-done.5.cross_rest = f32[448,128]{1,0:T(8,128)S(1)} collective-permute-done((f32[448,128]{1,0:T(8,128)S(1)}, f32[448,128]{1,0:T(8,128)S(1)}, u32[]{:S(2)}, u32[]{:S(2)}) %collective-permute-start.5) | collective-permute-done | bytes 229408 | tf_op jit(solution)/shard_map/ppermute | solution.py:335
  25.1 0.2 shard_map.50
  25.3 0.9 %collective-permute-start.7 = (f32[256,128]{1,0:T(8,128)S(1)}, f32[256,128]{1,0:T(8,128)S(1)}, u32[]{:S(2)}, u32[]{:S(2)}) collective-permute-start(f32[256,128]{1,0:T(8,128)S(1)} %get-tuple-element.33), channel_id=1, source_target_pairs={{0,8},{4,12},{8,0},{12,4},{16,24},{20,28},{24,16},{28,20},{32,40},... | collective-permute-start | bytes 393224 | tf_op jit(solution)/shard_map/ppermute | solution.py:352
  26.3 2.3 %collective-permute-done.6.relay.second = f32[264,128]{1,0:T(8,128)S(1)} collective-permute-done((f32[264,128]{1,0:T(8,128)S(1)}, f32[264,128]{1,0:T(8,128)S(1)}, u32[]{:S(2)}, u32[]{:S(2)}) %collective-permute-start.6) | collective-permute-done | bytes 135200 | tf_op jit(solution)/shard_map/ppermute | solution.py:343
  28.6 1.2 %shard_map.51.mine = f32[1024,128]{1,0:T(8,128)S(1)} custom-call(f32[1280,128]{1,0:T(8,128)S(1)} %get-tuple-element.25.whole, f32[1280,128]{1,0:T(8,128)S(1)} %get-tuple-element.31.pair_whole, f32[776,128]{1,0:T(8,128)S(1)} %collective-permute-done.4.cross, f32[448,128]{1,0:T(8,128)S(1)} %collective-permute-done.5.cross_rest, ...), custom_call_target="tpu_custom_call" | custom-call | tf_op jit(solution)/shard_map/pallas_call | solution.py:281
  29.8 0.6 %collective-permute-done.7.first = f32[256,128]{1,0:T(8,128)S(1)} collective-permute-done((f32[256,128]{1,0:T(8,128)S(1)}, f32[256,128]{1,0:T(8,128)S(1)}, u32[]{:S(2)}, u32[]{:S(2)}) %collective-permute-start.7) | collective-permute-done | bytes 131104 | tf_op jit(solution)/shard_map/ppermute | solution.py:352
  30.4 0.0 collective-permute-done.8.rest
  30.4 1.0 %shard_map.52 = f32[1024,128]{1,0:T(8,128)} custom-call(f32[1024,128]{1,0:T(8,128)S(1)} %shard_map.51.mine, f32[256,128]{1,0:T(8,128)S(1)} %collective-permute-done.7.first, f32[264,128]{1,0:T(8,128)S(1)} %collective-permute-done.6.relay.second, f32[512,128]{1,0:T(8,128)S(1)} %collective-permute-done.8.rest), custom_call_target="tpu_custom_call" | custom-call | tf_op jit(solution)/shard_map/pallas_call | solution.py:281
Async XLA Ops:
  2.9 2.1 %collective-permute-start = (f32[1152,128]{1,0:T(8,128)S(1)}, f32[1152,128]{1,0:T(8,128)S(1)}, u32[]{:S(2)}, u32[]{:S(2)}) collective-permute-start(f32[1152,128]{1,0:T(8,128)S(1)} %get-tuple-element.20.own), channel_id=1, source_target_pairs={{0,4},{4,0},{8,12},{12,8},{16,20},{20,16},{24,28},{28,24},{32,36},... | collective-permute-start | bytes 1769480 | tf_op jit(solution)/shard_map/ppermute | solution.py:318
  5.4 11.9 %collective-permute-start.2 = (f32[776,128]{1,0:T(8,128)S(1)}, f32[776,128]{1,0:T(8,128)S(1)}, u32[]{:S(2)}, u32[]{:S(2)}) collective-permute-start(f32[776,128]{1,0:T(8,128)S(1)} %get-tuple-element.26), channel_id=1, source_target_pairs={{0,8},{4,12},{8,0},{12,4},{16,24},{20,28},{24,16},{28,20},{32,40},... | collective-permute-start | bytes 1191944 | tf_op jit(solution)/shard_map/ppermute | solution.py:325
  7.0 13.0 %collective-permute-start.4 = (f32[776,128]{1,0:T(8,128)S(1)}, f32[776,128]{1,0:T(8,128)S(1)}, u32[]{:S(2)}, u32[]{:S(2)}) collective-permute-start(f32[776,128]{1,0:T(8,128)S(1)} %get-tuple-element.28), channel_id=1, source_target_pairs={{0,24},{4,28},{8,16},{12,20},{16,8},{20,12},{24,0},{28,4},{32,56},... | collective-permute-start | bytes 1191944 | tf_op jit(solution)/shard_map/ppermute | solution.py:326
  9.2 6.2 %collective-permute-start.1 = (f32[256,128]{1,0:T(8,128)S(1)}, f32[256,128]{1,0:T(8,128)S(1)}, u32[]{:S(2)}, u32[]{:S(2)}) collective-permute-start(f32[256,128]{1,0:T(8,128)S(1)} %get-tuple-element.24), channel_id=1, source_target_pairs={{0,1},{1,2},{2,3},{3,0},{4,5},{5,6},{6,7},{7,4},{8,9},{9,10},{10,1... | collective-permute-start | bytes 393224 | tf_op jit(solution)/shard_map/ppermute | solution.py:327
  15.6 8.0 %collective-permute-start.3 = (f32[448,128]{1,0:T(8,128)S(1)}, f32[448,128]{1,0:T(8,128)S(1)}, u32[]{:S(2)}, u32[]{:S(2)}) collective-permute-start(f32[448,128]{1,0:T(8,128)S(1)} %get-tuple-element.27), channel_id=1, source_target_pairs={{0,8},{4,12},{8,0},{12,4},{16,24},{20,28},{24,16},{28,20},{32,40},... | collective-permute-start | bytes 688136 | tf_op jit(solution)/shard_map/ppermute | solution.py:334
  16.4 8.8 %collective-permute-start.5 = (f32[448,128]{1,0:T(8,128)S(1)}, f32[448,128]{1,0:T(8,128)S(1)}, u32[]{:S(2)}, u32[]{:S(2)}) collective-permute-start(f32[448,128]{1,0:T(8,128)S(1)} %get-tuple-element.29), channel_id=1, source_target_pairs={{0,24},{4,28},{8,16},{12,20},{16,8},{20,12},{24,0},{28,4},{32,56},... | collective-permute-start | bytes 688136 | tf_op jit(solution)/shard_map/ppermute | solution.py:335
  21.1 9.4 %collective-permute-start.8 = (f32[512,128]{1,0:T(8,128)S(1)}, f32[512,128]{1,0:T(8,128)S(1)}, u32[]{:S(2)}, u32[]{:S(2)}) collective-permute-start(f32[512,128]{1,0:T(8,128)S(1)} %get-tuple-element.34), channel_id=1, source_target_pairs={{0,24},{4,28},{8,16},{12,20},{16,8},{20,12},{24,0},{28,4},{32,56},... | collective-permute-start | bytes 786440 | tf_op jit(solution)/shard_map/ppermute | solution.py:344
  23.6 5.0 %collective-permute-start.6 = (f32[264,128]{1,0:T(8,128)S(1)}, f32[264,128]{1,0:T(8,128)S(1)}, u32[]{:S(2)}, u32[]{:S(2)}) collective-permute-start(f32[264,128]{1,0:T(8,128)S(1)} %get-tuple-element.32), channel_id=1, source_target_pairs={{0,8},{4,12},{8,0},{12,4},{16,24},{20,28},{24,16},{28,20},{32,40},... | collective-permute-start | bytes 405512 | tf_op jit(solution)/shard_map/ppermute | solution.py:343
  25.3 5.1 %collective-permute-start.7 = (f32[256,128]{1,0:T(8,128)S(1)}, f32[256,128]{1,0:T(8,128)S(1)}, u32[]{:S(2)}, u32[]{:S(2)}) collective-permute-start(f32[256,128]{1,0:T(8,128)S(1)} %get-tuple-element.33), channel_id=1, source_target_pairs={{0,8},{4,12},{8,0},{12,4},{16,24},{20,28},{24,16},{28,20},{32,40},... | collective-permute-start | bytes 393224 | tf_op jit(solution)/shard_map/ppermute | solution.py:352

commit v5 on v4

--- a/solution.py
+++ b/solution.py
@@ -18,6 +18,7 @@
 WIDE = 20
 TO_PAIR, TO_CROSS = 12, 12
 PAIR_REST, CROSS_REST = 19 - TO_PAIR, 19 - TO_CROSS
+PART = 10
 SCALE = 1.0 / math.sqrt(2.0**LEVELS)
 F32 = jnp.float32
 
@@ -213,29 +214,22 @@
     plan[2:3, :] = term_codes(cross_tab, pair_tab, 1 - odd, 1 - upper, 8)
     copy = pltpu.make_async_copy(plan, terms, sem)
     copy.start()
-    for_pair[ROWS * 4 :, :] = cross[0:8, :]
+    for_pair[ROWS * (PART - 4) :, :] = cross[0:8, :]
     copy.wait()
-    shares(cross, 8 + 3, terms, 0, 4, into(for_pair))
-    shares(pair, 8 + TO_PAIR - 8, terms, 1, 8, into(for_cross))
-
-
-def first_relay_kernel(pair, pair_rest, cross, cross_rest, terms, for_pair, pair_whole, buf):
+    shares(cross, 8 + 3, terms, 0, PART - 4, into(for_pair))
+    shares(pair, 8 + TO_PAIR - 16 + PART, terms, 1, 16 - PART, into(for_cross))
+
+
+def first_relay_kernel(cross, cross_rest, terms, _, for_pair, buf):
     for row in range(ROWS):
         buf[pl.ds(row * 8 + 1, 4), :] = cross_rest[pl.ds(row * CROSS_REST, 4), :]
         buf[pl.ds(row * 8 + 5, 3), :] = cross[pl.ds(8 + row * TO_CROSS, 3), :]
     shares(buf, 4, terms, 2, 4, into(for_pair))
-    for row in range(ROWS):
-        to = row * WIDE
-        pair_whole[pl.ds(to, 1), :] = jnp.zeros((1, LANES), F32)
-        pair_whole[pl.ds(to + 1, PAIR_REST), :] = pair_rest[pl.ds(row * PAIR_REST, PAIR_REST), :]
-        pair_whole[pl.ds(to + 1 + PAIR_REST, TO_PAIR), :] = pair[
-            pl.ds(8 + row * TO_PAIR, TO_PAIR), :
-        ]
-
-
-def direct_kernel(whole, pair_whole, cross, cross_rest, tab, relay, out, buf, plan, terms, sem):
+
+
+def direct_kernel(whole, pair, pair_rest, cross, cross_rest, tab, relay, out, pair_buf, buf, plan, terms, sem):
     _, odd, upper = place()
-    own, other = tab[...], relay[ROWS * 4 :, :].astype(jnp.int32)
+    own, other = tab[...], relay[ROWS * (PART - 4) :, :].astype(jnp.int32)
     plan[...] = jnp.zeros_like(plan)
     plan[0:1, :] = term_codes(own, own, odd, upper, WIDE)
     plan[1:2, :] = term_codes(own, own, 1 - odd, upper, WIDE)
@@ -244,6 +238,10 @@
     copy.start()
     for row in range(ROWS):
         to, rest = row * WIDE, row * CROSS_REST
+        pair_buf[pl.ds(to + 1, PAIR_REST), :] = pair_rest[pl.ds(row * PAIR_REST, PAIR_REST), :]
+        pair_buf[pl.ds(to + 1 + PAIR_REST, TO_PAIR), :] = pair[
+            pl.ds(8 + row * TO_PAIR, TO_PAIR), :
+        ]
         buf[pl.ds(to + 1, 4), :] = cross_rest[pl.ds(rest, 4), :]
         buf[pl.ds(to + 5, TO_CROSS), :] = cross[pl.ds(8 + row * TO_CROSS, TO_CROSS), :]
         buf[pl.ds(to + 5 + TO_CROSS, CROSS_REST - 4), :] = cross_rest[
@@ -258,18 +256,29 @@
         for first in (0, 8):
             to = 4 + first
             total = None
-            for src, (at, turn) in zip((whole, pair_whole, buf), found):
+            for src, (at, turn) in zip((whole, pair_buf, buf), found):
                 term = turned(src[pl.ds(at + to, 8), :], src[pl.ds(at + (to - 1), 8), :], turn)
                 total = term if total is None else total + term
             out[pl.ds(row * CHUNKS + first, 8), :] = total
 
 
-def last_kernel(mine, first, second, rest, out):
-    for row in range(ROWS):
-        at = (row // 8) * 128 + row % 8
-        for arrived, chunk, count in ((first, 0, 4), (second, 4, 4), (rest, 8, 8)):
-            value = mine[pl.ds(row * CHUNKS + chunk, count), :] + arrived[pl.ds(row * count, count), :]
-            out[pl.ds(at + 8 * chunk, count, stride=8), :] = value * SCALE
+def last_kernel(mine, first, second, rest, out, buf, sems):
+    copies = []
+    for part in range(4):
+        for row in range(part * 16, part * 16 + 16):
+            at = (row // 8) * 128 + row % 8
+            spans = (first, 0, 4), (second, 4, PART - 4), (rest, PART, 16 - PART)
+            for arrived, chunk, count in spans:
+                value = (
+                    mine[pl.ds(row * CHUNKS + chunk, count), :]
+                    + arrived[pl.ds(row * count, count), :]
+                )
+                buf[pl.ds(at + 8 * chunk, count, stride=8), :] = value * SCALE
+        here = pl.ds(part * 256, 256)
+        copies.append(pltpu.make_async_copy(buf.at[here], out.at[here], sems.at[part]))
+        copies[-1].start()
+    for copy in copies:
+        copy.wait()
 
 
 def call(kernel, ins, outs, scratch=()):
@@ -282,9 +291,7 @@
         kernel,
         out_shape=outs,
         in_specs=[pl.BlockSpec(memory_space=kinds[where]) for _, where in ins],
-        out_specs=[
-            pl.BlockSpec(memory_space=pltpu.SMEM if "smem" in str(o).lower() else pltpu.VMEM) for o in outs
-        ],
+        out_specs=[pl.BlockSpec(memory_space=getattr(o, "memory_space", pltpu.VMEM)) for o in outs],
         scratch_shapes=list(scratch),
         compiler_params=pltpu.CompilerParams(vmem_limit_bytes=16 * 2**20),
     )(*values)
@@ -322,8 +329,8 @@
         [pinned(1024), pinned(8 + ROWS * TO_PAIR), pinned(8 + ROWS * TO_CROSS), pinned(ROWS * 4)],
         [pltpu.VMEM((2 * ROWS * PACKED, LANES), F32)],
     )
+    cross = lax.ppermute(cross, "freq", by_cross)
     pair = lax.ppermute(pair, "freq", by_pair)
-    cross = lax.ppermute(cross, "freq", by_cross)
     edge = lax.ppermute(edge, "tm", [(i, (i + 1) % 4) for i in range(4)])
 
     whole, pair_rest, cross_rest = call(
@@ -331,36 +338,37 @@
         [(l6, "v"), (edge, "v")],
         [pinned(ROWS * WIDE), pinned(ROWS * PAIR_REST), pinned(ROWS * CROSS_REST)],
     )
+    cross_rest = lax.ppermute(cross_rest, "freq", by_cross)
     pair_rest = lax.ppermute(pair_rest, "freq", by_pair)
-    cross_rest = lax.ppermute(cross_rest, "freq", by_cross)
 
     for_pair, for_cross, terms = call(
         relay_kernel,
         [(pair, "v"), (cross, "v")],
-        [pinned(ROWS * 4 + 8), pinned(ROWS * 8), terms_ref],
+        [pinned(ROWS * (PART - 4) + 8), pinned(ROWS * (16 - PART)), terms_ref],
         [plan, sem],
     )
     second = lax.ppermute(for_pair, "freq", by_pair)
     rest = lax.ppermute(for_cross, "freq", by_cross)
 
-    for_pair, pair_whole = call(
+    (for_pair,) = call(
         first_relay_kernel,
-        [(a, "v") for a in (pair, pair_rest, cross, cross_rest)] + [(terms, "t")],
-        [pinned(ROWS * 4), pinned(ROWS * WIDE)],
+        [(cross, "v"), (cross_rest, "v"), (terms, "t"), (pair_rest, "v")],
+        [pinned(ROWS * 4)],
         [pltpu.VMEM((512, LANES), F32)],
     )
     first = lax.ppermute(for_pair, "freq", by_pair)
 
     (mine,) = call(
         direct_kernel,
-        [(a, "v") for a in (whole, pair_whole, cross, cross_rest, own_tab, second)],
+        [(a, "v") for a in (whole, pair, pair_rest, cross, cross_rest, own_tab, second)],
         [pinned(ROWS * CHUNKS)],
-        [pltpu.VMEM((ROWS * WIDE, LANES), F32), plan, terms_ref, sem],
+        [pltpu.VMEM((ROWS * WIDE, LANES), F32)] * 2 + [plan, terms_ref, sem],
     )
     (out,) = call(
         last_kernel,
         [(a, "v") for a in (mine, first, second, rest)],
-        [jax.ShapeDtypeStruct((1024, LANES), F32)],
+        [pltpu.HBM((1024, LANES), F32)],
+        [pltpu.VMEM((1024, LANES), F32), sem((4,))],
     )
     return out.reshape(8, CHUNKS, 8, LANES).transpose(0, 2, 1, 3).reshape(ROWS, CHUNKS * LANES)
 

time: 31.5 us -> 31.3 us (level)
  starting transfers between devices: 10.6 us -> 9.84 us
  waiting for transfers between devices: 13.9 us -> 14.5 us
    ppermute x1, starting transfers between devices: 0.95 us -> 0.11 us  [on_device(): first = lax.ppermute(for_pair, 'freq', by_pair)]
    ppermute x1, waiting for transfers between devices: 2.3 us -> 2.92 us  [on_device(): second = lax.ppermute(for_pair, 'freq', by_pair)]
where the time goes in v5:
time: 31.3 us; the launch traced here: 31.2 us
  waiting for transfers between devices  14.5 us (46%)
  starting transfers between devices  9.84 us (31%)
  Pallas kernels  6.79 us (22%)
    pallas_call x7, Pallas kernels, call(): pl.pallas_call(kernel, out_shape=outs, in_specs=[pl.BlockSpec(memory_spac...  6.79 us
    ppermute x1, waiting for transfers between devices, on_device(): edge = lax.ppermute(edge, 'tm', [(i, (i + 1) % 4) for i in range(4)])  4.69 us
    ppermute x1, waiting for transfers between devices, on_device(): second = lax.ppermute(for_pair, 'freq', by_pair)  2.92 us
    ppermute x1, waiting for transfers between devices, on_device(): cross = lax.ppermute(cross, 'freq', by_cross)  2.81 us
    ppermute x1, starting transfers between devices, on_device(): rest = lax.ppermute(for_cross, 'freq', by_cross)  2.55 us
    ppermute x1, starting transfers between devices, on_device(): cross = lax.ppermute(cross, 'freq', by_cross)  2.18 us
    ppermute x1, waiting for transfers between devices, on_device(): l5_far = lax.ppermute(l5, 'freq', swap(1))  1.99 us
    ppermute x1, starting transfers between devices, on_device(): pair = lax.ppermute(pair, 'freq', by_pair)  1.67 us
  transfers between devices with their start and end apart: 9, of which 6 were waited for; matrix products, arithmetic and copies ran while one was open for 0% of the time, Pallas kernels for 8%

profile of v5, /device:TPU:96, one launch (start us, length us, event | category | flops | bytes accessed | tf_op | source)
XLA Modules:
  0.0 31.2 jit_solution(17536651382516286332)
XLA Ops:
  0.0 2.9 %shard_map.46 = (f32[1152,128]{1,0:T(8,128)S(1)}, s32[8,128]{1,0:T(8,128)S(1)}, s32[16,128]{1,0:T(8,128)S(4)}) custom-call(f32[1024,128]{1,0:T(8,128)} %bitcast.10, s32[9,64]{1,0:T(8,128)} %low_h.1, s32[9,64]{1,0:T(8,128)} %high_h.1, s32[9,64]{1,0:T(8,128)} %lag_h.1), custom_call_target="tpu_custom_call" | custom-call | tf_op jit(solution)/shard_map/pallas_call | solution.py:290
  2.9 0.1 collective-permute-start
  3.0 2.0 %collective-permute-done.partner = f32[1152,128]{1,0:T(8,128)S(1)} collective-permute-done((f32[1152,128]{1,0:T(8,128)S(1)}, f32[1152,128]{1,0:T(8,128)S(1)}, u32[]{:S(2)}, u32[]{:S(2)}) %collective-permute-start) | collective-permute-done | bytes 589856 | tf_op jit(solution)/shard_map/ppermute | solution.py:325
  5.0 0.4 %shard_map.47 = (f32[1024,128]{1,0:T(8,128)S(1)}, f32[776,128]{1,0:T(8,128)S(1)}, f32[776,128]{1,0:T(8,128)S(1)}, f32[256,128]{1,0:T(8,128)S(1)}) custom-call(f32[1152,128]{1,0:T(8,128)S(1)} %get-tuple-element.18.own, f32[1152,128]{1,0:T(8,128)S(1)} %collective-permute-done.partner, s32[16,128]{1,0:T(8,128)S(4)} %get-tuple-element.19.codes, ...), custom_call_target="tpu_custom_call" | custom-call | tf_op jit(solution)/shard_map/pallas_call | solution.py:290
  5.4 1.7 %collective-permute-start.2 = (f32[776,128]{1,0:T(8,128)S(1)}, f32[776,128]{1,0:T(8,128)S(1)}, u32[]{:S(2)}, u32[]{:S(2)}) collective-permute-start(f32[776,128]{1,0:T(8,128)S(1)} %get-tuple-element.24), channel_id=1, source_target_pairs={{0,8},{4,12},{8,0},{12,4},{16,24},{20,28},{24,16},{28,20},{32,40},... | collective-permute-start | bytes 1191944 | tf_op jit(solution)/shard_map/ppermute | solution.py:333
  7.0 2.2 %collective-permute-start.4 = (f32[776,128]{1,0:T(8,128)S(1)}, f32[776,128]{1,0:T(8,128)S(1)}, u32[]{:S(2)}, u32[]{:S(2)}) collective-permute-start(f32[776,128]{1,0:T(8,128)S(1)} %get-tuple-element.26), channel_id=1, source_target_pairs={{0,24},{4,28},{8,16},{12,20},{16,8},{20,12},{24,0},{28,4},{32,56},... | collective-permute-start | bytes 1191944 | tf_op jit(solution)/shard_map/ppermute | solution.py:332
  9.2 1.5 %collective-permute-start.1 = (f32[256,128]{1,0:T(8,128)S(1)}, f32[256,128]{1,0:T(8,128)S(1)}, u32[]{:S(2)}, u32[]{:S(2)}) collective-permute-start(f32[256,128]{1,0:T(8,128)S(1)} %get-tuple-element.22), channel_id=1, source_target_pairs={{0,1},{1,2},{2,3},{3,0},{4,5},{5,6},{6,7},{7,4},{8,9},{9,10},{10,1... | collective-permute-start | bytes 393224 | tf_op jit(solution)/shard_map/ppermute | solution.py:334
  10.7 4.7 %collective-permute-done.1.edge = f32[256,128]{1,0:T(8,128)S(1)} collective-permute-done((f32[256,128]{1,0:T(8,128)S(1)}, f32[256,128]{1,0:T(8,128)S(1)}, u32[]{:S(2)}, u32[]{:S(2)}) %collective-permute-start.1) | collective-permute-done | bytes 131104 | tf_op jit(solution)/shard_map/ppermute | solution.py:334
  15.4 0.2 shard_map.48
  15.6 0.8 %collective-permute-start.3 = (f32[448,128]{1,0:T(8,128)S(1)}, f32[448,128]{1,0:T(8,128)S(1)}, u32[]{:S(2)}, u32[]{:S(2)}) collective-permute-start(f32[448,128]{1,0:T(8,128)S(1)} %get-tuple-element.25), channel_id=1, source_target_pairs={{0,8},{4,12},{8,0},{12,4},{16,24},{20,28},{24,16},{28,20},{32,40},... | collective-permute-start | bytes 688136 | tf_op jit(solution)/shard_map/ppermute | solution.py:342
  16.4 0.9 %collective-permute-start.5 = (f32[448,128]{1,0:T(8,128)S(1)}, f32[448,128]{1,0:T(8,128)S(1)}, u32[]{:S(2)}, u32[]{:S(2)}) collective-permute-start(f32[448,128]{1,0:T(8,128)S(1)} %get-tuple-element.27), channel_id=1, source_target_pairs={{0,24},{4,28},{8,16},{12,20},{16,8},{20,12},{24,0},{28,4},{32,56},... | collective-permute-start | bytes 688136 | tf_op jit(solution)/shard_map/ppermute | solution.py:341
  17.2 0.0 collective-permute-done.2.pair
  17.2 2.8 %collective-permute-done.4.cross = f32[776,128]{1,0:T(8,128)S(1)} collective-permute-done((f32[776,128]{1,0:T(8,128)S(1)}, f32[776,128]{1,0:T(8,128)S(1)}, u32[]{:S(2)}, u32[]{:S(2)}) %collective-permute-start.4) | collective-permute-done | bytes 397344 | tf_op jit(solution)/shard_map/ppermute | solution.py:332
  20.0 1.0 %shard_map.49 = (f32[392,128]{1,0:T(8,128)S(1)}, f32[384,128]{1,0:T(8,128)S(1)}, s32[8,128]{1,0:T(8,128)S(4)}) custom-call(f32[776,128]{1,0:T(8,128)S(1)} %collective-permute-done.2.pair, f32[776,128]{1,0:T(8,128)S(1)} %collective-permute-done.4.cross), custom_call_target="tpu_custom_call" | custom-call | tf_op jit(solution)/shard_map/pallas_call | solution.py:290
  21.0 0.1 collective-permute-start.6
  21.1 2.6 %collective-permute-start.8 = (f32[384,128]{1,0:T(8,128)S(1)}, f32[384,128]{1,0:T(8,128)S(1)}, u32[]{:S(2)}, u32[]{:S(2)}) collective-permute-start(f32[384,128]{1,0:T(8,128)S(1)} %get-tuple-element.30), channel_id=1, source_target_pairs={{0,24},{4,28},{8,16},{12,20},{16,8},{20,12},{24,0},{28,4},{32,56},... | collective-permute-start | bytes 589832 | tf_op jit(solution)/shard_map/ppermute | solution.py:351
  23.7 0.0 collective-permute-done.3.pair_rest._
  23.7 1.3 %collective-permute-done.5.cross_rest = f32[448,128]{1,0:T(8,128)S(1)} collective-permute-done((f32[448,128]{1,0:T(8,128)S(1)}, f32[448,128]{1,0:T(8,128)S(1)}, u32[]{:S(2)}, u32[]{:S(2)}) %collective-permute-start.5) | collective-permute-done | bytes 229408 | tf_op jit(solution)/shard_map/ppermute | solution.py:341
  25.0 0.2 shard_map.51
  25.2 0.1 collective-permute-start.7
  25.3 2.9 %collective-permute-done.6.relay.second = f32[392,128]{1,0:T(8,128)S(1)} collective-permute-done((f32[392,128]{1,0:T(8,128)S(1)}, f32[392,128]{1,0:T(8,128)S(1)}, u32[]{:S(2)}, u32[]{:S(2)}) %collective-permute-start.6) | collective-permute-done | bytes 200736 | tf_op jit(solution)/shard_map/ppermute | solution.py:350
  28.2 1.2 %shard_map.50.mine = f32[1024,128]{1,0:T(8,128)S(1)} custom-call(f32[1280,128]{1,0:T(8,128)S(1)} %get-tuple-element.23.whole, f32[776,128]{1,0:T(8,128)S(1)} %collective-permute-done.2.pair, f32[448,128]{1,0:T(8,128)S(1)} %collective-permute-done.3.pair_rest._, f32[776,128]{1,0:T(8,128)S(1)} %collective-permute-done.4.cross, ...), custom_call_target="tpu_custom_call" | custom-call | tf_op jit(solution)/shard_map/pallas_call | solution.py:290
  29.5 0.8 %collective-permute-done.7.first = f32[256,128]{1,0:T(8,128)S(1)} collective-permute-done((f32[256,128]{1,0:T(8,128)S(1)}, f32[256,128]{1,0:T(8,128)S(1)}, u32[]{:S(2)}, u32[]{:S(2)}) %collective-permute-start.7) | collective-permute-done | bytes 131104 | tf_op jit(solution)/shard_map/ppermute | solution.py:359
  30.3 0.0 collective-permute-done.8.rest
  30.3 0.9 %shard_map.52 = f32[1024,128]{1,0:T(8,128)} custom-call(f32[1024,128]{1,0:T(8,128)S(1)} %shard_map.50.mine, f32[256,128]{1,0:T(8,128)S(1)} %collective-permute-done.7.first, f32[392,128]{1,0:T(8,128)S(1)} %collective-permute-done.6.relay.second, f32[384,128]{1,0:T(8,128)S(1)} %collective-permute-done.8.rest), custom_call_target="tpu_custom_call" | custom-call | tf_op jit(solution)/shard_map/pallas_call | solution.py:290
Async XLA Ops:
  2.9 2.1 %collective-permute-start = (f32[1152,128]{1,0:T(8,128)S(1)}, f32[1152,128]{1,0:T(8,128)S(1)}, u32[]{:S(2)}, u32[]{:S(2)}) collective-permute-start(f32[1152,128]{1,0:T(8,128)S(1)} %get-tuple-element.18.own), channel_id=1, source_target_pairs={{0,4},{4,0},{8,12},{12,8},{16,20},{20,16},{24,28},{28,24},{32,36},... | collective-permute-start | bytes 1769480 | tf_op jit(solution)/shard_map/ppermute | solution.py:325
  5.4 11.9 %collective-permute-start.2 = (f32[776,128]{1,0:T(8,128)S(1)}, f32[776,128]{1,0:T(8,128)S(1)}, u32[]{:S(2)}, u32[]{:S(2)}) collective-permute-start(f32[776,128]{1,0:T(8,128)S(1)} %get-tuple-element.24), channel_id=1, source_target_pairs={{0,8},{4,12},{8,0},{12,4},{16,24},{20,28},{24,16},{28,20},{32,40},... | collective-permute-start | bytes 1191944 | tf_op jit(solution)/shard_map/ppermute | solution.py:333
  7.0 13.0 %collective-permute-start.4 = (f32[776,128]{1,0:T(8,128)S(1)}, f32[776,128]{1,0:T(8,128)S(1)}, u32[]{:S(2)}, u32[]{:S(2)}) collective-permute-start(f32[776,128]{1,0:T(8,128)S(1)} %get-tuple-element.26), channel_id=1, source_target_pairs={{0,24},{4,28},{8,16},{12,20},{16,8},{20,12},{24,0},{28,4},{32,56},... | collective-permute-start | bytes 1191944 | tf_op jit(solution)/shard_map/ppermute | solution.py:332
  9.2 6.2 %collective-permute-start.1 = (f32[256,128]{1,0:T(8,128)S(1)}, f32[256,128]{1,0:T(8,128)S(1)}, u32[]{:S(2)}, u32[]{:S(2)}) collective-permute-start(f32[256,128]{1,0:T(8,128)S(1)} %get-tuple-element.22), channel_id=1, source_target_pairs={{0,1},{1,2},{2,3},{3,0},{4,5},{5,6},{6,7},{7,4},{8,9},{9,10},{10,1... | collective-permute-start | bytes 393224 | tf_op jit(solution)/shard_map/ppermute | solution.py:334
  15.6 8.1 %collective-permute-start.3 = (f32[448,128]{1,0:T(8,128)S(1)}, f32[448,128]{1,0:T(8,128)S(1)}, u32[]{:S(2)}, u32[]{:S(2)}) collective-permute-start(f32[448,128]{1,0:T(8,128)S(1)} %get-tuple-element.25), channel_id=1, source_target_pairs={{0,8},{4,12},{8,0},{12,4},{16,24},{20,28},{24,16},{28,20},{32,40},... | collective-permute-start | bytes 688136 | tf_op jit(solution)/shard_map/ppermute | solution.py:342
  16.4 8.6 %collective-permute-start.5 = (f32[448,128]{1,0:T(8,128)S(1)}, f32[448,128]{1,0:T(8,128)S(1)}, u32[]{:S(2)}, u32[]{:S(2)}) collective-permute-start(f32[448,128]{1,0:T(8,128)S(1)} %get-tuple-element.27), channel_id=1, source_target_pairs={{0,24},{4,28},{8,16},{12,20},{16,8},{20,12},{24,0},{28,4},{32,56},... | collective-permute-start | bytes 688136 | tf_op jit(solution)/shard_map/ppermute | solution.py:341
  21.0 7.2 %collective-permute-start.6 = (f32[392,128]{1,0:T(8,128)S(1)}, f32[392,128]{1,0:T(8,128)S(1)}, u32[]{:S(2)}, u32[]{:S(2)}) collective-permute-start(f32[392,128]{1,0:T(8,128)S(1)} %get-tuple-element.28), channel_id=1, source_target_pairs={{0,8},{4,12},{8,0},{12,4},{16,24},{20,28},{24,16},{28,20},{32,40},... | collective-permute-start | bytes 602120 | tf_op jit(solution)/shard_map/ppermute | solution.py:350
  21.1 9.1 %collective-permute-start.8 = (f32[384,128]{1,0:T(8,128)S(1)}, f32[384,128]{1,0:T(8,128)S(1)}, u32[]{:S(2)}, u32[]{:S(2)}) collective-permute-start(f32[384,128]{1,0:T(8,128)S(1)} %get-tuple-element.30), channel_id=1, source_target_pairs={{0,24},{4,28},{8,16},{12,20},{16,8},{20,12},{24,0},{28,4},{32,56},... | collective-permute-start | bytes 589832 | tf_op jit(solution)/shard_map/ppermute | solution.py:351
  25.2 5.1 %collective-permute-start.7 = (f32[256,128]{1,0:T(8,128)S(1)}, f32[256,128]{1,0:T(8,128)S(1)}, u32[]{:S(2)}, u32[]{:S(2)}) collective-permute-start(f32[256,128]{1,0:T(8,128)S(1)} %shard_map.51), channel_id=1, source_target_pairs={{0,8},{4,12},{8,0},{12,4},{16,24},{20,28},{24,16},{28,20},{32,40},... | collective-permute-start | bytes 393224 | tf_op jit(solution)/shard_map/ppermute | solution.py:359

commit v6 on v5

--- a/solution.py
+++ b/solution.py
@@ -16,9 +16,8 @@
 PITCH = 24
 PACKED = 18
 WIDE = 20
-TO_PAIR, TO_CROSS = 12, 12
-PAIR_REST, CROSS_REST = 19 - TO_PAIR, 19 - TO_CROSS
-PART = 10
+PART = 8
+TO_PAIR, TO_CROSS, TURN = 19 - PART, PART - 1, PART + 4
 SCALE = 1.0 / math.sqrt(2.0**LEVELS)
 F32 = jnp.float32
 
@@ -174,92 +173,96 @@
         edge[pl.ds(row * 4, 3), :] = second[5:8]
         edge[pl.ds(row * 4 + 3, 1), :] = past
         at = 8 + row * TO_PAIR
-        to_pair[pl.ds(at, TO_PAIR - 8), :] = first[16 - TO_PAIR :]
+        to_pair[pl.ds(at, TO_PAIR - 8), :] = first[PART - 3 :]
         to_pair[pl.ds(at + TO_PAIR - 8, 8), :] = second
         at = 8 + row * TO_CROSS
-        to_cross[pl.ds(at, 7), :] = first[1:8]
-        to_cross[pl.ds(at + 7, TO_CROSS - 7), :] = second[0 : TO_CROSS - 7]
-
-
-def history_kernel(l6, edge, whole, pair_rest, cross_rest):
+        to_cross[pl.ds(at, TO_CROSS), :] = first[1:PART]
+
+
+def history_kernel(l6, edge, whole, cross_rest):
     inner = lax.axis_index("tm") > 0
     for row in range(ROWS):
         at = row * WIDE
         ahead = jnp.where(inner, edge[pl.ds(row * 4, 4), :], 0.0)
         block = l6[pl.ds(row * CHUNKS, CHUNKS), :]
         whole[pl.ds(at, 1), :] = jnp.zeros((1, LANES), F32)
-        whole[pl.ds(at + 1, 3), :] = ahead[0:3]
-        whole[pl.ds(at + 4, 1), :] = ahead[3:4] + block[0:1]
+        for target, to in ((whole, at + 1), (cross_rest, row * 4)):
+            target[pl.ds(to, 3), :] = ahead[0:3]
+            target[pl.ds(to + 3, 1), :] = ahead[3:4] + block[0:1]
         whole[pl.ds(at + 5, CHUNKS - 1), :] = block[1:]
-        to = row * PAIR_REST
-        pair_rest[pl.ds(to, 3), :] = ahead[0:3]
-        pair_rest[pl.ds(to + 3, 1), :] = ahead[3:4] + block[0:1]
-        pair_rest[pl.ds(to + 4, PAIR_REST - 4), :] = block[1 : PAIR_REST - 3]
-        to = row * CROSS_REST
-        cross_rest[pl.ds(to, 3), :] = ahead[0:3]
-        cross_rest[pl.ds(to + 3, 1), :] = ahead[3:4] + block[0:1]
-        cross_rest[pl.ds(to + 4, CROSS_REST - 4), :] = block[TO_CROSS + 1 :]
 
 
 def tables_of(message):
     return message[0:8, :].astype(jnp.int32)
 
 
-def relay_kernel(pair, cross, for_pair, for_cross, terms, plan, sem):
+def onto(out):
+    def put(at, size, value):
+        out[pl.ds(at, size), :] += value
+
+    return put
+
+
+def relay_kernel(l6, pair, cross, for_pair, for_cross, terms, plan, sem):
     _, odd, upper = place()
     pair_tab, cross_tab = tables_of(pair), tables_of(cross)
     plan[...] = jnp.zeros_like(plan)
     plan[0:1, :] = term_codes(cross_tab, pair_tab, 1 - odd, 1 - upper, TO_CROSS)
     plan[1:2, :] = term_codes(pair_tab, cross_tab, 1 - odd, upper, TO_PAIR)
     plan[2:3, :] = term_codes(cross_tab, pair_tab, 1 - odd, 1 - upper, 8)
+    plan[3:4, :] = term_codes(pair_tab, pair_tab, odd, upper, CHUNKS)
+    plan[4:5, :] = term_codes(pair_tab, cross_tab, odd, upper, CHUNKS)
+    plan[5:6, :] = term_codes(pair_tab, pair_tab, odd, upper, WIDE)
     copy = pltpu.make_async_copy(plan, terms, sem)
     copy.start()
     for_pair[ROWS * (PART - 4) :, :] = cross[0:8, :]
     copy.wait()
     shares(cross, 8 + 3, terms, 0, PART - 4, into(for_pair))
-    shares(pair, 8 + TO_PAIR - 16 + PART, terms, 1, 16 - PART, into(for_cross))
-
-
-def first_relay_kernel(cross, cross_rest, terms, _, for_pair, buf):
-    for row in range(ROWS):
-        buf[pl.ds(row * 8 + 1, 4), :] = cross_rest[pl.ds(row * CROSS_REST, 4), :]
+    shares(l6, 4, terms, 3, PART - 4, onto(for_pair))
+    shares(pair, 8 + 3, terms, 1, 16 - PART, into(for_cross))
+    shares(l6, PART, terms, 4, 16 - PART, onto(for_cross))
+
+
+def first_relay_kernel(whole, cross, cross_rest, terms, for_pair, buf):
+    for row in range(ROWS):
+        buf[pl.ds(row * 8 + 1, 4), :] = cross_rest[pl.ds(row * 4, 4), :]
         buf[pl.ds(row * 8 + 5, 3), :] = cross[pl.ds(8 + row * TO_CROSS, 3), :]
     shares(buf, 4, terms, 2, 4, into(for_pair))
-
-
-def direct_kernel(whole, pair, pair_rest, cross, cross_rest, tab, relay, out, pair_buf, buf, plan, terms, sem):
+    shares(whole, 4, terms, 5, 4, onto(for_pair))
+
+
+def direct_kernel(whole, pair, cross, cross_rest, tab, relay, out, buf, plan, terms, sem):
     _, odd, upper = place()
     own, other = tab[...], relay[ROWS * (PART - 4) :, :].astype(jnp.int32)
     plan[...] = jnp.zeros_like(plan)
     plan[0:1, :] = term_codes(own, own, odd, upper, WIDE)
-    plan[1:2, :] = term_codes(own, own, 1 - odd, upper, WIDE)
-    plan[2:3, :] = term_codes(other, own, 1 - odd, 1 - upper, WIDE)
+    plan[1:2, :] = term_codes(own, own, 1 - odd, upper, TO_PAIR)
+    plan[2:3, :] = term_codes(other, own, 1 - odd, 1 - upper, TURN)
     copy = pltpu.make_async_copy(plan, terms, sem)
     copy.start()
     for row in range(ROWS):
-        to, rest = row * WIDE, row * CROSS_REST
-        pair_buf[pl.ds(to + 1, PAIR_REST), :] = pair_rest[pl.ds(row * PAIR_REST, PAIR_REST), :]
-        pair_buf[pl.ds(to + 1 + PAIR_REST, TO_PAIR), :] = pair[
-            pl.ds(8 + row * TO_PAIR, TO_PAIR), :
-        ]
-        buf[pl.ds(to + 1, 4), :] = cross_rest[pl.ds(rest, 4), :]
+        to = row * TURN
+        buf[pl.ds(to + 1, 4), :] = cross_rest[pl.ds(row * 4, 4), :]
         buf[pl.ds(to + 5, TO_CROSS), :] = cross[pl.ds(8 + row * TO_CROSS, TO_CROSS), :]
-        buf[pl.ds(to + 5 + TO_CROSS, CROSS_REST - 4), :] = cross_rest[
-            pl.ds(rest + 4, CROSS_REST - 4), :
-        ]
     copy.wait()
     for row in range(ROWS):
         found = []
         for which in range(3):
             code = terms[which, row]
             found.append((lax.shift_right_arithmetic(code, 7), jnp.bitwise_and(code, LANES - 1)))
-        for first in (0, 8):
+        (own_at, own_turn), near, away = found
+        for first, count, src, ahead, (at, turn) in (
+            (0, PART, buf, 4, away),
+            (PART, 16 - PART, pair, 8 + 3, near),
+        ):
             to = 4 + first
-            total = None
-            for src, (at, turn) in zip((whole, pair_buf, buf), found):
-                term = turned(src[pl.ds(at + to, 8), :], src[pl.ds(at + (to - 1), 8), :], turn)
-                total = term if total is None else total + term
-            out[pl.ds(row * CHUNKS + first, 8), :] = total
+            out[pl.ds(row * CHUNKS + first, count), :] = turned(
+                whole[pl.ds(own_at + to, count), :],
+                whole[pl.ds(own_at + (to - 1), count), :],
+                own_turn,
+            ) + turned(
+                src[pl.ds(at + ahead, count), :], src[pl.ds(at + (ahead - 1), count), :], turn
+            )
 
 
 def last_kernel(mine, first, second, rest, out, buf, sems):
@@ -333,17 +336,16 @@
     pair = lax.ppermute(pair, "freq", by_pair)
     edge = lax.ppermute(edge, "tm", [(i, (i + 1) % 4) for i in range(4)])
 
-    whole, pair_rest, cross_rest = call(
+    whole, cross_rest = call(
         history_kernel,
         [(l6, "v"), (edge, "v")],
-        [pinned(ROWS * WIDE), pinned(ROWS * PAIR_REST), pinned(ROWS * CROSS_REST)],
+        [pinned(ROWS * WIDE), pinned(ROWS * 4)],
     )
     cross_rest = lax.ppermute(cross_rest, "freq", by_cross)
-    pair_rest = lax.ppermute(pair_rest, "freq", by_pair)
 
     for_pair, for_cross, terms = call(
         relay_kernel,
-        [(pair, "v"), (cross, "v")],
+        [(l6, "v"), (pair, "v"), (cross, "v")],
         [pinned(ROWS * (PART - 4) + 8), pinned(ROWS * (16 - PART)), terms_ref],
         [plan, sem],
     )
@@ -352,7 +354,7 @@
 
     (for_pair,) = call(
         first_relay_kernel,
-        [(cross, "v"), (cross_rest, "v"), (terms, "t"), (pair_rest, "v")],
+        [(whole, "v"), (cross, "v"), (cross_rest, "v"), (terms, "t")],
         [pinned(ROWS * 4)],
         [pltpu.VMEM((512, LANES), F32)],
     )
@@ -360,9 +362,9 @@
 
     (mine,) = call(
         direct_kernel,
-        [(a, "v") for a in (whole, pair, pair_rest, cross, cross_rest, own_tab, second)],
+        [(a, "v") for a in (whole, pair, cross, cross_rest, own_tab, second)],
         [pinned(ROWS * CHUNKS)],
-        [pltpu.VMEM((ROWS * WIDE, LANES), F32)] * 2 + [plan, terms_ref, sem],
+        [pltpu.VMEM((ROWS * TURN, LANES), F32), plan, terms_ref, sem],
     )
     (out,) = call(
         last_kernel,

time: 31.3 us -> 29.5 us (0.942)
  waiting for transfers between devices: 14.5 us -> 13.3 us
  starting transfers between devices: 9.84 us -> 9.23 us
    ppermute x1, waiting for transfers between devices: 2.81 us -> 0.01 us  [on_device(): cross = lax.ppermute(cross, 'freq', by_cross)]
    ppermute x1, waiting for transfers between devices: 1.3 us -> 2.69 us  [on_device(): cross_rest = lax.ppermute(cross_rest, 'freq', by_cross)]
    ppermute x1 -> x0, starting transfers between devices: 0.76 us -> none  [on_device(): pair_rest = lax.ppermute(pair_rest, 'freq', by_pair)]
    ppermute x1, waiting for transfers between devices: 0.78 us -> 1.23 us  [on_device(): first = lax.ppermute(for_pair, 'freq', by_pair)]
  transfers between devices with their start and end apart: 9 -> 8, of which waited for: 6 -> 5; matrix products, arithmetic and copies ran while one was open for 0% -> 0% of each run, Pallas kernels for 8% -> 9%
where the time goes in v6:
time: 29.5 us; the launch traced here: 29.4 us
  waiting for transfers between devices  13.3 us (45%)
  starting transfers between devices  9.23 us (31%)
  Pallas kernels  6.82 us (23%)
    pallas_call x7, Pallas kernels, call(): pl.pallas_call(kernel, out_shape=outs, in_specs=[pl.BlockSpec(memory_spac...  6.82 us
    ppermute x1, waiting for transfers between devices, on_device(): edge = lax.ppermute(edge, 'tm', [(i, (i + 1) % 4) for i in range(4)])  4.7 us
    ppermute x1, waiting for transfers between devices, on_device(): cross_rest = lax.ppermute(cross_rest, 'freq', by_cross)  2.69 us
    ppermute x1, waiting for transfers between devices, on_device(): second = lax.ppermute(for_pair, 'freq', by_pair)  2.65 us
    ppermute x1, starting transfers between devices, on_device(): rest = lax.ppermute(for_cross, 'freq', by_cross)  2.42 us
    ppermute x1, starting transfers between devices, on_device(): cross = lax.ppermute(cross, 'freq', by_cross)  2.18 us
    ppermute x1, waiting for transfers between devices, on_device(): l5_far = lax.ppermute(l5, 'freq', swap(1))  1.99 us
    ppermute x1, starting transfers between devices, on_device(): pair = lax.ppermute(pair, 'freq', by_pair)  1.67 us
  transfers between devices with their start and end apart: 8, of which 5 were waited for; matrix products, arithmetic and copies ran while one was open for 0% of the time, Pallas kernels for 9%

profile of v6, /device:TPU:96, one launch (start us, length us, event | category | flops | bytes accessed | tf_op | source)
XLA Modules:
  0.0 29.4 jit_solution(17307009217882702255)
XLA Ops:
  0.0 2.9 %shard_map.46 = (f32[1152,128]{1,0:T(8,128)S(1)}, s32[8,128]{1,0:T(8,128)S(1)}, s32[16,128]{1,0:T(8,128)S(4)}) custom-call(f32[1024,128]{1,0:T(8,128)} %bitcast.10, s32[9,64]{1,0:T(8,128)} %low_h.1, s32[9,64]{1,0:T(8,128)} %high_h.1, s32[9,64]{1,0:T(8,128)} %lag_h.1), custom_call_target="tpu_custom_call" | custom-call | tf_op jit(solution)/shard_map/pallas_call | solution.py:293
  2.9 0.1 collective-permute-start
  3.0 2.0 %collective-permute-done.partner = f32[1152,128]{1,0:T(8,128)S(1)} collective-permute-done((f32[1152,128]{1,0:T(8,128)S(1)}, f32[1152,128]{1,0:T(8,128)S(1)}, u32[]{:S(2)}, u32[]{:S(2)}) %collective-permute-start) | collective-permute-done | bytes 589856 | tf_op jit(solution)/shard_map/ppermute | solution.py:328
  5.0 0.4 %shard_map.47 = (f32[1024,128]{1,0:T(8,128)S(1)}, f32[712,128]{1,0:T(8,128)S(1)}, f32[456,128]{1,0:T(8,128)S(1)}, f32[256,128]{1,0:T(8,128)S(1)}) custom-call(f32[1152,128]{1,0:T(8,128)S(1)} %get-tuple-element.17.own, f32[1152,128]{1,0:T(8,128)S(1)} %collective-permute-done.partner, s32[16,128]{1,0:T(8,128)S(4)} %get-tuple-element.18.codes, ...), custom_call_target="tpu_custom_call" | custom-call | tf_op jit(solution)/shard_map/pallas_call | solution.py:293
  5.4 1.7 %collective-permute-start.2 = (f32[712,128]{1,0:T(8,128)S(1)}, f32[712,128]{1,0:T(8,128)S(1)}, u32[]{:S(2)}, u32[]{:S(2)}) collective-permute-start(f32[712,128]{1,0:T(8,128)S(1)} %get-tuple-element.23), channel_id=1, source_target_pairs={{0,8},{4,12},{8,0},{12,4},{16,24},{20,28},{24,16},{28,20},{32,40},... | collective-permute-start | bytes 1093640 | tf_op jit(solution)/shard_map/ppermute | solution.py:336
  7.0 2.2 %collective-permute-start.3 = (f32[456,128]{1,0:T(8,128)S(1)}, f32[456,128]{1,0:T(8,128)S(1)}, u32[]{:S(2)}, u32[]{:S(2)}) collective-permute-start(f32[456,128]{1,0:T(8,128)S(1)} %get-tuple-element.24), channel_id=1, source_target_pairs={{0,24},{4,28},{8,16},{12,20},{16,8},{20,12},{24,0},{28,4},{32,56},... | collective-permute-start | bytes 700424 | tf_op jit(solution)/shard_map/ppermute | solution.py:335
  9.2 1.5 %collective-permute-start.1 = (f32[256,128]{1,0:T(8,128)S(1)}, f32[256,128]{1,0:T(8,128)S(1)}, u32[]{:S(2)}, u32[]{:S(2)}) collective-permute-start(f32[256,128]{1,0:T(8,128)S(1)} %get-tuple-element.21), channel_id=1, source_target_pairs={{0,1},{1,2},{2,3},{3,0},{4,5},{5,6},{6,7},{7,4},{8,9},{9,10},{10,1... | collective-permute-start | bytes 393224 | tf_op jit(solution)/shard_map/ppermute | solution.py:337
  10.7 4.7 %collective-permute-done.1.edge = f32[256,128]{1,0:T(8,128)S(1)} collective-permute-done((f32[256,128]{1,0:T(8,128)S(1)}, f32[256,128]{1,0:T(8,128)S(1)}, u32[]{:S(2)}, u32[]{:S(2)}) %collective-permute-start.1) | collective-permute-done | bytes 131104 | tf_op jit(solution)/shard_map/ppermute | solution.py:337
  15.4 0.1 shard_map.48
  15.5 1.1 %collective-permute-start.4 = (f32[256,128]{1,0:T(8,128)S(1)}, f32[256,128]{1,0:T(8,128)S(1)}, u32[]{:S(2)}, u32[]{:S(2)}) collective-permute-start(f32[256,128]{1,0:T(8,128)S(1)} %get-tuple-element.25), channel_id=1, source_target_pairs={{0,24},{4,28},{8,16},{12,20},{16,8},{20,12},{24,0},{28,4},{32,56},... | collective-permute-start | bytes 393224 | tf_op jit(solution)/shard_map/ppermute | solution.py:344
  16.7 0.0 collective-permute-done.3.cross
  16.7 0.0 collective-permute-done.2.pair
  16.7 1.2 %shard_map.49 = (f32[264,128]{1,0:T(8,128)S(1)}, f32[512,128]{1,0:T(8,128)S(1)}, s32[8,128]{1,0:T(8,128)S(4)}) custom-call(f32[1024,128]{1,0:T(8,128)S(1)} %get-tuple-element.20.l6, f32[712,128]{1,0:T(8,128)S(1)} %collective-permute-done.2.pair, f32[456,128]{1,0:T(8,128)S(1)} %collective-permute-done.3.cross), custom_call_target="tpu_custom_call" | custom-call | tf_op jit(solution)/shard_map/pallas_call | solution.py:293
  17.9 2.4 %collective-permute-start.7 = (f32[512,128]{1,0:T(8,128)S(1)}, f32[512,128]{1,0:T(8,128)S(1)}, u32[]{:S(2)}, u32[]{:S(2)}) collective-permute-start(f32[512,128]{1,0:T(8,128)S(1)} %get-tuple-element.28), channel_id=1, source_target_pairs={{0,24},{4,28},{8,16},{12,20},{16,8},{20,12},{24,0},{28,4},{32,56},... | collective-permute-start | bytes 786440 | tf_op jit(solution)/shard_map/ppermute | solution.py:353
  20.3 0.1 collective-permute-start.5
  20.4 2.7 %collective-permute-done.4.cross_rest = f32[256,128]{1,0:T(8,128)S(1)} collective-permute-done((f32[256,128]{1,0:T(8,128)S(1)}, f32[256,128]{1,0:T(8,128)S(1)}, u32[]{:S(2)}, u32[]{:S(2)}) %collective-permute-start.4) | collective-permute-done | bytes 131104 | tf_op jit(solution)/shard_map/ppermute | solution.py:344
  23.1 0.3 %shard_map.51 = f32[256,128]{1,0:T(8,128)S(1)} custom-call(f32[1280,128]{1,0:T(8,128)S(1)} %get-tuple-element.22.whole, f32[456,128]{1,0:T(8,128)S(1)} %collective-permute-done.3.cross, f32[256,128]{1,0:T(8,128)S(1)} %collective-permute-done.4.cross_rest, s32[8,128]{1,0:T(8,128)S(4)} %get-tuple-element.27.terms), custom_call_target="tpu_custom_call" | custom-call | tf_op jit(solution)/shard_map/pallas_call | solution.py:293
  23.5 0.1 collective-permute-start.6
  23.6 2.7 %collective-permute-done.5.relay.second = f32[264,128]{1,0:T(8,128)S(1)} collective-permute-done((f32[264,128]{1,0:T(8,128)S(1)}, f32[264,128]{1,0:T(8,128)S(1)}, u32[]{:S(2)}, u32[]{:S(2)}) %collective-permute-start.5) | collective-permute-done | bytes 135200 | tf_op jit(solution)/shard_map/ppermute | solution.py:352
  26.2 1.1 %shard_map.50.mine = f32[1024,128]{1,0:T(8,128)S(1)} custom-call(f32[1280,128]{1,0:T(8,128)S(1)} %get-tuple-element.22.whole, f32[712,128]{1,0:T(8,128)S(1)} %collective-permute-done.2.pair, f32[456,128]{1,0:T(8,128)S(1)} %collective-permute-done.3.cross, f32[256,128]{1,0:T(8,128)S(1)} %collective-permute-done.4.cross_rest, ...), custom_call_target="tpu_custom_call" | custom-call | tf_op jit(solution)/shard_map/pallas_call | solution.py:293
  27.3 1.2 %collective-permute-done.6.first = f32[256,128]{1,0:T(8,128)S(1)} collective-permute-done((f32[256,128]{1,0:T(8,128)S(1)}, f32[256,128]{1,0:T(8,128)S(1)}, u32[]{:S(2)}, u32[]{:S(2)}) %collective-permute-start.6) | collective-permute-done | bytes 131104 | tf_op jit(solution)/shard_map/ppermute | solution.py:361
  28.5 0.0 collective-permute-done.7.rest
  28.5 0.9 %shard_map.52 = f32[1024,128]{1,0:T(8,128)} custom-call(f32[1024,128]{1,0:T(8,128)S(1)} %shard_map.50.mine, f32[256,128]{1,0:T(8,128)S(1)} %collective-permute-done.6.first, f32[264,128]{1,0:T(8,128)S(1)} %collective-permute-done.5.relay.second, f32[512,128]{1,0:T(8,128)S(1)} %collective-permute-done.7.rest), custom_call_target="tpu_custom_call" | custom-call | tf_op jit(solution)/shard_map/pallas_call | solution.py:293
Async XLA Ops:
  2.9 2.1 %collective-permute-start = (f32[1152,128]{1,0:T(8,128)S(1)}, f32[1152,128]{1,0:T(8,128)S(1)}, u32[]{:S(2)}, u32[]{:S(2)}) collective-permute-start(f32[1152,128]{1,0:T(8,128)S(1)} %get-tuple-element.17.own), channel_id=1, source_target_pairs={{0,4},{4,0},{8,12},{12,8},{16,20},{20,16},{24,28},{28,24},{32,36},... | collective-permute-start | bytes 1769480 | tf_op jit(solution)/shard_map/ppermute | solution.py:328
  5.4 11.3 %collective-permute-start.2 = (f32[712,128]{1,0:T(8,128)S(1)}, f32[712,128]{1,0:T(8,128)S(1)}, u32[]{:S(2)}, u32[]{:S(2)}) collective-permute-start(f32[712,128]{1,0:T(8,128)S(1)} %get-tuple-element.23), channel_id=1, source_target_pairs={{0,8},{4,12},{8,0},{12,4},{16,24},{20,28},{24,16},{28,20},{32,40},... | collective-permute-start | bytes 1093640 | tf_op jit(solution)/shard_map/ppermute | solution.py:336
  7.0 9.6 %collective-permute-start.3 = (f32[456,128]{1,0:T(8,128)S(1)}, f32[456,128]{1,0:T(8,128)S(1)}, u32[]{:S(2)}, u32[]{:S(2)}) collective-permute-start(f32[456,128]{1,0:T(8,128)S(1)} %get-tuple-element.24), channel_id=1, source_target_pairs={{0,24},{4,28},{8,16},{12,20},{16,8},{20,12},{24,0},{28,4},{32,56},... | collective-permute-start | bytes 700424 | tf_op jit(solution)/shard_map/ppermute | solution.py:335
  9.2 6.2 %collective-permute-start.1 = (f32[256,128]{1,0:T(8,128)S(1)}, f32[256,128]{1,0:T(8,128)S(1)}, u32[]{:S(2)}, u32[]{:S(2)}) collective-permute-start(f32[256,128]{1,0:T(8,128)S(1)} %get-tuple-element.21), channel_id=1, source_target_pairs={{0,1},{1,2},{2,3},{3,0},{4,5},{5,6},{6,7},{7,4},{8,9},{9,10},{10,1... | collective-permute-start | bytes 393224 | tf_op jit(solution)/shard_map/ppermute | solution.py:337
  15.5 7.6 %collective-permute-start.4 = (f32[256,128]{1,0:T(8,128)S(1)}, f32[256,128]{1,0:T(8,128)S(1)}, u32[]{:S(2)}, u32[]{:S(2)}) collective-permute-start(f32[256,128]{1,0:T(8,128)S(1)} %get-tuple-element.25), channel_id=1, source_target_pairs={{0,24},{4,28},{8,16},{12,20},{16,8},{20,12},{24,0},{28,4},{32,56},... | collective-permute-start | bytes 393224 | tf_op jit(solution)/shard_map/ppermute | solution.py:344
  17.9 10.6 %collective-permute-start.7 = (f32[512,128]{1,0:T(8,128)S(1)}, f32[512,128]{1,0:T(8,128)S(1)}, u32[]{:S(2)}, u32[]{:S(2)}) collective-permute-start(f32[512,128]{1,0:T(8,128)S(1)} %get-tuple-element.28), channel_id=1, source_target_pairs={{0,24},{4,28},{8,16},{12,20},{16,8},{20,12},{24,0},{28,4},{32,56},... | collective-permute-start | bytes 786440 | tf_op jit(solution)/shard_map/ppermute | solution.py:353
  20.3 5.9 %collective-permute-start.5 = (f32[264,128]{1,0:T(8,128)S(1)}, f32[264,128]{1,0:T(8,128)S(1)}, u32[]{:S(2)}, u32[]{:S(2)}) collective-permute-start(f32[264,128]{1,0:T(8,128)S(1)} %get-tuple-element.26), channel_id=1, source_target_pairs={{0,8},{4,12},{8,0},{12,4},{16,24},{20,28},{24,16},{28,20},{32,40},... | collective-permute-start | bytes 405512 | tf_op jit(solution)/shard_map/ppermute | solution.py:352
  23.5 5.0 %collective-permute-start.6 = (f32[256,128]{1,0:T(8,128)S(1)}, f32[256,128]{1,0:T(8,128)S(1)}, u32[]{:S(2)}, u32[]{:S(2)}) collective-permute-start(f32[256,128]{1,0:T(8,128)S(1)} %shard_map.51), channel_id=1, source_target_pairs={{0,8},{4,12},{8,0},{12,4},{16,24},{20,28},{24,16},{28,20},{32,40},... | collective-permute-start | bytes 393224 | tf_op jit(solution)/shard_map/ppermute | solution.py:361

commit v7 on v6

--- a/solution.py
+++ b/solution.py
@@ -16,7 +16,7 @@
 PITCH = 24
 PACKED = 18
 WIDE = 20
-PART = 8
+PART = 10
 TO_PAIR, TO_CROSS, TURN = 19 - PART, PART - 1, PART + 4
 SCALE = 1.0 / math.sqrt(2.0**LEVELS)
 F32 = jnp.float32
@@ -176,7 +176,8 @@
         to_pair[pl.ds(at, TO_PAIR - 8), :] = first[PART - 3 :]
         to_pair[pl.ds(at + TO_PAIR - 8, 8), :] = second
         at = 8 + row * TO_CROSS
-        to_cross[pl.ds(at, TO_CROSS), :] = first[1:PART]
+        to_cross[pl.ds(at, 7), :] = first[1:8]
+        to_cross[pl.ds(at + 7, PART - 8), :] = second[0 : PART - 8]
 
 
 def history_kernel(l6, edge, whole, cross_rest):

time: 29.5 us -> 28.7 us (0.973)
  waiting for transfers between devices: 13.3 us -> 12 us
    ppermute x1, waiting for transfers between devices: 2.69 us -> 1.16 us  [on_device(): cross_rest = lax.ppermute(cross_rest, 'freq', by_cross)]
    ppermute x1, waiting for transfers between devices: 0.01 us -> 0.43 us  [on_device(): cross = lax.ppermute(cross, 'freq', by_cross)]
    ppermute x1, waiting for transfers between devices: 1.23 us -> 0.84 us  [on_device(): first = lax.ppermute(for_pair, 'freq', by_pair)]
    ppermute x1, starting transfers between devices: 2.42 us -> 2.76 us  [on_device(): rest = lax.ppermute(for_cross, 'freq', by_cross)]
  transfers between devices with their start and end apart: 8 -> 8, of which waited for: 5 -> 6; matrix products, arithmetic and copies ran while one was open for 0% -> 0% of each run, Pallas kernels for 9% -> 10%
where the time goes in v7:
time: 28.7 us; the launch traced here: 28.6 us
  waiting for transfers between devices  12 us (42%)
  starting transfers between devices  9.52 us (33%)
  Pallas kernels  7 us (24%)
    pallas_call x7, Pallas kernels, call(): pl.pallas_call(kernel, out_shape=outs, in_specs=[pl.BlockSpec(memory_spac...  7 us
    ppermute x1, waiting for transfers between devices, on_device(): edge = lax.ppermute(edge, 'tm', [(i, (i + 1) % 4) for i in range(4)])  4.7 us
    ppermute x1, waiting for transfers between devices, on_device(): second = lax.ppermute(for_pair, 'freq', by_pair)  2.92 us
    ppermute x1, starting transfers between devices, on_device(): rest = lax.ppermute(for_cross, 'freq', by_cross)  2.76 us
    ppermute x1, starting transfers between devices, on_device(): cross = lax.ppermute(cross, 'freq', by_cross)  2.18 us
    ppermute x1, waiting for transfers between devices, on_device(): l5_far = lax.ppermute(l5, 'freq', swap(1))  1.99 us
    ppermute x1, starting transfers between devices, on_device(): pair = lax.ppermute(pair, 'freq', by_pair)  1.67 us
    ppermute x1, starting transfers between devices, on_device(): edge = lax.ppermute(edge, 'tm', [(i, (i + 1) % 4) for i in range(4)])  1.49 us
  transfers between devices with their start and end apart: 8, of which 6 were waited for; matrix products, arithmetic and copies ran while one was open for 0% of the time, Pallas kernels for 10%

profile of v7, /device:TPU:96, one launch (start us, length us, event | category | flops | bytes accessed | tf_op | source)
XLA Modules:
  0.0 28.6 jit_solution(13444117651792378948)
XLA Ops:
  0.0 2.9 %shard_map.46 = (f32[1152,128]{1,0:T(8,128)S(1)}, s32[8,128]{1,0:T(8,128)S(1)}, s32[16,128]{1,0:T(8,128)S(4)}) custom-call(f32[1024,128]{1,0:T(8,128)} %bitcast.10, s32[9,64]{1,0:T(8,128)} %low_h.1, s32[9,64]{1,0:T(8,128)} %high_h.1, s32[9,64]{1,0:T(8,128)} %lag_h.1), custom_call_target="tpu_custom_call" | custom-call | tf_op jit(solution)/shard_map/pallas_call | solution.py:294
  2.9 0.1 collective-permute-start
  3.0 2.0 %collective-permute-done.partner = f32[1152,128]{1,0:T(8,128)S(1)} collective-permute-done((f32[1152,128]{1,0:T(8,128)S(1)}, f32[1152,128]{1,0:T(8,128)S(1)}, u32[]{:S(2)}, u32[]{:S(2)}) %collective-permute-start) | collective-permute-done | bytes 589856 | tf_op jit(solution)/shard_map/ppermute | solution.py:329
  5.0 0.4 %shard_map.47 = (f32[1024,128]{1,0:T(8,128)S(1)}, f32[584,128]{1,0:T(8,128)S(1)}, f32[584,128]{1,0:T(8,128)S(1)}, f32[256,128]{1,0:T(8,128)S(1)}) custom-call(f32[1152,128]{1,0:T(8,128)S(1)} %get-tuple-element.17.own, f32[1152,128]{1,0:T(8,128)S(1)} %collective-permute-done.partner, s32[16,128]{1,0:T(8,128)S(4)} %get-tuple-element.18.codes, ...), custom_call_target="tpu_custom_call" | custom-call | tf_op jit(solution)/shard_map/pallas_call | solution.py:294
  5.4 1.7 %collective-permute-start.2 = (f32[584,128]{1,0:T(8,128)S(1)}, f32[584,128]{1,0:T(8,128)S(1)}, u32[]{:S(2)}, u32[]{:S(2)}) collective-permute-start(f32[584,128]{1,0:T(8,128)S(1)} %get-tuple-element.23), channel_id=1, source_target_pairs={{0,8},{4,12},{8,0},{12,4},{16,24},{20,28},{24,16},{28,20},{32,40},... | collective-permute-start | bytes 897032 | tf_op jit(solution)/shard_map/ppermute | solution.py:337
  7.0 2.2 %collective-permute-start.3 = (f32[584,128]{1,0:T(8,128)S(1)}, f32[584,128]{1,0:T(8,128)S(1)}, u32[]{:S(2)}, u32[]{:S(2)}) collective-permute-start(f32[584,128]{1,0:T(8,128)S(1)} %get-tuple-element.24), channel_id=1, source_target_pairs={{0,24},{4,28},{8,16},{12,20},{16,8},{20,12},{24,0},{28,4},{32,56},... | collective-permute-start | bytes 897032 | tf_op jit(solution)/shard_map/ppermute | solution.py:336
  9.2 1.5 %collective-permute-start.1 = (f32[256,128]{1,0:T(8,128)S(1)}, f32[256,128]{1,0:T(8,128)S(1)}, u32[]{:S(2)}, u32[]{:S(2)}) collective-permute-start(f32[256,128]{1,0:T(8,128)S(1)} %get-tuple-element.21), channel_id=1, source_target_pairs={{0,1},{1,2},{2,3},{3,0},{4,5},{5,6},{6,7},{7,4},{8,9},{9,10},{10,1... | collective-permute-start | bytes 393224 | tf_op jit(solution)/shard_map/ppermute | solution.py:338
  10.7 4.7 %collective-permute-done.1.edge = f32[256,128]{1,0:T(8,128)S(1)} collective-permute-done((f32[256,128]{1,0:T(8,128)S(1)}, f32[256,128]{1,0:T(8,128)S(1)}, u32[]{:S(2)}, u32[]{:S(2)}) %collective-permute-start.1) | collective-permute-done | bytes 131104 | tf_op jit(solution)/shard_map/ppermute | solution.py:338
  15.4 0.1 shard_map.48
  15.5 1.1 %collective-permute-start.4 = (f32[256,128]{1,0:T(8,128)S(1)}, f32[256,128]{1,0:T(8,128)S(1)}, u32[]{:S(2)}, u32[]{:S(2)}) collective-permute-start(f32[256,128]{1,0:T(8,128)S(1)} %get-tuple-element.25), channel_id=1, source_target_pairs={{0,24},{4,28},{8,16},{12,20},{16,8},{20,12},{24,0},{28,4},{32,56},... | collective-permute-start | bytes 393224 | tf_op jit(solution)/shard_map/ppermute | solution.py:345
  16.7 0.0 collective-permute-done.2.pair
  16.7 0.4 %collective-permute-done.3.cross = f32[584,128]{1,0:T(8,128)S(1)} collective-permute-done((f32[584,128]{1,0:T(8,128)S(1)}, f32[584,128]{1,0:T(8,128)S(1)}, u32[]{:S(2)}, u32[]{:S(2)}) %collective-permute-start.3) | collective-permute-done | bytes 299040 | tf_op jit(solution)/shard_map/ppermute | solution.py:336
  17.1 1.2 %shard_map.49 = (f32[392,128]{1,0:T(8,128)S(1)}, f32[384,128]{1,0:T(8,128)S(1)}, s32[8,128]{1,0:T(8,128)S(4)}) custom-call(f32[1024,128]{1,0:T(8,128)S(1)} %get-tuple-element.20.l6, f32[584,128]{1,0:T(8,128)S(1)} %collective-permute-done.2.pair, f32[584,128]{1,0:T(8,128)S(1)} %collective-permute-done.3.cross), custom_call_target="tpu_custom_call" | custom-call | tf_op jit(solution)/shard_map/pallas_call | solution.py:294
  18.3 0.1 collective-permute-start.5
  18.4 2.8 %collective-permute-start.7 = (f32[384,128]{1,0:T(8,128)S(1)}, f32[384,128]{1,0:T(8,128)S(1)}, u32[]{:S(2)}, u32[]{:S(2)}) collective-permute-start(f32[384,128]{1,0:T(8,128)S(1)} %get-tuple-element.28), channel_id=1, source_target_pairs={{0,24},{4,28},{8,16},{12,20},{16,8},{20,12},{24,0},{28,4},{32,56},... | collective-permute-start | bytes 589832 | tf_op jit(solution)/shard_map/ppermute | solution.py:354
  21.2 1.2 %collective-permute-done.4.cross_rest = f32[256,128]{1,0:T(8,128)S(1)} collective-permute-done((f32[256,128]{1,0:T(8,128)S(1)}, f32[256,128]{1,0:T(8,128)S(1)}, u32[]{:S(2)}, u32[]{:S(2)}) %collective-permute-start.4) | collective-permute-done | bytes 131104 | tf_op jit(solution)/shard_map/ppermute | solution.py:345
  22.3 0.3 %shard_map.51 = f32[256,128]{1,0:T(8,128)S(1)} custom-call(f32[1280,128]{1,0:T(8,128)S(1)} %get-tuple-element.22.whole, f32[584,128]{1,0:T(8,128)S(1)} %collective-permute-done.3.cross, f32[256,128]{1,0:T(8,128)S(1)} %collective-permute-done.4.cross_rest, s32[8,128]{1,0:T(8,128)S(4)} %get-tuple-element.27.terms), custom_call_target="tpu_custom_call" | custom-call | tf_op jit(solution)/shard_map/pallas_call | solution.py:294
  22.7 0.1 collective-permute-start.6
  22.8 2.9 %collective-permute-done.5.relay.second = f32[392,128]{1,0:T(8,128)S(1)} collective-permute-done((f32[392,128]{1,0:T(8,128)S(1)}, f32[392,128]{1,0:T(8,128)S(1)}, u32[]{:S(2)}, u32[]{:S(2)}) %collective-permute-start.5) | collective-permute-done | bytes 200736 | tf_op jit(solution)/shard_map/ppermute | solution.py:353
  25.7 1.2 %shard_map.50.mine = f32[1024,128]{1,0:T(8,128)S(1)} custom-call(f32[1280,128]{1,0:T(8,128)S(1)} %get-tuple-element.22.whole, f32[584,128]{1,0:T(8,128)S(1)} %collective-permute-done.2.pair, f32[584,128]{1,0:T(8,128)S(1)} %collective-permute-done.3.cross, f32[256,128]{1,0:T(8,128)S(1)} %collective-permute-done.4.cross_rest, ...), custom_call_target="tpu_custom_call" | custom-call | tf_op jit(solution)/shard_map/pallas_call | solution.py:294
  26.9 0.8 %collective-permute-done.6.first = f32[256,128]{1,0:T(8,128)S(1)} collective-permute-done((f32[256,128]{1,0:T(8,128)S(1)}, f32[256,128]{1,0:T(8,128)S(1)}, u32[]{:S(2)}, u32[]{:S(2)}) %collective-permute-start.6) | collective-permute-done | bytes 131104 | tf_op jit(solution)/shard_map/ppermute | solution.py:362
  27.7 0.0 collective-permute-done.7.rest
  27.7 0.9 %shard_map.52 = f32[1024,128]{1,0:T(8,128)} custom-call(f32[1024,128]{1,0:T(8,128)S(1)} %shard_map.50.mine, f32[256,128]{1,0:T(8,128)S(1)} %collective-permute-done.6.first, f32[392,128]{1,0:T(8,128)S(1)} %collective-permute-done.5.relay.second, f32[384,128]{1,0:T(8,128)S(1)} %collective-permute-done.7.rest), custom_call_target="tpu_custom_call" | custom-call | tf_op jit(solution)/shard_map/pallas_call | solution.py:294
Async XLA Ops:
  2.9 2.1 %collective-permute-start = (f32[1152,128]{1,0:T(8,128)S(1)}, f32[1152,128]{1,0:T(8,128)S(1)}, u32[]{:S(2)}, u32[]{:S(2)}) collective-permute-start(f32[1152,128]{1,0:T(8,128)S(1)} %get-tuple-element.17.own), channel_id=1, source_target_pairs={{0,4},{4,0},{8,12},{12,8},{16,20},{20,16},{24,28},{28,24},{32,36},... | collective-permute-start | bytes 1769480 | tf_op jit(solution)/shard_map/ppermute | solution.py:329
  5.4 11.3 %collective-permute-start.2 = (f32[584,128]{1,0:T(8,128)S(1)}, f32[584,128]{1,0:T(8,128)S(1)}, u32[]{:S(2)}, u32[]{:S(2)}) collective-permute-start(f32[584,128]{1,0:T(8,128)S(1)} %get-tuple-element.23), channel_id=1, source_target_pairs={{0,8},{4,12},{8,0},{12,4},{16,24},{20,28},{24,16},{28,20},{32,40},... | collective-permute-start | bytes 897032 | tf_op jit(solution)/shard_map/ppermute | solution.py:337
  7.0 10.1 %collective-permute-start.3 = (f32[584,128]{1,0:T(8,128)S(1)}, f32[584,128]{1,0:T(8,128)S(1)}, u32[]{:S(2)}, u32[]{:S(2)}) collective-permute-start(f32[584,128]{1,0:T(8,128)S(1)} %get-tuple-element.24), channel_id=1, source_target_pairs={{0,24},{4,28},{8,16},{12,20},{16,8},{20,12},{24,0},{28,4},{32,56},... | collective-permute-start | bytes 897032 | tf_op jit(solution)/shard_map/ppermute | solution.py:336
  9.2 6.2 %collective-permute-start.1 = (f32[256,128]{1,0:T(8,128)S(1)}, f32[256,128]{1,0:T(8,128)S(1)}, u32[]{:S(2)}, u32[]{:S(2)}) collective-permute-start(f32[256,128]{1,0:T(8,128)S(1)} %get-tuple-element.21), channel_id=1, source_target_pairs={{0,1},{1,2},{2,3},{3,0},{4,5},{5,6},{6,7},{7,4},{8,9},{9,10},{10,1... | collective-permute-start | bytes 393224 | tf_op jit(solution)/shard_map/ppermute | solution.py:338
  15.5 6.8 %collective-permute-start.4 = (f32[256,128]{1,0:T(8,128)S(1)}, f32[256,128]{1,0:T(8,128)S(1)}, u32[]{:S(2)}, u32[]{:S(2)}) collective-permute-start(f32[256,128]{1,0:T(8,128)S(1)} %get-tuple-element.25), channel_id=1, source_target_pairs={{0,24},{4,28},{8,16},{12,20},{16,8},{20,12},{24,0},{28,4},{32,56},... | collective-permute-start | bytes 393224 | tf_op jit(solution)/shard_map/ppermute | solution.py:345
  18.3 7.4 %collective-permute-start.5 = (f32[392,128]{1,0:T(8,128)S(1)}, f32[392,128]{1,0:T(8,128)S(1)}, u32[]{:S(2)}, u32[]{:S(2)}) collective-permute-start(f32[392,128]{1,0:T(8,128)S(1)} %get-tuple-element.26), channel_id=1, source_target_pairs={{0,8},{4,12},{8,0},{12,4},{16,24},{20,28},{24,16},{28,20},{32,40},... | collective-permute-start | bytes 602120 | tf_op jit(solution)/shard_map/ppermute | solution.py:353
  18.4 9.3 %collective-permute-start.7 = (f32[384,128]{1,0:T(8,128)S(1)}, f32[384,128]{1,0:T(8,128)S(1)}, u32[]{:S(2)}, u32[]{:S(2)}) collective-permute-start(f32[384,128]{1,0:T(8,128)S(1)} %get-tuple-element.28), channel_id=1, source_target_pairs={{0,24},{4,28},{8,16},{12,20},{16,8},{20,12},{24,0},{28,4},{32,56},... | collective-permute-start | bytes 589832 | tf_op jit(solution)/shard_map/ppermute | solution.py:354
  22.7 5.1 %collective-permute-start.6 = (f32[256,128]{1,0:T(8,128)S(1)}, f32[256,128]{1,0:T(8,128)S(1)}, u32[]{:S(2)}, u32[]{:S(2)}) collective-permute-start(f32[256,128]{1,0:T(8,128)S(1)} %shard_map.51), channel_id=1, source_target_pairs={{0,8},{4,12},{8,0},{12,4},{16,24},{20,28},{24,16},{28,20},{32,40},... | collective-permute-start | bytes 393224 | tf_op jit(solution)/shard_map/ppermute | solution.py:362

commit v8 on v7

--- a/solution.py
+++ b/solution.py
@@ -224,12 +224,19 @@
     shares(l6, PART, terms, 4, 16 - PART, onto(for_cross))
 
 
-def first_relay_kernel(whole, cross, cross_rest, terms, for_pair, buf):
+def first_own_kernel(whole, terms, for_pair):
+    shares(whole, 4, terms, 5, 4, into(for_pair))
+
+
+def first_relay_kernel(own, cross, cross_rest, terms, for_pair, buf):
     for row in range(ROWS):
         buf[pl.ds(row * 8 + 1, 4), :] = cross_rest[pl.ds(row * 4, 4), :]
         buf[pl.ds(row * 8 + 5, 3), :] = cross[pl.ds(8 + row * TO_CROSS, 3), :]
-    shares(buf, 4, terms, 2, 4, into(for_pair))
-    shares(whole, 4, terms, 5, 4, onto(for_pair))
+
+    def put(at, size, value):
+        for_pair[pl.ds(at, size), :] = value + own[pl.ds(at, size), :]
+
+    shares(buf, 4, terms, 2, 4, put)
 
 
 def direct_kernel(whole, pair, cross, cross_rest, tab, relay, out, buf, plan, terms, sem):
@@ -353,9 +360,10 @@
     second = lax.ppermute(for_pair, "freq", by_pair)
     rest = lax.ppermute(for_cross, "freq", by_cross)
 
+    (own_first,) = call(first_own_kernel, [(whole, "v"), (terms, "t")], [pinned(ROWS * 4)])
     (for_pair,) = call(
         first_relay_kernel,
-        [(whole, "v"), (cross, "v"), (cross_rest, "v"), (terms, "t")],
+        [(own_first, "v"), (cross, "v"), (cross_rest, "v"), (terms, "t")],
         [pinned(ROWS * 4)],
         [pltpu.VMEM((512, LANES), F32)],
     )

time: 28.7 us -> 28.6 us (level)
    pallas_call x7 -> x8, Pallas kernels: 7 us -> 7.05 us  [call(): pl.pallas_call(kernel, out_shape=outs, in_specs=[pl.BlockSpec(memory_spac...]
where the time goes in v8:
time: 28.6 us; the launch traced here: 28.5 us
  waiting for transfers between devices  11.9 us (42%)
  starting transfers between devices  9.52 us (33%)
  Pallas kernels  7.05 us (25%)
    pallas_call x8, Pallas kernels, call(): pl.pallas_call(kernel, out_shape=outs, in_specs=[pl.BlockSpec(memory_spac...  7.05 us
    ppermute x1, waiting for transfers between devices, on_device(): edge = lax.ppermute(edge, 'tm', [(i, (i + 1) % 4) for i in range(4)])  4.7 us
    ppermute x1, waiting for transfers between devices, on_device(): second = lax.ppermute(for_pair, 'freq', by_pair)  3.03 us
    ppermute x1, starting transfers between devices, on_device(): rest = lax.ppermute(for_cross, 'freq', by_cross)  2.78 us
    ppermute x1, starting transfers between devices, on_device(): cross = lax.ppermute(cross, 'freq', by_cross)  2.18 us
    ppermute x1, waiting for transfers between devices, on_device(): l5_far = lax.ppermute(l5, 'freq', swap(1))  1.99 us
    ppermute x1, starting transfers between devices, on_device(): pair = lax.ppermute(pair, 'freq', by_pair)  1.66 us
    ppermute x1, starting transfers between devices, on_device(): edge = lax.ppermute(edge, 'tm', [(i, (i + 1) % 4) for i in range(4)])  1.49 us
  transfers between devices with their start and end apart: 8, of which 6 were waited for; matrix products, arithmetic and copies ran while one was open for 0% of the time, Pallas kernels for 10%

profile of v8, /device:TPU:96, one launch (start us, length us, event | category | flops | bytes accessed | tf_op | source)
XLA Modules:
  0.0 28.5 jit_solution(1599849150710889819)
XLA Ops:
  0.0 2.9 %shard_map.46 = (f32[1152,128]{1,0:T(8,128)S(1)}, s32[8,128]{1,0:T(8,128)S(1)}, s32[16,128]{1,0:T(8,128)S(4)}) custom-call(f32[1024,128]{1,0:T(8,128)} %bitcast.10, s32[9,64]{1,0:T(8,128)} %low_h.1, s32[9,64]{1,0:T(8,128)} %high_h.1, s32[9,64]{1,0:T(8,128)} %lag_h.1), custom_call_target="tpu_custom_call" | custom-call | tf_op jit(solution)/shard_map/pallas_call | solution.py:301
  2.9 0.1 collective-permute-start
  3.0 2.0 %collective-permute-done.partner = f32[1152,128]{1,0:T(8,128)S(1)} collective-permute-done((f32[1152,128]{1,0:T(8,128)S(1)}, f32[1152,128]{1,0:T(8,128)S(1)}, u32[]{:S(2)}, u32[]{:S(2)}) %collective-permute-start) | collective-permute-done | bytes 589856 | tf_op jit(solution)/shard_map/ppermute | solution.py:336
  5.0 0.4 %shard_map.47 = (f32[1024,128]{1,0:T(8,128)S(1)}, f32[584,128]{1,0:T(8,128)S(1)}, f32[584,128]{1,0:T(8,128)S(1)}, f32[256,128]{1,0:T(8,128)S(1)}) custom-call(f32[1152,128]{1,0:T(8,128)S(1)} %get-tuple-element.17.own, f32[1152,128]{1,0:T(8,128)S(1)} %collective-permute-done.partner, s32[16,128]{1,0:T(8,128)S(4)} %get-tuple-element.18.codes, ...), custom_call_target="tpu_custom_call" | custom-call | tf_op jit(solution)/shard_map/pallas_call | solution.py:301
  5.4 1.7 %collective-permute-start.2 = (f32[584,128]{1,0:T(8,128)S(1)}, f32[584,128]{1,0:T(8,128)S(1)}, u32[]{:S(2)}, u32[]{:S(2)}) collective-permute-start(f32[584,128]{1,0:T(8,128)S(1)} %get-tuple-element.23), channel_id=1, source_target_pairs={{0,8},{4,12},{8,0},{12,4},{16,24},{20,28},{24,16},{28,20},{32,40},... | collective-permute-start | bytes 897032 | tf_op jit(solution)/shard_map/ppermute | solution.py:344
  7.0 2.2 %collective-permute-start.3 = (f32[584,128]{1,0:T(8,128)S(1)}, f32[584,128]{1,0:T(8,128)S(1)}, u32[]{:S(2)}, u32[]{:S(2)}) collective-permute-start(f32[584,128]{1,0:T(8,128)S(1)} %get-tuple-element.24), channel_id=1, source_target_pairs={{0,24},{4,28},{8,16},{12,20},{16,8},{20,12},{24,0},{28,4},{32,56},... | collective-permute-start | bytes 897032 | tf_op jit(solution)/shard_map/ppermute | solution.py:343
  9.2 1.5 %collective-permute-start.1 = (f32[256,128]{1,0:T(8,128)S(1)}, f32[256,128]{1,0:T(8,128)S(1)}, u32[]{:S(2)}, u32[]{:S(2)}) collective-permute-start(f32[256,128]{1,0:T(8,128)S(1)} %get-tuple-element.21), channel_id=1, source_target_pairs={{0,1},{1,2},{2,3},{3,0},{4,5},{5,6},{6,7},{7,4},{8,9},{9,10},{10,1... | collective-permute-start | bytes 393224 | tf_op jit(solution)/shard_map/ppermute | solution.py:345
  10.7 4.7 %collective-permute-done.1.edge = f32[256,128]{1,0:T(8,128)S(1)} collective-permute-done((f32[256,128]{1,0:T(8,128)S(1)}, f32[256,128]{1,0:T(8,128)S(1)}, u32[]{:S(2)}, u32[]{:S(2)}) %collective-permute-start.1) | collective-permute-done | bytes 131104 | tf_op jit(solution)/shard_map/ppermute | solution.py:345
  15.4 0.1 shard_map.48
  15.5 1.1 %collective-permute-start.4 = (f32[256,128]{1,0:T(8,128)S(1)}, f32[256,128]{1,0:T(8,128)S(1)}, u32[]{:S(2)}, u32[]{:S(2)}) collective-permute-start(f32[256,128]{1,0:T(8,128)S(1)} %get-tuple-element.25), channel_id=1, source_target_pairs={{0,24},{4,28},{8,16},{12,20},{16,8},{20,12},{24,0},{28,4},{32,56},... | collective-permute-start | bytes 393224 | tf_op jit(solution)/shard_map/ppermute | solution.py:352
  16.7 0.0 collective-permute-done.2.pair
  16.7 0.4 %collective-permute-done.3.cross = f32[584,128]{1,0:T(8,128)S(1)} collective-permute-done((f32[584,128]{1,0:T(8,128)S(1)}, f32[584,128]{1,0:T(8,128)S(1)}, u32[]{:S(2)}, u32[]{:S(2)}) %collective-permute-start.3) | collective-permute-done | bytes 299040 | tf_op jit(solution)/shard_map/ppermute | solution.py:343
  17.1 1.2 %shard_map.49 = (f32[392,128]{1,0:T(8,128)S(1)}, f32[384,128]{1,0:T(8,128)S(1)}, s32[8,128]{1,0:T(8,128)S(4)}) custom-call(f32[1024,128]{1,0:T(8,128)S(1)} %get-tuple-element.20.l6, f32[584,128]{1,0:T(8,128)S(1)} %collective-permute-done.2.pair, f32[584,128]{1,0:T(8,128)S(1)} %collective-permute-done.3.cross), custom_call_target="tpu_custom_call" | custom-call | tf_op jit(solution)/shard_map/pallas_call | solution.py:301
  18.3 0.1 collective-permute-start.5
  18.4 2.8 %collective-permute-start.7 = (f32[384,128]{1,0:T(8,128)S(1)}, f32[384,128]{1,0:T(8,128)S(1)}, u32[]{:S(2)}, u32[]{:S(2)}) collective-permute-start(f32[384,128]{1,0:T(8,128)S(1)} %get-tuple-element.28), channel_id=1, source_target_pairs={{0,24},{4,28},{8,16},{12,20},{16,8},{20,12},{24,0},{28,4},{32,56},... | collective-permute-start | bytes 589832 | tf_op jit(solution)/shard_map/ppermute | solution.py:361
  21.2 0.2 shard_map.51.own
  21.3 1.0 %collective-permute-done.4.cross_rest = f32[256,128]{1,0:T(8,128)S(1)} collective-permute-done((f32[256,128]{1,0:T(8,128)S(1)}, f32[256,128]{1,0:T(8,128)S(1)}, u32[]{:S(2)}, u32[]{:S(2)}) %collective-permute-start.4) | collective-permute-done | bytes 131104 | tf_op jit(solution)/shard_map/ppermute | solution.py:352
  22.3 0.2 shard_map.52
  22.5 0.1 collective-permute-start.6
  22.6 3.0 %collective-permute-done.5.relay.second = f32[392,128]{1,0:T(8,128)S(1)} collective-permute-done((f32[392,128]{1,0:T(8,128)S(1)}, f32[392,128]{1,0:T(8,128)S(1)}, u32[]{:S(2)}, u32[]{:S(2)}) %collective-permute-start.5) | collective-permute-done | bytes 200736 | tf_op jit(solution)/shard_map/ppermute | solution.py:360
  25.7 1.2 %shard_map.50.mine = f32[1024,128]{1,0:T(8,128)S(1)} custom-call(f32[1280,128]{1,0:T(8,128)S(1)} %get-tuple-element.22.whole, f32[584,128]{1,0:T(8,128)S(1)} %collective-permute-done.2.pair, f32[584,128]{1,0:T(8,128)S(1)} %collective-permute-done.3.cross, f32[256,128]{1,0:T(8,128)S(1)} %collective-permute-done.4.cross_rest, ...), custom_call_target="tpu_custom_call" | custom-call | tf_op jit(solution)/shard_map/pallas_call | solution.py:301
  26.9 0.7 %collective-permute-done.6.first = f32[256,128]{1,0:T(8,128)S(1)} collective-permute-done((f32[256,128]{1,0:T(8,128)S(1)}, f32[256,128]{1,0:T(8,128)S(1)}, u32[]{:S(2)}, u32[]{:S(2)}) %collective-permute-start.6) | collective-permute-done | bytes 131104 | tf_op jit(solution)/shard_map/ppermute | solution.py:370
  27.6 0.0 collective-permute-done.7.rest
  27.6 0.9 %shard_map.53 = f32[1024,128]{1,0:T(8,128)} custom-call(f32[1024,128]{1,0:T(8,128)S(1)} %shard_map.50.mine, f32[256,128]{1,0:T(8,128)S(1)} %collective-permute-done.6.first, f32[392,128]{1,0:T(8,128)S(1)} %collective-permute-done.5.relay.second, f32[384,128]{1,0:T(8,128)S(1)} %collective-permute-done.7.rest), custom_call_target="tpu_custom_call" | custom-call | tf_op jit(solution)/shard_map/pallas_call | solution.py:301
Async XLA Ops:
  2.9 2.1 %collective-permute-start = (f32[1152,128]{1,0:T(8,128)S(1)}, f32[1152,128]{1,0:T(8,128)S(1)}, u32[]{:S(2)}, u32[]{:S(2)}) collective-permute-start(f32[1152,128]{1,0:T(8,128)S(1)} %get-tuple-element.17.own), channel_id=1, source_target_pairs={{0,4},{4,0},{8,12},{12,8},{16,20},{20,16},{24,28},{28,24},{32,36},... | collective-permute-start | bytes 1769480 | tf_op jit(solution)/shard_map/ppermute | solution.py:336
  5.4 11.3 %collective-permute-start.2 = (f32[584,128]{1,0:T(8,128)S(1)}, f32[584,128]{1,0:T(8,128)S(1)}, u32[]{:S(2)}, u32[]{:S(2)}) collective-permute-start(f32[584,128]{1,0:T(8,128)S(1)} %get-tuple-element.23), channel_id=1, source_target_pairs={{0,8},{4,12},{8,0},{12,4},{16,24},{20,28},{24,16},{28,20},{32,40},... | collective-permute-start | bytes 897032 | tf_op jit(solution)/shard_map/ppermute | solution.py:344
  7.0 10.1 %collective-permute-start.3 = (f32[584,128]{1,0:T(8,128)S(1)}, f32[584,128]{1,0:T(8,128)S(1)}, u32[]{:S(2)}, u32[]{:S(2)}) collective-permute-start(f32[584,128]{1,0:T(8,128)S(1)} %get-tuple-element.24), channel_id=1, source_target_pairs={{0,24},{4,28},{8,16},{12,20},{16,8},{20,12},{24,0},{28,4},{32,56},... | collective-permute-start | bytes 897032 | tf_op jit(solution)/shard_map/ppermute | solution.py:343
  9.2 6.2 %collective-permute-start.1 = (f32[256,128]{1,0:T(8,128)S(1)}, f32[256,128]{1,0:T(8,128)S(1)}, u32[]{:S(2)}, u32[]{:S(2)}) collective-permute-start(f32[256,128]{1,0:T(8,128)S(1)} %get-tuple-element.21), channel_id=1, source_target_pairs={{0,1},{1,2},{2,3},{3,0},{4,5},{5,6},{6,7},{7,4},{8,9},{9,10},{10,1... | collective-permute-start | bytes 393224 | tf_op jit(solution)/shard_map/ppermute | solution.py:345
  15.5 6.8 %collective-permute-start.4 = (f32[256,128]{1,0:T(8,128)S(1)}, f32[256,128]{1,0:T(8,128)S(1)}, u32[]{:S(2)}, u32[]{:S(2)}) collective-permute-start(f32[256,128]{1,0:T(8,128)S(1)} %get-tuple-element.25), channel_id=1, source_target_pairs={{0,24},{4,28},{8,16},{12,20},{16,8},{20,12},{24,0},{28,4},{32,56},... | collective-permute-start | bytes 393224 | tf_op jit(solution)/shard_map/ppermute | solution.py:352
  18.3 7.4 %collective-permute-start.5 = (f32[392,128]{1,0:T(8,128)S(1)}, f32[392,128]{1,0:T(8,128)S(1)}, u32[]{:S(2)}, u32[]{:S(2)}) collective-permute-start(f32[392,128]{1,0:T(8,128)S(1)} %get-tuple-element.26), channel_id=1, source_target_pairs={{0,8},{4,12},{8,0},{12,4},{16,24},{20,28},{24,16},{28,20},{32,40},... | collective-permute-start | bytes 602120 | tf_op jit(solution)/shard_map/ppermute | solution.py:360
  18.4 9.2 %collective-permute-start.7 = (f32[384,128]{1,0:T(8,128)S(1)}, f32[384,128]{1,0:T(8,128)S(1)}, u32[]{:S(2)}, u32[]{:S(2)}) collective-permute-start(f32[384,128]{1,0:T(8,128)S(1)} %get-tuple-element.28), channel_id=1, source_target_pairs={{0,24},{4,28},{8,16},{12,20},{16,8},{20,12},{24,0},{28,4},{32,56},... | collective-permute-start | bytes 589832 | tf_op jit(solution)/shard_map/ppermute | solution.py:361
  22.5 5.1 %collective-permute-start.6 = (f32[256,128]{1,0:T(8,128)S(1)}, f32[256,128]{1,0:T(8,128)S(1)}, u32[]{:S(2)}, u32[]{:S(2)}) collective-permute-start(f32[256,128]{1,0:T(8,128)S(1)} %shard_map.52), channel_id=1, source_target_pairs={{0,8},{4,12},{8,0},{12,4},{16,24},{20,28},{24,16},{28,20},{32,40},... | collective-permute-start | bytes 393224 | tf_op jit(solution)/shard_map/ppermute | solution.py:370
